TPU v7x, 32 devices: a whole 2x2x4 slice. The times are simulated.
32 devices in a mesh: wide: 8 (over z, x), narrow: 4 (over y, core).
Axes of the slice: x: 2, y: 2, z: 4, core: 2. Of those that a mesh axis runs over, the one named last changes fastest.
Arguments:
- inputs: bfloat16 [81920, 512], P(('wide', 'narrow')), may hold values from -6 to 6
- segments: int32 [81920], P(('wide', 'narrow')), may hold values from 0 to 8, as said below
- pad_mask: int32 [81920], P(('wide', 'narrow')), may hold values from 0 to 1, as said below
- cotangent: bfloat16 [81920, 512], P(('wide', 'narrow')), may hold values from -6 to 6
- w_query: bfloat16 [512, 512], P(None, ('wide', 'narrow')), may hold values from -0.25 to 0.25
- b_query: bfloat16 [512], P(('wide', 'narrow')), may hold values from -3 to 3
- w_key: bfloat16 [512, 512], P(None, ('wide', 'narrow')), may hold values from -0.25 to 0.25
- w_value: bfloat16 [512, 512], P(None, ('wide', 'narrow')), may hold values from -0.25 to 0.25
- b_value: bfloat16 [512], P(('wide', 'narrow')), may hold values from -3 to 3
- w_out: bfloat16 [512, 512], P(None, ('wide', 'narrow')), may hold values from -0.75 to 0.75
- b_out: bfloat16 [512], P(('wide', 'narrow')), may hold values from -2 to 2
- gain_one: bfloat16 [512], P(('wide', 'narrow')), may hold values from 0.25 to 1.75
- shift_one: bfloat16 [512], P(('wide', 'narrow')), may hold values from -3 to 3
- w_up: bfloat16 [512, 3200], P(('wide', 'narrow')), may hold values from -0.25 to 0.25
- b_up: bfloat16 [3200], P('narrow'), may hold values from -3 to 3
- w_down: bfloat16 [3200, 512], P(None, ('wide', 'narrow')), may hold values from -0.109375 to 0.109375
- b_down: bfloat16 [512], P(('wide', 'narrow')), may hold values from -2 to 2
- gain_two: bfloat16 [512], P(('wide', 'narrow')), may hold values from 0.25 to 1.75
- shift_two: bfloat16 [512], P(('wide', 'narrow')), may hold values from -3 to 3
- pos_table: bfloat16 [302, 512], P(None, ('wide', 'narrow')), may hold values from -3 to 3
Outputs:
- layer_out: bfloat16 [81920, 512], P(('wide', 'narrow'))
- input_grad: bfloat16 [81920, 512], P(('wide', 'narrow'))
- grad_w_query: float32 [512, 512], P(None, ('wide', 'narrow'))
- grad_b_query: float32 [512], P(('wide', 'narrow'))
- grad_w_key: float32 [512, 512], P(None, ('wide', 'narrow'))
- grad_w_value: float32 [512, 512], P(None, ('wide', 'narrow'))
- grad_b_value: float32 [512], P(('wide', 'narrow'))
- grad_w_out: float32 [512, 512], P(None, ('wide', 'narrow'))
- grad_b_out: float32 [512], P(('wide', 'narrow'))
- grad_gain_one: float32 [512], P(('wide', 'narrow'))
- grad_shift_one: float32 [512], P(('wide', 'narrow'))
- grad_w_up: float32 [512, 3200], P(('wide', 'narrow'))
- grad_b_up: float32 [3200], P('narrow')
- grad_w_down: float32 [3200, 512], P(None, ('wide', 'narrow'))
- grad_b_down: float32 [512], P(('wide', 'narrow'))
- grad_gain_two: float32 [512], P(('wide', 'narrow'))
- grad_shift_two: float32 [512], P(('wide', 'narrow'))
- grad_pos_table: float32 [302, 512], P(None, ('wide', 'narrow'))
Inputs may be any that keep to these rules, and one draw needn't show every extreme that they name: `segments`: within each pack of 640 rows, items of 77 or 302 tokens follow one another from the pack's first row, numbered 0, 1, 2, ... in order; the rows after the last item, fewer than 302, carry the next number. `pad_mask`: 1 on the rows of a pack's items, 0 on the rows after them.
All inputs are finite; a program needn't handle non-finite values.
Results may differ from a plain program's by a relative error of at most 0.015.
The roundings to bfloat16 on the way count: a program that leaves them out, or rounds other values in their place, can miss the bound.
Values may be sent and summed in bfloat16 or wider, within the bound.
No kernel may reach another device: no remote copies, remote signals or barrier semaphores. Data moves between devices by JAX's collectives and lax.ppermute only.
A program may use at most 192 MiB of HBM per device.

v0:
```python
import math

import jax
import jax.numpy as jnp
from jax import lax
from jax.sharding import PartitionSpec as P

D = 512
H = 8
FF = 3200
HD = 64
PACK = 640
LONG = 302


exact_prec = lax.Precision.HIGHEST
eps_norm = 1e-05
neg_fill = -1000000000.0


def layout(seg_ids):
    row_index = jnp.arange(seg_ids.shape[0], dtype=jnp.int32)
    same_item = seg_ids[:, None] == seg_ids[None, :]
    first_row = jnp.min(jnp.where(same_item, row_index[None, :], seg_ids.shape[0]), axis=1)
    return (same_item, row_index - first_row)


def sinusoid(item_place, model_width):
    half_width = model_width // 2
    frequency = jnp.exp(
        jnp.arange(half_width, dtype=jnp.float32) * (-2.0 * math.log(10000.0) / model_width)
    )
    angles = item_place.astype(jnp.float32)[:, None] * frequency[None, :]
    return jnp.concatenate([jnp.sin(angles), jnp.cos(angles)], axis=1)


def normalize(vector_in):
    centered = vector_in - jnp.mean(vector_in, axis=-1, keepdims=True)
    variance = jnp.mean(centered * centered, axis=-1, keepdims=True)
    return centered * lax.rsqrt(variance + eps_norm)


def matmul_low(left_op, right_op):
    return jnp.dot(left_op, right_op, preferred_element_type=jnp.float32)


def rows_inner(left_op, right_op):
    return lax.dot_general(
        left_op, right_op, (((0,), (0,)), ((), ())), preferred_element_type=jnp.float32
    )


def cols_inner(left_op, right_op):
    return lax.dot_general(
        left_op, right_op, (((1,), (1,)), ((), ())), preferred_element_type=jnp.float32
    )


def split_heads(block):
    return block.reshape(PACK, H, HD)


def split_columns(full_cols):
    return (
        full_cols[0:D],
        full_cols[D : 2 * D],
        full_cols[2 * D : 3 * D],
        full_cols[3 * D : 4 * D],
        full_cols[4 * D : 4 * D + FF],
        full_cols[4 * D + FF :],
    )


def masked_scores(query, keys, same_item):
    score_scale = 1.0 / math.sqrt(HD)
    scores = (
        jnp.einsum(
            "qhd,khd->hqk",
            split_heads(query),
            split_heads(keys),
            preferred_element_type=jnp.float32,
        )
        * score_scale
    )
    return jnp.where(same_item[None, :, :], scores, neg_fill)


def attend_forward(packed):
    query, keys, values, same_item = packed
    scores = masked_scores(query, keys, same_item)
    row_max = jnp.max(scores, axis=-1, keepdims=True)
    exp_scores = jnp.exp(scores - row_max)
    row_total = jnp.sum(exp_scores, axis=-1, keepdims=True)
    probs_low = (exp_scores / row_total).astype(jnp.bfloat16)
    mixed = jnp.einsum(
        "hqk,khd->qhd", probs_low, split_heads(values), preferred_element_type=jnp.float32
    )
    log_total = row_max[:, :, 0] + jnp.log(row_total[:, :, 0])
    return (mixed.reshape(PACK, D).astype(jnp.bfloat16), log_total)


def attend_backward(packed):
    query, keys, values, same_item, log_total, d_attn = packed
    score_scale = 1.0 / math.sqrt(HD)
    scores = masked_scores(query, keys, same_item)
    attn_probs = jnp.exp(scores - log_total[:, :, None])
    d_heads = split_heads(d_attn)
    d_probs = jnp.einsum(
        "qhd,khd->hqk", d_heads, split_heads(values), preferred_element_type=jnp.float32
    )
    d_values = jnp.einsum(
        "hqk,qhd->khd", attn_probs.astype(jnp.bfloat16), d_heads, preferred_element_type=jnp.float32
    )
    row_delta = jnp.sum(attn_probs * d_probs, axis=-1, keepdims=True)
    d_scores = (attn_probs * (d_probs - row_delta)).astype(jnp.bfloat16)
    d_query = (
        jnp.einsum("hqk,khd->qhd", d_scores, split_heads(keys), preferred_element_type=jnp.float32)
        * score_scale
    )
    d_keys = (
        jnp.einsum("hqk,qhd->khd", d_scores, split_heads(query), preferred_element_type=jnp.float32)
        * score_scale
    )
    return (
        d_query.reshape(PACK, D).astype(jnp.bfloat16),
        d_keys.reshape(PACK, D).astype(jnp.bfloat16),
        d_values.reshape(PACK, D).astype(jnp.bfloat16),
    )


def local(
    inputs,
    segments,
    pad_mask,
    cotangent,
    w_query,
    b_query,
    w_key,
    w_value,
    b_value,
    w_out,
    b_out,
    gain_one,
    shift_one,
    w_up,
    b_up,
    w_down,
    b_down,
    gain_two,
    shift_two,
    pos_table,
):
    columns = jnp.concatenate([w_query, w_key, w_value, w_out, w_down, pos_table], axis=0)
    vectors = jnp.stack(
        [b_query, b_value, b_out, gain_one, shift_one, b_down, gain_two, shift_two], axis=0
    )
    full_cols, full_up, full_vec = (
        lax.all_gather(columns, ("wide", "narrow"), axis=1, tiled=True),
        lax.all_gather(w_up, ("wide", "narrow"), axis=0, tiled=True),
        lax.all_gather(vectors, ("wide", "narrow"), axis=1, tiled=True),
    )
    full_bias = lax.all_gather(b_up, "narrow", axis=0, tiled=True)
    m_query, m_key, m_value, m_out, m_down, m_table = split_columns(full_cols)
    (
        bias_query,
        bias_value,
        bias_out,
        gain_first,
        shift_first,
        bias_down,
        gain_second,
        shift_second,
    ) = jnp.split(full_vec.astype(jnp.float32), 8, axis=0)
    row_count = inputs.shape[0]
    pack_count = row_count // PACK
    same_item, item_place = jax.vmap(layout)(segments.reshape(pack_count, PACK))
    item_place = item_place.reshape(row_count)
    picks_float = (item_place[:, None] == jnp.arange(LONG, dtype=jnp.int32)[None, :]).astype(
        jnp.float32
    )
    picks = picks_float.astype(jnp.bfloat16)
    input_float = inputs.astype(jnp.float32)
    positions = sinusoid(item_place, D) + matmul_low(picks, m_table)
    mixed_in = (input_float + positions).astype(jnp.bfloat16)
    query = (matmul_low(mixed_in, m_query) + bias_query).astype(jnp.bfloat16)
    keys = matmul_low(mixed_in, m_key).astype(jnp.bfloat16)
    values = (matmul_low(inputs, m_value) + bias_value).astype(jnp.bfloat16)
    query_packs = query.reshape(pack_count, PACK, D)
    key_packs = keys.reshape(pack_count, PACK, D)
    value_packs = values.reshape(pack_count, PACK, D)
    attn_packs, log_total = lax.map(
        attend_forward, (query_packs, key_packs, value_packs, same_item)
    )
    attn = attn_packs.reshape(row_count, D)
    first_sum = input_float + (matmul_low(attn, m_out) + bias_out)
    norm_first = normalize(first_sum)
    hidden_first = gain_first * norm_first + shift_first
    hidden_low = hidden_first.astype(jnp.bfloat16)
    pre_act = matmul_low(hidden_low, full_up) + full_bias.astype(jnp.float32)
    act_low = jax.nn.gelu(pre_act).astype(jnp.bfloat16)
    second_sum = hidden_first + (matmul_low(act_low, m_down) + bias_down)
    norm_second = normalize(second_sum)
    keep_rows = pad_mask.astype(jnp.float32)[:, None]
    layer_out = ((gain_second * norm_second + shift_second) * keep_rows).astype(jnp.bfloat16)
    full_cols, full_up, full_vec = (
        lax.all_gather(columns, ("wide", "narrow"), axis=1, tiled=True),
        lax.all_gather(w_up, ("wide", "narrow"), axis=0, tiled=True),
        lax.all_gather(vectors, ("wide", "narrow"), axis=1, tiled=True),
    )
    m_query, m_key, m_value, m_out, m_down, m_table = split_columns(full_cols)
    (
        bias_query,
        bias_value,
        bias_out,
        gain_first,
        shift_first,
        bias_down,
        gain_second,
        shift_second,
    ) = jnp.split(full_vec.astype(jnp.float32), 8, axis=0)
    grad_top = cotangent.astype(jnp.float32) * keep_rows
    d_gain_second = jnp.sum(grad_top * norm_second, axis=0)
    d_shift_second = jnp.sum(grad_top, axis=0)
    d_second = jax.vjp(normalize, second_sum)[1](grad_top * gain_second)[0]
    d_ff = d_second.astype(jnp.bfloat16)
    d_down = rows_inner(act_low, d_ff)
    d_bias_down = jnp.sum(d_ff.astype(jnp.float32), axis=0)
    d_act = cols_inner(d_ff, m_down)
    d_pre = jax.vjp(jax.nn.gelu, pre_act)[1](d_act)[0].astype(jnp.bfloat16)
    d_up = rows_inner(hidden_low, d_pre)
    d_bias_up = jnp.sum(d_pre.astype(jnp.float32), axis=0)
    d_hidden = d_second + cols_inner(d_pre, full_up)
    d_gain_first = jnp.sum(d_hidden * norm_first, axis=0)
    d_shift_first = jnp.sum(d_hidden, axis=0)
    d_first = jax.vjp(normalize, first_sum)[1](d_hidden * gain_first)[0]
    d_branch = d_first.astype(jnp.bfloat16)
    d_wout = rows_inner(attn, d_branch)
    d_bias_out = jnp.sum(d_branch.astype(jnp.float32), axis=0)
    d_attn = cols_inner(d_branch, m_out).astype(jnp.bfloat16)
    d_query_packs, d_key_packs, d_value_packs = lax.map(
        attend_backward,
        (
            query_packs,
            key_packs,
            value_packs,
            same_item,
            log_total,
            d_attn.reshape(pack_count, PACK, D),
        ),
    )
    d_query = d_query_packs.reshape(row_count, D)
    d_keys = d_key_packs.reshape(row_count, D)
    d_values = d_value_packs.reshape(row_count, D)
    d_wquery = rows_inner(mixed_in, d_query)
    d_bias_query = jnp.sum(d_query.astype(jnp.float32), axis=0)
    d_wkey = rows_inner(mixed_in, d_keys)
    d_wvalue = rows_inner(inputs, d_values)
    d_bias_value = jnp.sum(d_values.astype(jnp.float32), axis=0)
    d_mixed = cols_inner(d_query, m_query) + cols_inner(d_keys, m_key)
    d_table = lax.dot_general(picks_float, d_mixed, (((0,), (0,)), ((), ())), precision=exact_prec)
    input_grad = (d_first + d_mixed + cols_inner(d_values, m_value)).astype(jnp.bfloat16)
    grad_cols = jnp.concatenate([d_wquery, d_wkey, d_wvalue, d_wout, d_down, d_table], axis=0)
    grad_vec = jnp.stack(
        [
            d_bias_query,
            d_bias_value,
            d_bias_out,
            d_gain_first,
            d_shift_first,
            d_bias_down,
            d_gain_second,
            d_shift_second,
        ],
        axis=0,
    )
    own_cols, own_up, own_vec = (
        lax.psum_scatter(grad_cols, ("wide", "narrow"), scatter_dimension=1, tiled=True),
        lax.psum_scatter(d_up, ("wide", "narrow"), scatter_dimension=0, tiled=True),
        lax.psum_scatter(grad_vec, ("wide", "narrow"), scatter_dimension=1, tiled=True),
    )
    bias_total = lax.psum(d_bias_up, ("wide", "narrow"))
    bias_width = bias_total.shape[0] // lax.axis_size("narrow")
    grad_b_up = lax.dynamic_slice_in_dim(
        bias_total, lax.axis_index("narrow") * bias_width, bias_width
    )
    g_query, g_key, g_value, g_out, g_down, g_table = split_columns(own_cols)
    return (
        layer_out,
        input_grad,
        g_query,
        own_vec[0],
        g_key,
        g_value,
        own_vec[1],
        g_out,
        own_vec[2],
        own_vec[3],
        own_vec[4],
        own_up,
        grad_b_up,
        g_down,
        own_vec[5],
        own_vec[6],
        own_vec[7],
        g_table,
    )


def solution(mesh):
    in_specs = (
        P(("wide", "narrow"), None),
        P(("wide", "narrow")),
        P(("wide", "narrow")),
        P(("wide", "narrow"), None),
        P(None, ("wide", "narrow")),
        P(("wide", "narrow")),
        P(None, ("wide", "narrow")),
        P(None, ("wide", "narrow")),
        P(("wide", "narrow")),
        P(None, ("wide", "narrow")),
        P(("wide", "narrow")),
        P(("wide", "narrow")),
        P(("wide", "narrow")),
        P(("wide", "narrow"), None),
        P("narrow"),
        P(None, ("wide", "narrow")),
        P(("wide", "narrow")),
        P(("wide", "narrow")),
        P(("wide", "narrow")),
        P(None, ("wide", "narrow")),
    )
    out_specs = (
        P(("wide", "narrow"), None),
        P(("wide", "narrow"), None),
        P(None, ("wide", "narrow")),
        P(("wide", "narrow")),
        P(None, ("wide", "narrow")),
        P(None, ("wide", "narrow")),
        P(("wide", "narrow")),
        P(None, ("wide", "narrow")),
        P(("wide", "narrow")),
        P(("wide", "narrow")),
        P(("wide", "narrow")),
        P(("wide", "narrow"), None),
        P("narrow"),
        P(None, ("wide", "narrow")),
        P(("wide", "narrow")),
        P(("wide", "narrow")),
        P(("wide", "narrow")),
        P(None, ("wide", "narrow")),
    )
    return jax.shard_map(local, mesh=mesh, in_specs=in_specs, out_specs=out_specs, check_vma=False)
```

profile of v0, /device:TPU:0, one launch (start us, length us, event | category | flops | bytes accessed | tf_op | source)
XLA Modules:
  0.0 887.2 jit_solution(2582076242429681076)
XLA Ops:
  19.8 8.7 all-reduce
  31.2 41.3 %all-gather = bf16[32,16,8]{1,2,0:T(8,128)(2,1)S(1)} all-gather(bf16[1,16,8]{1,2,0:T(8,128)(2,1)S(1)} %bitcast.222), channel_id=1, replica_groups=mesh['wide'=8,'narrow'=4] {'wide','narrow'}, dimensions={0}, use_global_device_ids=true | all-gather | bytes 8448 | tf_op jit(solution)/shard_map/all_gather | solution.py:160
  73.5 10.6 %multiply_sine_fusion = (f32[2560,256]{1,0:T(8,128)S(1)}, f32[2560,256]{1,0:T(8,128)}) fusion(f32[256]{0:T(256)S(1)} %multiply_exponential_fusion, f32[2560]{0:T(1024)S(1)} %convert_element_type.162), kind=kLoop, calls=%fused_computation.83 | loop fusion | flops 655360 | bytes 5254144 | tf_op jit(solution)/shard_map/sin | solution.py:34
  107.8 65.3 %while.26 = (s32[]{:T(128)}, bf16[4,640,512]{2,1,0:T(8,128)(2,1)}, f32[4,8,640]{2,1,0:T(8,128)}, bf16[4,640,512]{1,2,0:T(8,128)(2,1)}, pred[4,640,640]{1,2,0:T(8...) while((s32[]{:T(128)}, bf16[4,640,512]{2,1,0:T(8,128)(2,1)}, ...), condition=%wide.region_4.5_spmd, body=%wide.region_1.4_spmd.sunk | while | flops 878504960 | bytes 50708592 | solution.py:191
  181.0 24.6 %multiply_convert_fusion.1 = (bf16[2560,3200]{1,0:T(8,128)(2,1)}, f32[2560,3200]{1,0:T(8,128)}) fusion(f32[3200]{0:T(1024)S(1)} %copy-done.27, bf16[512,3200]{1,0:T(8,128)(2,1)} %all-gather.6.cloned.1.call-done, f32[2560,512]{1,0:T(8,128)} %copy-done.1, f32[512]{0:T(512)S(1)} %bitcast.226, f32[2560]{0:T(1024)S(1)} %fusion.41, ...), kind=kOutput, calls=%fused_computation.44 | convolution fusion | flops 8477081600 | bytes 57709056 | tf_op jit(solution)/shard_map/dot_general | solution.py:44
  205.6 14.2 %fusion.53 = (f32[2560]{0:T(1024)S(1)}, f32[2560,512]{1,0:T(8,128)S(1)}) fusion(f32[512]{0:T(512)S(1)} %bitcast.231, bf16[2560,3200]{1,0:T(8,128)(2,1)} %get-tuple-element.336, bf16[5550,512]{0,1:T(8,128)(2,1)} %all-gather.4.cloned.1.call-done, f32[512]{0:T(512)S(1)} %bitcast.227, f32[2560]{0:T(1024)S(1)} %fusion.41, f32[2560,512]{1,0:T(8,128)S(1)} %copy-done.2, ...), kind=kOutput, calls=%fused_computation.132 | convolution fusion | flops 8397780480 | bytes 30183424 | tf_op jit(solution)/shard_map/dot_general | solution.py:44
  232.7 34.3 %convert_reduce_fusion = (f32[3200]{0:T(1024)}, bf16[2560,3200]{1,0:T(8,128)(2,1)}) fusion(f32[2560,3200]{1,0:T(8,128)} %get-tuple-element.337, f32[3200]{0:T(1024)S(1)} %copy-done.27, bf16[2560,512]{1,0:T(8,128)(2,1)S(1)} %get-tuple-element.296, bf16[5550,512]{0,1:T(8,128)(2,1)} %all-gather.4.cloned.1.call-done), kind=kOutput, calls=%fused_computation.43 | convolution fusion | flops 8577020928 | bytes 55075840 | tf_op jit(solution)/shard_map/dot_general | solution.py:54
  267.0 17.9 %multiply_reduce_fusion.2 = (f32[512]{0:T(512)}, f32[2560]{0:T(1024)S(1)}, f32[512]{0:T(512)}, f32[2560,512]{1,0:T(8,128)}) fusion(f32[2560,512]{1,0:T(8,128)S(1)} %copy-done.2, f32[2560]{0:T(1024)S(1)} %fusion.41, f32[2560]{0:T(1024)S(1)} %broadcast_multiply_fusion.1, f32[512]{0:T(512)S(1)} %bitcast.215, bf16[2560,3200]{1,0:T(8,128)(2,1)} %get-tuple-element.342, ...), kind=kOutput, calls=%fused_computation.55 | convolution fusion | flops 8401711616 | bytes 35436544 | tf_op jit(solution)/shard_map/dot_general | solution.py:54
  299.4 139.4 %while.27 = (s32[]{:T(128)}, bf16[4,640,512]{1,2,0:T(8,128)(2,1)}, bf16[4,640,512]{2,1,0:T(8,128)(2,1)}, bf16[4,640,512]{1,2,0:T(8,128)(2,1)}, bf16[4,640,512]{1...) while((s32[]{:T(128)}, bf16[4,640,512]{1,2,0:T(8,128)(2,1)}, ...), condition=%wide.region_15.16_spmd, body=%wide.region_13.15_spmd.sunk | while | flops 2128276480 | bytes 117985424 | solution.py:240
  308.0 7.5 multiply_reduce_fusion.8
  315.4 6.1 multiply_convert_fusion.4
  321.5 6.9 fusion.129
  342.8 7.5 multiply_reduce_fusion.8
  350.3 6.1 multiply_convert_fusion.4
  356.4 6.9 fusion.129
  377.6 7.5 multiply_reduce_fusion.8
  385.1 6.1 multiply_convert_fusion.4
  391.2 6.9 fusion.129
  412.4 7.5 multiply_reduce_fusion.8
  419.9 6.1 multiply_convert_fusion.4
  426.0 6.9 fusion.129
  449.7 5.2 convolution_dynamic-update-slice_fusion.3
  462.6 15.2 %convolution_dynamic-update-slice_fusion = f32[5550,512]{1,0:T(8,128)} fusion(f32[5550,512]{1,0:T(8,128)} %convolution_dynamic-update-slice_fusion.1, bf16[2560,3200]{1,0:T(8,128)(2,1)} %get-tuple-element.336, bf16[2560,512]{1,0:T(8,128)(2,1)S(1)} %copy-done.11), kind=kOutput, calls=%fused_computation.47 | convolution fusion | flops 8388608000 | bytes 25559040 | tf_op jit(solution)/shard_map/dot_general | solution.py:48
  480.4 5.2 convolution_add_fusion
  485.5 8.0 fusion.30
  493.5 12.0 %copy.136 = f32[5550,512]{0,1:T(8,128)} copy(f32[5550,512]{1,0:T(8,128)} %fusion.30) | data formatting | bytes 22732800
  506.3 17.5 %fusion.43 = f32[512,3200]{1,0:T(8,128)} fusion(bf16[2560,3200]{1,0:T(8,128)(2,1)} %get-tuple-element.342, f32[2560,512]{1,0:T(8,128)} %copy-done.1, f32[512]{0:T(512)S(1)} %bitcast.228, f32[2560]{0:T(1024)S(1)} %copy-done.25, f32[2560]{0:T(1024)S(1)} %copy-done.18, f32[512]{0:T(512)S(1)} %bitcast.217), kind=kOutput, calls=%fused_computation.124 | convolution fusion | flops 8395161600 | bytes 28205056 | tf_op jit(solution)/shard_map/dot_general | solution.py:48
  524.5 38.3 %psum.7 = f32[3200]{0:T(1024)S(1)} all-reduce(f32[3200]{0:T(1024)S(1)} %copy-done.28), channel_id=1, replica_groups=mesh['wide'=8,'narrow'=4] {'wide','narrow'}, use_global_device_ids=true, to_apply=%region_28.29 | all-reduce | flops 3200 | bytes 25600 | tf_op jit(solution)/shard_map/psum | solution.py:281
  563.5 6.3 add_convert_fusion
  569.8 10.8 %reduce-scatter.12.cloned.1.call-done = f32[16,8]{1,0:T(8,128)} async-done(((f32[512,8]{1,0:T(8,128)}), f32[16,8]{1,0:T(8,128)}) %reduce-scatter.12.cloned.1.call-update) | async-done | bytes 528
  586.3 147.3 %reduce-scatter.10.cloned.1.call-done = f32[16,5550]{1,0:T(8,128)} async-done(((f32[512,5550]{1,0:T(8,128)}), f32[16,5550]{1,0:T(8,128)}) %reduce-scatter.10.cloned.1.call-update) | async-done | bytes 355216
  738.1 142.4 %reduce-scatter.8.cloned.1.call-done = f32[16,3200]{1,0:T(8,128)} async-done(((f32[512,3200]{1,0:T(8,128)}), f32[16,3200]{1,0:T(8,128)}) %reduce-scatter.8.cloned.1.call-update) | async-done | bytes 204816 | tf_op jit(solution)/shard_map/reduce_scatter | solution.py:278
  (268 shorter events, 229.6 us)
Async XLA Ops:
  7.2 76.9 %all-gather.4.cloned.1.call-start = ((), (), s32[]{:S(2)}) async-start(), calls=%async_computation.3 | async-start | bytes 5947392 | tf_op jit(solution)/shard_map/all_gather | solution.py:158
  12.4 168.5 %all-gather.6.cloned.1.call-start = ((), (), s32[]{:S(2)}) async-start(), calls=%async_computation.4 | async-start | bytes 3379200 | tf_op jit(solution)/shard_map/all_gather | solution.py:159
  13.2 567.4 %reduce-scatter.12.cloned.1.call-start = ((), (), s32[]{:S(2)}) async-start(), calls=%async_computation.7 | async-start | bytes 270336
  29.1 60.2 %copy-start.21 = (s32[2560]{0:T(1024)}, s32[2560]{0:T(1024)S(1)}, u32[]{:S(2)}) copy-start(s32[2560]{0:T(1024)S(1)} %sub.74) | copy-start | bytes 30724
  87.6 3.5 copy-start.43
  107.8 65.3 %copy-start.41 = (f32[1,512]{1,0:T(1,128)S(1)}, f32[1,512]{1,0:T(1,128)}, u32[]{:S(2)}) copy-start(f32[1,512]{1,0:T(1,128)} %get-tuple-element.320) | copy-start | bytes 6148
  177.6 3.3 copy-start.27
  177.6 3.3 copy-start.29
  177.6 107.3 %copy-start.17 = (f32[2560]{0:T(1024)}, f32[2560]{0:T(1024)S(1)}, u32[]{:S(2)}) copy-start(f32[2560]{0:T(1024)S(1)} %broadcast_multiply_fusion.1) | copy-start | bytes 30724
  180.9 104.1 %copy-start.24 = (f32[2560]{0:T(1024)}, f32[2560]{0:T(1024)S(1)}, u32[]{:S(2)}) copy-start(f32[2560]{0:T(1024)S(1)} %fusion.41) | copy-start | bytes 30724
  180.9 24.7 %copy-start.2 = (f32[2560,512]{1,0:T(8,128)S(1)}, f32[2560,512]{1,0:T(8,128)}, u32[]{:S(2)}) copy-start(f32[2560,512]{1,0:T(8,128)} %copy-done.1) | copy-start | bytes 15728644
  180.9 24.7 %copy-start.40 = (f32[1,512]{1,0:T(1,128)S(1)}, f32[1,512]{1,0:T(1,128)}, u32[]{:S(2)}) copy-start(f32[1,512]{1,0:T(1,128)} %get-tuple-element.318) | copy-start | bytes 6148
  220.9 4.1 copy-start.35
  232.7 34.3 %copy-start.10 = (bf16[2560,512]{1,0:T(8,128)(2,1)}, bf16[2560,512]{1,0:T(8,128)(2,1)S(1)}, u32[]{:S(2)}) copy-start(bf16[2560,512]{1,0:T(8,128)(2,1)S(1)} %get-tuple-element.296) | copy-start | bytes 7864324
  232.7 34.3 %copy-start.42 = (bf16[512,3200]{1,0:T(8,128)(2,1)S(1)}, bf16[512,3200]{1,0:T(8,128)(2,1)}, u32[]{:S(2)}) copy-start(bf16[512,3200]{1,0:T(8,128)(2,1)} %all-gather.6.cloned.1.call-done) | copy-start | bytes 9830404
  289.8 7.9 copy-start.19
  293.2 6.1 copy-start.12
  438.8 4.5 copy-start.8
  443.3 5.3 copy-start.31
  443.3 5.3 copy-start.32
  443.3 5.4 copy-start.33
  443.3 5.4 copy-start.34
  443.3 5.3 copy-start.38
  443.3 5.3 copy-start.39
  448.6 6.3 copy-start.4
  449.6 284.0 %reduce-scatter.10.cloned.1.call-start = ((), (), s32[]{:S(2)}) async-start(), calls=%async_computation.6 | async-start | bytes 11894784
  449.7 5.2 copy-start.46
  462.6 15.2 %copy-start.5 = (bf16[4,640,512]{2,1,0:T(8,128)(2,1)S(1)}, bf16[4,640,512]{2,1,0:T(8,128)(2,1)}, u32[]{:S(2)}) copy-start(bf16[4,640,512]{2,1,0:T(8,128)(2,1)} %copy.121) | copy-start | bytes 7864324
  480.4 5.2 copy-start.22
  505.6 374.8 %reduce-scatter.8.cloned.1.call-start = ((), (), s32[]{:S(2)}) async-start(), calls=%async_computation.5 | async-start | bytes 6758400 | tf_op jit(solution)/shard_map/reduce_scatter | solution.py:278
  523.8 39.7 %copy-start.7 = (bf16[4,640,512]{2,1,0:T(8,128)(2,1)S(1)}, bf16[4,640,512]{2,1,0:T(8,128)(2,1)}, u32[]{:S(2)}) copy-start(bf16[4,640,512]{2,1,0:T(8,128)(2,1)} %copy.123) | copy-start | bytes 7864324
  523.8 39.7 %copy-start.20 = (f32[2560]{0:T(1024)S(1)}, f32[2560]{0:T(1024)}, u32[]{:S(2)}) copy-start(f32[2560]{0:T(1024)} %copy-done.19) | copy-start | bytes 30724
  (20 other events, 38.5 us)
Sparse Core Ops, SparseCore 0:
  12.6 69.9 all-gather.3
  85.4 58.2 all-gather.5
  449.7 130.7 reduce-scatter.11
  582.8 150.7 reduce-scatter.9
  736.5 143.9 reduce-scatter.7
where the time goes:
time: 898 us; the launch traced here: 887 us
  waiting for transfers between devices  301 us (34%)
  matrix products  288 us (32%)
  local copies, waits for them, and re-layouts  122 us (14%)
  blocking collectives  88.3 us (10%)
  other arithmetic  72.2 us (8%)
  between operations  15.2 us (2%)
    unnamed x7, waiting for transfers between devices  159 us
    reduce_scatter x1, waiting for transfers between devices, local(): lax.psum_scatter(d_up, ('wide', 'narrow'), scatter_dimension=0, tiled=True)  142 us
    dot_general x6, matrix products, cols_inner(): lax.dot_general(left_op, right_op, (((1,), (1,)), ((), ())), preferred_el...  70.7 us
    dot_general x7, matrix products, matmul_low(): return jnp.dot(left_op, right_op, preferred_element_type=jnp.float32)  56.6 us
    dot_general x6, matrix products, rows_inner(): lax.dot_general(left_op, right_op, (((0,), (0,)), ((), ())), preferred_el...  45.5 us
    all_gather x1, blocking collectives, local(): lax.all_gather(vectors, ('wide', 'narrow'), axis=1, tiled=True)  41.3 us
    dot_general x8, matrix products, masked_scores(): jnp.einsum('qhd,khd->hqk', split_heads(query), split_heads(keys), preferr...  38.9 us
    psum x1, blocking collectives, local(): bias_total = lax.psum(d_bias_up, ('wide', 'narrow'))  38.3 us
  transfers between devices with their start and end apart: 5, of which 3 were waited for; matrix products, arithmetic and copies ran while one was open for 23% of the time, Pallas kernels for 0%

commit v1 on v0

v1 whole, which is shorter than its diff:
```python
import math

import jax
import jax.numpy as jnp
from jax import lax
from jax.experimental import pallas as pl
from jax.experimental.pallas import tpu as pltpu
from jax.sharding import PartitionSpec as P

D = 512
H = 8
FF = 3200
HD = 64
PACK = 640
LONG = 302
PLACES = 384
SCALE = 0.125
EPS = 1e-05
NEG = -1e9
WT = 3 * D + PLACES
WA = WT + 128
BLOCK = 16
BLOCKS = D // BLOCK
WB = D + 2 * FF
TILE = 512
FF_CHUNKS = ((0, 768), (768, 768), (1536, 768), (2304, 896))
Q_CHUNKS = ((0, 256), (256, 256), (512, 128))
AXES = ("wide", "narrow")
VMEM = 60 * 1024 * 1024
BF = jnp.bfloat16
F32 = jnp.float32


def nn(a, b):
    return lax.dot_general(a, b, (((1,), (0,)), ((), ())), preferred_element_type=F32)


def nt(a, b):
    return lax.dot_general(a, b, (((1,), (1,)), ((), ())), preferred_element_type=F32)


def item_masks(seg_row):
    wide = jnp.broadcast_to(seg_row.astype(F32), (8, PACK))
    col = jnp.transpose(wide)[:, 0:1]
    return col == wide[0:1]


def head_lanes(block, half):
    lane = lax.broadcasted_iota(jnp.int32, block.shape, 1)
    keep = (lane < HD) if half == 0 else (lane >= HD)
    return jnp.where(keep, block, jnp.zeros_like(block))


def block_rows(me_ref, place):
    owner = me_ref[0] ^ offsets(BLOCKS)[place]
    return pl.ds(pl.multiple_of(owner * BLOCK, BLOCK), BLOCK)


def load_blocks(me_ref, halves, full_ref, sem):
    copies = []
    for place in range(BLOCKS):
        half, at = divmod(place, BLOCKS // 2)
        copies.append(pltpu.make_async_copy(halves[half].at[at * BLOCK : (at + 1) * BLOCK], full_ref.at[block_rows(me_ref, place)], sem))
    for copy in copies:
        copy.start()
    for copy in copies:
        copy.wait()


def store_blocks(me_ref, spans, halves, sem):
    copies = []
    for place in range(BLOCKS):
        half, at = divmod(place, BLOCKS // 2)
        for ref, col, width in spans:
            target = halves[half].at[at * BLOCK : (at + 1) * BLOCK, col : col + width]
            copies.append(pltpu.make_async_copy(ref.at[block_rows(me_ref, place)], target, sem))
    for copy in copies:
        copy.start()
    for copy in copies:
        copy.wait()


def attend_kernel(me_ref, seg_ref, x_ref, al_ref, ar_ref, st_ref, q_ref, k_ref, v_ref, mix_ref, attn_ref, pt_ref, vec_ref, ga_ref, hi_ref, lo_ref, bias_ref, vt_ref, at_ref, sem):
    @pl.when(pl.program_id(0) == 0)
    def _():
        load_blocks(me_ref, (al_ref, ar_ref), ga_ref, sem)
        vec_ref[...] = jnp.transpose(ga_ref[:, WT:].astype(F32))
        pos = st_ref[...] + ga_ref[:, 3 * D : 3 * D + PLACES].astype(F32)
        hi = pos.astype(BF)
        hi_ref[...] = hi
        lo_ref[...] = (pos - hi.astype(F32)).astype(BF)

    same = item_masks(seg_ref[0])
    bias_ref[...] = jnp.where(same, 0.0, NEG)
    lane = lax.broadcasted_iota(jnp.int32, (PACK, PACK), 1).astype(F32)
    first = jnp.min(jnp.where(same, lane, 1e6), axis=1, keepdims=True)
    place = lax.broadcasted_iota(jnp.int32, (PACK, 1), 0).astype(F32) - first
    slot = lax.broadcasted_iota(jnp.int32, (PACK, PLACES), 1).astype(F32)
    picks = jnp.where(place == slot, 1.0, 0.0).astype(BF)
    x = x_ref[...]
    positions = nt(picks, hi_ref[...]) + nt(picks, lo_ref[...])
    mixed = (x.astype(F32) + positions).astype(BF)
    mix_ref[...] = mixed
    q_ref[...] = ((nt(mixed, ga_ref[:, 0:D]) + vec_ref[0:1]).astype(BF).astype(F32) * SCALE).astype(BF)
    k_ref[...] = nt(mixed, ga_ref[:, D : 2 * D]).astype(BF)
    v = (nt(x, ga_ref[:, 2 * D : 3 * D]) + vec_ref[1:2]).astype(BF)
    v_ref[...] = v
    vt_ref[...] = jnp.transpose(v)

    def pair(j, carry):
        lanes = pl.ds(pl.multiple_of(j * 2 * HD, 2 * HD), 2 * HD)
        keys = k_ref[:, lanes]
        for half in range(2):
            rows = pl.ds(pl.multiple_of((2 * j + half) * HD, HD), HD)
            values_t = vt_ref[rows, :]
            for start, size in Q_CHUNKS:
                query = head_lanes(q_ref[start : start + size, lanes], half)
                scores = nt(keys, query) + bias_ref[:, start : start + size]
                top = jnp.max(scores, axis=0, keepdims=True)
                exps = jnp.exp(scores - top)
                total = jnp.sum(exps, axis=0, keepdims=True)
                probs = (exps * (1.0 / total)).astype(BF)
                pt_ref[0, 2 * j + half, :, start : start + size] = probs
                at_ref[rows, start : start + size] = nn(values_t, probs).astype(BF)
        return carry

    lax.fori_loop(0, H // 2, pair, 0)
    attn_ref[...] = jnp.transpose(at_ref[...])


def whole(shape):
    return pl.BlockSpec(shape, lambda i: tuple(0 for _ in shape), pipeline_mode=pl.Buffered(1))


def rows_of(count, width):
    return pl.BlockSpec((count, width), lambda i: (i, 0))


SCALAR = pl.BlockSpec(memory_space=pltpu.SMEM)
LOOSE = pl.BlockSpec(memory_space=pl.ANY)


def attend(where, seg, x, halves, st):
    packs = seg.shape[0]
    tokens = packs * PACK
    low = jax.ShapeDtypeStruct((tokens, D), BF)
    return pl.pallas_call(
        attend_kernel,
        grid=(packs,),
        in_specs=[SCALAR, pl.BlockSpec((1, 1, PACK), lambda i: (i, 0, 0)), rows_of(PACK, D), LOOSE, LOOSE, whole((D, PLACES))],
        out_specs=[rows_of(PACK, D)] * 5 + [pl.BlockSpec((1, H, PACK, PACK), lambda i: (i, 0, 0, 0)), whole((128, D))],
        out_shape=[low] * 5 + [jax.ShapeDtypeStruct((packs, H, PACK, PACK), BF), jax.ShapeDtypeStruct((128, D), F32)],
        scratch_shapes=[
            pltpu.VMEM((D, WA), BF),
            pltpu.VMEM((D, PLACES), BF),
            pltpu.VMEM((D, PLACES), BF),
            pltpu.VMEM((PACK, PACK), F32),
            pltpu.VMEM((D, PACK), BF),
            pltpu.VMEM((D, PACK), BF),
            pltpu.SemaphoreType.DMA,
        ],
        compiler_params=pltpu.CompilerParams(vmem_limit_bytes=VMEM),
        cost_estimate=pl.CostEstimate(flops=40 * 10**9, bytes_accessed=50 * 10**6, transcendentals=0),
        name="attend",
    )(where, seg, x, *halves, st)


def centre(v):
    c = v - jnp.mean(v, axis=-1, keepdims=True)
    r = lax.rsqrt(jnp.mean(c * c, axis=-1, keepdims=True) + EPS)
    return c * r, r


def norm_back(g, n, r):
    return r * (g - jnp.mean(g, axis=-1, keepdims=True) - n * jnp.mean(g * n, axis=-1, keepdims=True))


def col_sum(v):
    return jnp.sum(v, axis=0, keepdims=True)


GELU_A = math.sqrt(2.0 / math.pi)
GELU_B = 0.044715


def feed_kernel(me_ref, x_ref, attn_ref, cot_ref, pad_ref, bl_ref, br_ref, vec_ref, bup_ref, out_ref, dfirst_ref, dattn_ref, keep_ref, send_ref, gv_ref, gbu_ref, gb_ref, act_ref, slope_ref, up_acc, down_acc, wo_acc, wo_low, sem):
    step = pl.program_id(0)

    @pl.when(step == 0)
    def _():
        load_blocks(me_ref, (bl_ref, br_ref), gb_ref, sem)
        up_acc[...] = jnp.zeros_like(up_acc)
        down_acc[...] = jnp.zeros_like(down_acc)
        wo_acc[...] = jnp.zeros_like(wo_acc)
        gv_ref[...] = jnp.zeros_like(gv_ref)
        gbu_ref[...] = jnp.zeros_like(gbu_ref)

    keep = jnp.transpose(jnp.broadcast_to(pad_ref[0].astype(F32), (8, TILE)))[:, 0:1]
    attn = attn_ref[...]
    gain_one, gain_two = vec_ref[3:4], vec_ref[6:7]
    first_sum = x_ref[...].astype(F32) + (nt(attn, gb_ref[:, 0:D]) + vec_ref[2:3])
    norm_one, r_one = centre(first_sum)
    hidden = gain_one * norm_one + vec_ref[4:5]
    hidden_low = hidden.astype(BF)
    hidden_t = jnp.transpose(hidden_low)
    ff = jnp.zeros((TILE, D), F32)
    for start, size in FF_CHUNKS:
        cols = slice(start, start + size)
        u = nn(hidden_low, gb_ref[:, D + start : D + start + size]) + bup_ref[0:1, cols]
        u2 = u * u
        t = jnp.tanh(u * (GELU_A + GELU_A * GELU_B * u2))
        h = 0.5 + 0.5 * t
        act = (u * h).astype(BF)
        act_ref[:, cols] = act
        slope_ref[:, cols] = (h + (u * h) * (1.0 - t) * (GELU_A + 3.0 * GELU_A * GELU_B * u2)).astype(BF)
        ff = ff + nt(act, gb_ref[:, D + FF + start : D + FF + start + size])
    norm_two, r_two = centre(hidden + (ff + vec_ref[5:6]))
    out_ref[...] = ((gain_two * norm_two + vec_ref[7:8]) * keep).astype(BF)
    top = cot_ref[...].astype(F32) * keep
    gv_ref[6:7] += col_sum(top * norm_two)
    gv_ref[7:8] += col_sum(top)
    d_second = norm_back(top * gain_two, norm_two, r_two)
    d_ff = d_second.astype(BF)
    gv_ref[5:6] += col_sum(d_ff.astype(F32))
    d_ff_t = jnp.transpose(d_ff)
    d_hidden = d_second
    for start, size in FF_CHUNKS:
        cols = slice(start, start + size)
        d_act = nn(d_ff, gb_ref[:, D + FF + start : D + FF + start + size])
        d_pre = (slope_ref[:, cols].astype(F32) * d_act).astype(BF)
        gbu_ref[0:1, cols] += col_sum(d_pre.astype(F32))
        down_acc[:, cols] += nn(d_ff_t, act_ref[:, cols])
        up_acc[:, cols] += nn(hidden_t, d_pre)
        d_hidden = d_hidden + nt(d_pre, gb_ref[:, D + start : D + start + size])
    gv_ref[3:4] += col_sum(d_hidden * norm_one)
    gv_ref[4:5] += col_sum(d_hidden)
    d_first = norm_back(d_hidden * gain_one, norm_one, r_one)
    dfirst_ref[...] = d_first
    d_branch = d_first.astype(BF)
    gv_ref[2:3] += col_sum(d_branch.astype(F32))
    wo_acc[...] += nn(jnp.transpose(d_branch), attn)
    dattn_ref[...] = nn(d_branch, gb_ref[:, 0:D]).astype(BF)

    @pl.when(step == pl.num_programs(0) - 1)
    def _():
        wo_low[...] = wo_acc[...].astype(BF)
        act_ref[...] = up_acc[...].astype(BF)
        slope_ref[...] = down_acc[...].astype(BF)
        spans = ((wo_low, 0, D), (act_ref, D, FF), (slope_ref, D + FF, FF))
        store_blocks(me_ref, spans, (keep_ref, send_ref), sem)


def feed(where, x, attn, cot, pad, halves, vec, bup):
    tokens = x.shape[0]
    return pl.pallas_call(
        feed_kernel,
        grid=(tokens // TILE,),
        in_specs=[
            SCALAR,
            rows_of(TILE, D),
            rows_of(TILE, D),
            rows_of(TILE, D),
            pl.BlockSpec((1, 1, TILE), lambda i: (i, 0, 0)),
            LOOSE,
            LOOSE,
            whole((128, D)),
            whole((1, FF)),
        ],
        out_specs=[rows_of(TILE, D), rows_of(TILE, D), rows_of(TILE, D), LOOSE, LOOSE, whole((8, D)), whole((1, FF))],
        out_shape=[
            jax.ShapeDtypeStruct((tokens, D), BF),
            jax.ShapeDtypeStruct((tokens, D), F32),
            jax.ShapeDtypeStruct((tokens, D), BF),
            jax.ShapeDtypeStruct((D // 2, WB), BF),
            jax.ShapeDtypeStruct((D // 2, WB), BF),
            jax.ShapeDtypeStruct((8, D), F32),
            jax.ShapeDtypeStruct((1, FF), F32),
        ],
        scratch_shapes=[
            pltpu.VMEM((D, WB), BF),
            pltpu.VMEM((TILE, FF), BF),
            pltpu.VMEM((TILE, FF), BF),
            pltpu.VMEM((D, FF), F32),
            pltpu.VMEM((D, FF), F32),
            pltpu.VMEM((D, D), F32),
            pltpu.VMEM((D, D), BF),
            pltpu.SemaphoreType.DMA,
        ],
        compiler_params=pltpu.CompilerParams(vmem_limit_bytes=VMEM),
        cost_estimate=pl.CostEstimate(flops=80 * 10**9, bytes_accessed=40 * 10**6, transcendentals=0),
        name="feed",
    )(where, x, attn, cot, pad.reshape(tokens // TILE, 1, TILE), *halves, vec, bup)


def back_kernel(me_ref, seg_ref, x_ref, q_ref, k_ref, v_ref, mix_ref, dattn_ref, dfirst_ref, pt_ref, al_ref, ar_ref, gv_ref, extra_ref, ig_ref, keep_ref, send_ref, ga_ref, gw_ref, ds_ref, kt_ref, dqt_ref, dk_ref, dv_ref, q_acc, k_acc, v_acc, t_acc, b_acc, sem):
    step = pl.program_id(0)

    @pl.when(step == 0)
    def _():
        load_blocks(me_ref, (al_ref, ar_ref), ga_ref, sem)
        for acc in (q_acc, k_acc, v_acc, t_acc):
            acc[...] = jnp.zeros_like(acc)
        b_acc[...] = gv_ref[...]

    kt_ref[...] = jnp.transpose(k_ref[...])

    def pair(j, carry):
        lanes = pl.ds(pl.multiple_of(j * 2 * HD, 2 * HD), 2 * HD)
        d_keys = jnp.zeros((PACK, 2 * HD), F32)
        d_values = jnp.zeros((PACK, 2 * HD), F32)
        for half in range(2):
            head = 2 * j + half
            rows = pl.ds(pl.multiple_of(head * HD, HD), HD)
            values = head_lanes(v_ref[:, lanes], half)
            for start, size in Q_CHUNKS:
                cols = slice(start, start + size)
                probs = pt_ref[0, head, :, cols].astype(F32)
                d_probs = nt(values, dattn_ref[cols, lanes])
                delta = jnp.sum(probs * d_probs, axis=0, keepdims=True)
                d_scores = (probs * (d_probs - delta)).astype(BF)
                ds_ref[half, :, cols] = d_scores
                dqt_ref[rows, cols] = (nn(kt_ref[rows, :], d_scores) * SCALE).astype(BF)
            d_values = d_values + nn(pt_ref[0, head], head_lanes(dattn_ref[:, lanes], half))
            d_keys = d_keys + nn(ds_ref[half], head_lanes(q_ref[:, lanes], half))
        dk_ref[:, lanes] = d_keys.astype(BF)
        dv_ref[:, lanes] = d_values.astype(BF)
        return carry

    lax.fori_loop(0, H // 2, pair, 0)
    dq_t = dqt_ref[...]
    dq = jnp.transpose(dq_t)
    dk = dk_ref[...]
    dv = dv_ref[...]
    mixed = mix_ref[...]
    q_acc[...] += nn(dq_t, mixed)
    k_acc[...] += nn(jnp.transpose(dk), mixed)
    v_acc[...] += nn(jnp.transpose(dv), x_ref[...])
    b_acc[0:1] += col_sum(dq.astype(F32))
    b_acc[1:2] += col_sum(dv.astype(F32))
    d_mixed = nn(dq, ga_ref[:, 0:D]) + nn(dk, ga_ref[:, D : 2 * D])
    same = item_masks(seg_ref[0])
    sub = lax.broadcasted_iota(jnp.int32, (PACK, PACK), 0).astype(F32)
    first = jnp.min(jnp.where(same, sub, 1e6), axis=0, keepdims=True)
    place = lax.broadcasted_iota(jnp.int32, (1, PACK), 1).astype(F32) - first
    slot = lax.broadcasted_iota(jnp.int32, (PLACES, PACK), 0).astype(F32)
    picks_t = jnp.where(place == slot, 1.0, 0.0).astype(BF)
    t_acc[...] += nn(picks_t, d_mixed.astype(BF))
    ig_ref[...] = (dfirst_ref[...] + d_mixed + nn(dv, ga_ref[:, 2 * D : 3 * D])).astype(BF)

    @pl.when(step == pl.num_programs(0) - 1)
    def _():
        gw_ref[:, 0:D] = q_acc[...].astype(BF)
        gw_ref[:, D : 2 * D] = k_acc[...].astype(BF)
        gw_ref[:, 2 * D : 3 * D] = v_acc[...].astype(BF)
        gw_ref[:, 3 * D : WT] = jnp.transpose(t_acc[...]).astype(BF)
        extra = extra_ref[...]
        vec = jnp.concatenate([b_acc[...], jnp.zeros((extra.shape[1] - 8, D), F32)], axis=0)
        gw_ref[:, WT:] = (jnp.transpose(vec) + extra).astype(BF)
        store_blocks(me_ref, ((gw_ref, 0, gw_ref.shape[1]),), (keep_ref, send_ref), sem)


def back(where, seg, x, q, k, v, mixed, d_attn, d_first, pt, halves, gv, extra):
    packs = seg.shape[0]
    width = WT + extra.shape[1]
    tokens = packs * PACK
    return pl.pallas_call(
        back_kernel,
        grid=(packs,),
        in_specs=[SCALAR, pl.BlockSpec((1, 1, PACK), lambda i: (i, 0, 0))]
        + [rows_of(PACK, D)] * 7
        + [pl.BlockSpec((1, H, PACK, PACK), lambda i: (i, 0, 0, 0)), LOOSE, LOOSE, whole((8, D)), whole(extra.shape)],
        out_specs=[rows_of(PACK, D), LOOSE, LOOSE],
        out_shape=[jax.ShapeDtypeStruct((tokens, D), BF)] + [jax.ShapeDtypeStruct((D // 2, width), BF)] * 2,
        scratch_shapes=[
            pltpu.VMEM((D, WA), BF),
            pltpu.VMEM((D, width), BF),
            pltpu.VMEM((2, PACK, PACK), BF),
            pltpu.VMEM((D, PACK), BF),
            pltpu.VMEM((D, PACK), BF),
            pltpu.VMEM((PACK, D), BF),
            pltpu.VMEM((PACK, D), BF),
            pltpu.VMEM((D, D), F32),
            pltpu.VMEM((D, D), F32),
            pltpu.VMEM((D, D), F32),
            pltpu.VMEM((PLACES, D), F32),
            pltpu.VMEM((8, D), F32),
            pltpu.SemaphoreType.DMA,
        ],
        compiler_params=pltpu.CompilerParams(vmem_limit_bytes=VMEM),
        cost_estimate=pl.CostEstimate(flops=60 * 10**9, bytes_accessed=50 * 10**6, transcendentals=0),
        name="back",
    )(where, seg, x, q, k, v, mixed, d_attn, d_first, pt, *halves, gv, extra)


def sines():
    half = D // 2
    frequency = jnp.exp(jnp.arange(half, dtype=F32) * (-2.0 * math.log(10000.0) / D))
    angles = frequency[:, None] * jnp.arange(PLACES, dtype=F32)[None, :]
    return jnp.concatenate([jnp.sin(angles), jnp.cos(angles)], axis=0)


def bit_groups(count):
    bits = count.bit_length() - 1
    return [(0,)] + [tuple(range(at, min(at + 2, bits))) for at in range(1, bits, 2)]


def offsets(count):
    found = [0]
    for group in bit_groups(count):
        found = [old | mask for old in found for mask in masks(group)]
    return found


def masks(group):
    return [index << group[0] for index in range(1 << len(group))]


def swap(block, mask, count):
    return lax.ppermute(block, AXES, [(i, i ^ mask) for i in range(count)])


def gather_phase(own, group, count):
    return [own] + [swap(own, mask, count) for mask in masks(group)[1:]]


def scatter_phase(pieces, group, count):
    total = pieces[0].astype(F32)
    for piece, mask in zip(pieces[1:], masks(group)[1:]):
        total = total + swap(piece, mask, count).astype(F32)
    return total


def split_rows(block, count):
    rows = block.shape[0] // count
    return [block[at * rows : (at + 1) * rows] for at in range(count)]


def scatter_rest(block, groups, count):
    for group in groups:
        block = scatter_phase(split_rows(block.astype(BF), 1 << len(group)), group, count)
    return block


def local(
    inputs,
    segments,
    pad_mask,
    cotangent,
    w_query,
    b_query,
    w_key,
    w_value,
    b_value,
    w_out,
    b_out,
    gain_one,
    shift_one,
    w_up,
    b_up,
    w_down,
    b_down,
    gain_two,
    shift_two,
    pos_table,
):
    tokens = inputs.shape[0]
    narrow = lax.axis_size("narrow")
    wide = lax.axis_size("wide")
    count = wide * narrow
    me = lax.axis_index(AXES)
    groups = bit_groups(count)
    own_rows = D // count
    bits = count.bit_length() - 1
    places = [bits - 1 - bit for group in groups for bit in reversed(group)] + [bits, bits + 1]
    in_kernel = own_rows == BLOCK
    where = (me if in_kernel else jnp.zeros((), jnp.int32)).reshape(1).astype(jnp.int32)

    def flips(full):
        for axis in range(bits):
            mine = (me >> (bits - 1 - axis)) & 1
            full = jnp.where(mine == 1, jnp.flip(full, axis), full)
        return full

    def absolute(halves):
        if in_kernel:
            return halves
        full = jnp.concatenate(halves, axis=0).reshape([2] * bits + [own_rows, -1])
        full = flips(full.transpose([places.index(axis) for axis in range(bits + 2)])).reshape(D, -1)
        return full[: D // 2], full[D // 2 :]

    def relative(halves):
        if in_kernel:
            return halves
        full = flips(jnp.concatenate(halves, axis=0).reshape([2] * bits + [own_rows, -1]))
        full = full.transpose(places).reshape(D, -1)
        return full[: D // 2], full[D // 2 :]

    seg = segments.reshape(tokens // PACK, 1, PACK)
    bias_width = b_up.shape[0]
    bias_piece = -(-bias_width // wide)
    piece_cols = -(-bias_piece // own_rows)
    bias_own = jnp.pad(b_up, (0, bias_piece * wide - bias_width))
    bias_own = lax.dynamic_slice_in_dim(bias_own, lax.axis_index("wide") * bias_piece, bias_piece)
    bias_own = jnp.pad(bias_own, (0, piece_cols * own_rows - bias_piece)).reshape(piece_cols, own_rows)
    rows = jnp.stack([b_query, b_value, b_out, gain_one, shift_one, b_down, gain_two, shift_two], axis=0)
    rows = jnp.concatenate([rows, bias_own, jnp.zeros((120 - piece_cols, own_rows), BF)], axis=0)
    table = jnp.pad(pos_table, ((0, PLACES - LONG), (0, 0)))
    own_a = jnp.concatenate([w_query, w_key, w_value, table, rows], axis=0).T
    own_b = jnp.concatenate([w_out.T, w_up, w_down.T], axis=1)

    for group in reversed(groups[1:]):
        own_a = jnp.concatenate(gather_phase(own_a, group, count), axis=0)
    a_halves = absolute(tuple(gather_phase(own_a, groups[0], count)))
    for group in reversed(groups[1:]):
        own_b = jnp.concatenate(gather_phase(own_b, group, count), axis=0)
    b_halves = absolute(tuple(gather_phase(own_b, groups[0], count)))

    q, k, v, mixed, attn, pt, vec = attend(where, seg, inputs, a_halves, sines())
    bup = vec[8 : 8 + piece_cols].reshape(piece_cols, wide, narrow, own_rows)
    bup = bup.transpose(2, 1, 0, 3).reshape(narrow, wide, piece_cols * own_rows)[:, :, :bias_piece]
    bup = bup.reshape(narrow, wide * bias_piece)[:, :bias_width].reshape(1, FF)
    layer_out, d_first, d_attn, keep_b, send_b, gv, gbu = feed(where, inputs, attn, cotangent, pad_mask, b_halves, vec, bup)
    grad_cols = -(-bias_width // own_rows)
    extra = jnp.pad(gbu.reshape(narrow, bias_width), ((0, 0), (0, grad_cols * own_rows - bias_width)))
    extra = jnp.broadcast_to(extra.reshape(1, narrow, own_rows, grad_cols), (wide, narrow, own_rows, grad_cols))
    extra_width = -(-(8 + grad_cols) // 128) * 128
    extra = jnp.pad(extra.reshape(D, grad_cols), ((0, 0), (8, extra_width - 8 - grad_cols)))
    own_grad_b = scatter_phase(relative((keep_b, send_b)), groups[0], count)
    own_grad_b = scatter_rest(own_grad_b, groups[1:], count)
    input_grad, keep_a, send_a = back(where, seg, inputs, q, k, v, mixed, d_attn, d_first, pt, a_halves, gv, extra)
    own_grad_a = scatter_phase(relative((keep_a, send_a)), groups[0], count)
    own_grad_a = scatter_rest(own_grad_a, groups[1:], count)
    grad_b_up = own_grad_a[:, WT + 8 : WT + 8 + grad_cols].reshape(grad_cols * own_rows)[:bias_width]
    own_vec = own_grad_a[:, WT : WT + 8]
    return (
        layer_out,
        input_grad,
        own_grad_a[:, 0:D].T,
        own_vec[:, 0],
        own_grad_a[:, D : 2 * D].T,
        own_grad_a[:, 2 * D : 3 * D].T,
        own_vec[:, 1],
        own_grad_b[:, 0:D].T,
        own_vec[:, 2],
        own_vec[:, 3],
        own_vec[:, 4],
        own_grad_b[:, D : D + FF],
        grad_b_up,
        own_grad_b[:, D + FF :].T,
        own_vec[:, 5],
        own_vec[:, 6],
        own_vec[:, 7],
        own_grad_a[:, 3 * D : 3 * D + LONG].T,
    )


def solution(mesh):
    both = P(("wide", "narrow"))
    rows = P(("wide", "narrow"), None)
    cols = P(None, ("wide", "narrow"))
    in_specs = (rows, both, both, rows, cols, both, cols, cols, both, cols, both, both, both, rows, P("narrow"), cols, both, both, both, cols)
    out_specs = (rows, rows, cols, both, cols, cols, both, cols, both, both, both, rows, P("narrow"), cols, both, both, both, cols)
    return jax.shard_map(local, mesh=mesh, in_specs=in_specs, out_specs=out_specs, check_vma=False)
```

time: 898 us -> 417 us (0.46); the launches traced: 887 us -> 416 us
  matrix products: 288 us -> 0 us
  Pallas kernels: 0 us -> 236 us
  waiting for transfers between devices: 301 us -> 98.2 us
  local copies, waits for them, and re-layouts: 122 us -> 30.9 us
  blocking collectives: 88.3 us -> 0 us
  other arithmetic: 72.2 us -> 11.9 us
  starting transfers between devices: 0.2 us -> 38.9 us
  between operations: 15.2 us -> 0.94 us
    dot_general x48 -> x0, matrix products: 288 us -> none  [the longest x6 70.7 us: cols_inner(): lax.dot_general(left_op, right_op, (((1,), (1,)), ((), ())), preferred_el...]
    pallas_call x0 -> x3, Pallas kernels: none -> 236 us  [the longest x1 85.6 us: feed(): pl.pallas_call(feed_kernel, grid=(tokens // TILE,), in_specs=[SCALAR, row...]
    unnamed x7 -> x0, waiting for transfers between devices: 159 us -> none
    reduce_scatter x1 -> x0, waiting for transfers between devices: 142 us -> none  [local(): lax.psum_scatter(d_up, ('wide', 'narrow'), scatter_dimension=0, tiled=True)]
    ppermute x0 -> x28, waiting for transfers between devices: none -> 98.2 us  [swap(): return lax.ppermute(block, AXES, [(i, i ^ mask) for i in range(count)])]
    all_gather x1 -> x0, blocking collectives: 41.3 us -> none  [local(): lax.all_gather(vectors, ('wide', 'narrow'), axis=1, tiled=True)]
    ppermute x0 -> x28, starting transfers between devices: none -> 38.9 us  [swap(): return lax.ppermute(block, AXES, [(i, i ^ mask) for i in range(count)])]
    psum x1 -> x0, blocking collectives: 38.3 us -> none  [local(): bias_total = lax.psum(d_bias_up, ('wide', 'narrow'))]
  transfers between devices with their start and end apart: 5 -> 28, of which waited for: 3 -> 14; matrix products, arithmetic and copies ran while one was open for 23% -> 6% of each run, Pallas kernels for 0% -> 36%
where the time goes in v1:
time: 417 us; the launch traced here: 416 us
  Pallas kernels  236 us (57%)
  waiting for transfers between devices  98.2 us (24%)
  starting transfers between devices  38.9 us (9%)
  local copies, waits for them, and re-layouts  30.9 us (7%)
  other arithmetic  11.9 us (3%)
    ppermute x28, waiting for transfers between devices, swap(): return lax.ppermute(block, AXES, [(i, i ^ mask) for i in range(count)])  98.2 us
    pallas_call x1, Pallas kernels, feed(): pl.pallas_call(feed_kernel, grid=(tokens // TILE,), in_specs=[SCALAR, row...  85.6 us
    pallas_call x1, Pallas kernels, back(): pl.pallas_call(back_kernel, grid=(packs,), in_specs=[SCALAR, pl.BlockSpec...  80.8 us
    pallas_call x1, Pallas kernels, attend(): pl.pallas_call(attend_kernel, grid=(packs,), in_specs=[SCALAR, pl.BlockSp...  69.2 us
    ppermute x28, starting transfers between devices, swap(): return lax.ppermute(block, AXES, [(i, i ^ mask) for i in range(count)])  38.9 us
  transfers between devices with their start and end apart: 28, of which 14 were waited for; matrix products, arithmetic and copies ran while one was open for 6% of the time, Pallas kernels for 36%

profile of v1, /device:TPU:0, one launch (start us, length us, event | category | flops | bytes accessed | tf_op | source)
XLA Modules:
  0.0 416.3 jit_solution(6903873267727191781)
XLA Ops:
  9.2 5.1 %collective-permute-start.2 = (bf16[16,2048]{1,0:T(8,128)(2,1)S(1)}, bf16[16,2048]{1,0:T(8,128)(2,1)S(1)}, u32[]{:S(2)}, u32[]{:S(2)}) collective-permute-start(bf16[16,2048]{1,0:T(8,128)(2,1)S(1)} %bitcast.31), channel_id=1, source_target_pairs={{0,24},{1,25},{2,26},{3,27},{4,28},{5,29},{6,30},{7,31},{8,16},{9,... | collective-permute-start | bytes 196616 | tf_op jit(solution)/shard_map/ppermute | solution.py:419
  15.0 1.7 pad_maximum_fusion.3
  16.7 2.3 collective-permute-start.8
  18.9 2.0 collective-permute-start.7
  26.1 2.7 collective-permute-start.5
  29.3 1.8 collective-permute-done.8
  31.1 1.7 collective-permute-start.3
  32.8 2.5 collective-permute-done.9
  35.4 2.5 collective-permute-start.12
  40.5 18.4 %collective-permute-done.3 = bf16[64,2048]{1,0:T(8,128)(2,1)S(1)} collective-permute-done((bf16[64,2048]{1,0:T(8,128)(2,1)S(1)}, bf16[64,2048]{1,0:T(8,128)(2,1)S(1)}, u32[]{:S(2)}, u32[]{:S(2)}) %collective-permute-start.3) | collective-permute-done | bytes 262176 | tf_op jit(solution)/shard_map/ppermute | solution.py:419
  58.9 2.5 collective-permute-start.11
  61.5 15.9 %collective-permute-done.10 = bf16[64,6912]{1,0:T(8,128)(2,1)S(1)} collective-permute-done((bf16[64,6912]{1,0:T(8,128)(2,1)S(1)}, bf16[64,6912]{1,0:T(8,128)(2,1)S(1)}, u32[]{:S(2)}, u32[]{:S(2)}) %collective-permute-start.10) | collective-permute-done | bytes 884768 | tf_op jit(solution)/shard_map/ppermute | solution.py:419
  81.5 69.2 %attend.1 = (bf16[2560,512]{1,0:T(8,128)(2,1)}, bf16[2560,512]{1,0:T(8,128)(2,1)}, bf16[2560,512]{1,0:T(8,128)(2,1)}, bf16[2560,512]{1,0:T(8,128)(2,1)}, bf16[25...) custom-call(s32[1]{0:T(128)} %bitcast.me_ref, s32[4,1,640]{2,1,0:T(1,128)} %reshape.70.seg_ref, ...), custom_call_target="tpu_custom_call" | custom-call | flops 40000000000 | bytes 50000000 | tf_op jit(solution)/shard_map/attend/pallas_call | solution.py:147
  152.4 85.6 %feed.1 = (bf16[2560,512]{1,0:T(8,128)(2,1)}, f32[2560,512]{1,0:T(8,128)}, bf16[2560,512]{1,0:T(8,128)(2,1)}, bf16[256,6912]{1,0:T(8,128)(2,1)}, bf16[256,6912]{...) custom-call(s32[1]{0:T(128)} %bitcast.me_ref, bf16[2560,512]{1,0:T(8,128)(2,1)} %x_ref.5, ...), custom_call_target="tpu_custom_call" | custom-call | flops 80000000000 | bytes 40000000 | tf_op jit(solution)/shard_map/feed/pallas_call | solution.py:255
  240.3 80.8 %back.1 = (bf16[2560,512]{1,0:T(8,128)(2,1)}, bf16[256,2048]{1,0:T(8,128)(2,1)}, bf16[256,2048]{1,0:T(8,128)(2,1)}) custom-call(s32[1]{0:T(128)} %bitcast.me_ref, s32[4,1,640]{2,1,0:T(1,128)} %reshape.70.seg_ref, bf16[2560,512]{1,0:T(8,128)(2,1)} %x_ref.5, bf16[2560,512]{1,0:T(8,128)(2,1)} %get-tuple-element.38.q_ref, ...), custom_call_target="tpu_custom_call" | custom-call | flops 60000002048 | bytes 50000000 | tf_op jit(solution)/shard_map/back/pallas_call | solution.py:366
  321.2 2.8 collective-permute-done.14
  324.0 1.6 add_convert_fusion.1
  325.7 1.6 collective-permute-start.15
  329.3 10.5 %collective-permute-done.15 = bf16[64,2048]{1,0:T(8,128)(2,1)S(1)} collective-permute-done((bf16[64,2048]{1,0:T(8,128)(2,1)S(1)}, bf16[64,2048]{1,0:T(8,128)(2,1)S(1)}, u32[]{:S(2)}, u32[]{:S(2)}) %collective-permute-start.15) | collective-permute-done | bytes 262176 | tf_op jit(solution)/shard_map/ppermute | solution.py:419
  341.1 3.1 collective-permute-start.18
  344.2 1.8 copy-done.1
  346.0 3.0 add_convert_fusion
  354.0 3.4 collective-permute-start.20
  357.4 2.8 collective-permute-done.20
  360.2 2.4 collective-permute-done.19
  364.0 1.8 slice_reduce_fusion
  367.3 22.9 %collective-permute-done.22 = bf16[64,6912]{1,0:T(8,128)(2,1)} collective-permute-done((bf16[64,6912]{1,0:T(8,128)(2,1)}, bf16[64,6912]{1,0:T(8,128)(2,1)}, u32[]{:S(2)}, u32[]{:S(2)}) %collective-permute-start.22) | collective-permute-done | bytes 884768 | tf_op jit(solution)/shard_map/ppermute | solution.py:419
  391.3 2.1 add_convert_fusion.2
  393.9 3.8 collective-permute-start.27
  399.0 3.8 collective-permute-done.25
  402.8 4.9 %collective-permute-done.27 = bf16[16,6912]{1,0:T(8,128)(2,1)S(1)} collective-permute-done((bf16[16,6912]{1,0:T(8,128)(2,1)S(1)}, bf16[16,6912]{1,0:T(8,128)(2,1)S(1)}, u32[]{:S(2)}, u32[]{:S(2)}) %collective-permute-start.27) | collective-permute-done | bytes 221216 | tf_op jit(solution)/shard_map/ppermute | solution.py:419
  407.7 7.1 %collective-permute-done.26 = bf16[16,6912]{1,0:T(8,128)(2,1)S(1)} collective-permute-done((bf16[16,6912]{1,0:T(8,128)(2,1)S(1)}, bf16[16,6912]{1,0:T(8,128)(2,1)S(1)}, u32[]{:S(2)}, u32[]{:S(2)}) %collective-permute-start.26) | collective-permute-done | bytes 221216 | tf_op jit(solution)/shard_map/ppermute | solution.py:419
  (105 shorter events, 41.6 us)
Async XLA Ops:
  0.7 34.6 %copy-start.4 = (bf16[16,3200]{1,0:T(8,128)(2,1)S(1)}, bf16[16,3200]{1,0:T(8,128)(2,1)}, u32[]{:S(2)}) copy-start(bf16[16,3200]{1,0:T(8,128)(2,1)} %param.33) | copy-start | bytes 307204
  0.7 34.6 %copy-start.3 = (bf16[3200,16]{0,1:T(8,128)(2,1)S(1)}, bf16[3200,16]{0,1:T(8,128)(2,1)}, u32[]{:S(2)}) copy-start(bf16[3200,16]{0,1:T(8,128)(2,1)} %param.35) | copy-start | bytes 307204
  0.7 34.6 %copy-start.5 = (bf16[512,16]{0,1:T(8,128)(2,1)S(1)}, bf16[512,16]{0,1:T(8,128)(2,1)}, u32[]{:S(2)}) copy-start(bf16[512,16]{0,1:T(8,128)(2,1)} %param.29) | copy-start | bytes 49156
  9.2 16.8 %collective-permute-start.2 = (bf16[16,2048]{1,0:T(8,128)(2,1)S(1)}, bf16[16,2048]{1,0:T(8,128)(2,1)S(1)}, u32[]{:S(2)}, u32[]{:S(2)}) collective-permute-start(bf16[16,2048]{1,0:T(8,128)(2,1)S(1)} %bitcast.31), channel_id=1, source_target_pairs={{0,24},{1,25},{2,26},{3,27},{4,28},{5,29},{6,30},{7,31},{8,16},{9,... | collective-permute-start | bytes 196616 | tf_op jit(solution)/shard_map/ppermute | solution.py:419
  14.4 11.7 %collective-permute-start.1 = (bf16[16,2048]{1,0:T(8,128)(2,1)S(1)}, bf16[16,2048]{1,0:T(8,128)(2,1)S(1)}, u32[]{:S(2)}, u32[]{:S(2)}) collective-permute-start(bf16[16,2048]{1,0:T(8,128)(2,1)S(1)} %bitcast.32), channel_id=1, source_target_pairs={{0,16},{1,17},{2,18},{3,19},{4,20},{5,21},{6,22},{7,23},{8,24},{9,... | collective-permute-start | bytes 196616 | tf_op jit(solution)/shard_map/ppermute | solution.py:419
  14.4 11.7 %collective-permute-start = (bf16[16,2048]{1,0:T(8,128)(2,1)S(1)}, bf16[16,2048]{1,0:T(8,128)(2,1)S(1)}, u32[]{:S(2)}, u32[]{:S(2)}) collective-permute-start(bf16[16,2048]{1,0:T(8,128)(2,1)S(1)} %bitcast.33), channel_id=1, source_target_pairs={{0,8},{1,9},{2,10},{3,11},{4,12},{5,13},{6,14},{7,15},{8,0},{9,1},... | collective-permute-start | bytes 196616 | tf_op jit(solution)/shard_map/ppermute | solution.py:419
  16.7 14.5 %collective-permute-start.8 = (bf16[16,6912]{1,0:T(8,128)(2,1)S(1)}, bf16[16,6912]{1,0:T(8,128)(2,1)S(1)}, u32[]{:S(2)}, u32[]{:S(2)}) collective-permute-start(bf16[16,6912]{1,0:T(8,128)(2,1)S(1)} %get-tuple-element.74), channel_id=1, source_target_pairs={{0,16},{1,17},{2,18},{3,19},{4,20},{5,21},{6,22},{7,23},{8,24},{9,... | collective-permute-start | bytes 663560 | tf_op jit(solution)/shard_map/ppermute | solution.py:419
  18.9 13.8 %collective-permute-start.7 = (bf16[16,6912]{1,0:T(8,128)(2,1)S(1)}, bf16[16,6912]{1,0:T(8,128)(2,1)S(1)}, u32[]{:S(2)}, u32[]{:S(2)}) collective-permute-start(bf16[16,6912]{1,0:T(8,128)(2,1)S(1)} %get-tuple-element.74), channel_id=1, source_target_pairs={{0,8},{1,9},{2,10},{3,11},{4,12},{5,13},{6,14},{7,15},{8,0},{9,1},... | collective-permute-start | bytes 663560 | tf_op jit(solution)/shard_map/ppermute | solution.py:419
  26.0 9.3 %collective-permute-start.9 = (bf16[16,6912]{1,0:T(8,128)(2,1)S(1)}, bf16[16,6912]{1,0:T(8,128)(2,1)S(1)}, u32[]{:S(2)}, u32[]{:S(2)}) collective-permute-start(bf16[16,6912]{1,0:T(8,128)(2,1)S(1)} %get-tuple-element.74), channel_id=1, source_target_pairs={{0,24},{1,25},{2,26},{3,27},{4,28},{5,29},{6,30},{7,31},{8,16},{9,... | collective-permute-start | bytes 663560 | tf_op jit(solution)/shard_map/ppermute | solution.py:419
  26.1 35.3 %collective-permute-start.5 = (bf16[64,2048]{1,0:T(8,128)(2,1)S(1)}, bf16[64,2048]{1,0:T(8,128)(2,1)S(1)}, u32[]{:S(2)}, u32[]{:S(2)}) collective-permute-start(bf16[64,2048]{1,0:T(8,128)(2,1)S(1)} %pad_maximum_fusion.2), channel_id=1, source_target_pairs={{0,6},{1,7},{2,4},{3,5},{4,2},{5,3},{6,0},{7,1},{8,14},{9,15},{10,... | collective-permute-start | bytes 786440 | tf_op jit(solution)/shard_map/ppermute | solution.py:419
  28.8 32.6 %collective-permute-start.4 = (bf16[64,2048]{1,0:T(8,128)(2,1)S(1)}, bf16[64,2048]{1,0:T(8,128)(2,1)S(1)}, u32[]{:S(2)}, u32[]{:S(2)}) collective-permute-start(bf16[64,2048]{1,0:T(8,128)(2,1)S(1)} %pad_maximum_fusion.2), channel_id=1, source_target_pairs={{0,4},{1,5},{2,6},{3,7},{4,0},{5,1},{6,2},{7,3},{8,12},{9,13},{10,... | collective-permute-start | bytes 786440 | tf_op jit(solution)/shard_map/ppermute | solution.py:419
  31.1 27.7 %collective-permute-start.3 = (bf16[64,2048]{1,0:T(8,128)(2,1)S(1)}, bf16[64,2048]{1,0:T(8,128)(2,1)S(1)}, u32[]{:S(2)}, u32[]{:S(2)}) collective-permute-start(bf16[64,2048]{1,0:T(8,128)(2,1)S(1)} %pad_maximum_fusion.2), channel_id=1, source_target_pairs={{0,2},{1,3},{2,0},{3,1},{4,6},{5,7},{6,4},{7,5},{8,10},{9,11},{10,... | collective-permute-start | bytes 786440 | tf_op jit(solution)/shard_map/ppermute | solution.py:419
  35.4 44.1 %collective-permute-start.12 = (bf16[64,6912]{1,0:T(8,128)(2,1)S(1)}, bf16[64,6912]{1,0:T(8,128)(2,1)S(1)}, u32[]{:S(2)}, u32[]{:S(2)}) collective-permute-start(bf16[64,6912]{1,0:T(8,128)(2,1)S(1)} %pad_maximum_fusion), channel_id=1, source_target_pairs={{0,6},{1,7},{2,4},{3,5},{4,2},{5,3},{6,0},{7,1},{8,14},{9,15},{10,... | collective-permute-start | bytes 2654216 | tf_op jit(solution)/shard_map/ppermute | solution.py:419
  37.9 39.5 %collective-permute-start.10 = (bf16[64,6912]{1,0:T(8,128)(2,1)S(1)}, bf16[64,6912]{1,0:T(8,128)(2,1)S(1)}, u32[]{:S(2)}, u32[]{:S(2)}) collective-permute-start(bf16[64,6912]{1,0:T(8,128)(2,1)S(1)} %pad_maximum_fusion), channel_id=1, source_target_pairs={{0,2},{1,3},{2,0},{3,1},{4,6},{5,7},{6,4},{7,5},{8,10},{9,11},{10,... | collective-permute-start | bytes 2654216 | tf_op jit(solution)/shard_map/ppermute | solution.py:419
  58.9 19.6 %collective-permute-start.11 = (bf16[64,6912]{1,0:T(8,128)(2,1)S(1)}, bf16[64,6912]{1,0:T(8,128)(2,1)S(1)}, u32[]{:S(2)}, u32[]{:S(2)}) collective-permute-start(bf16[64,6912]{1,0:T(8,128)(2,1)S(1)} %pad_maximum_fusion), channel_id=1, source_target_pairs={{0,4},{1,5},{2,6},{3,7},{4,0},{5,1},{6,2},{7,3},{8,12},{9,13},{10,... | collective-permute-start | bytes 2654216 | tf_op jit(solution)/shard_map/ppermute | solution.py:419
  61.4 19.0 %collective-permute-start.6 = (bf16[256,2048]{1,0:T(8,128)(2,1)S(1)}, bf16[256,2048]{1,0:T(8,128)(2,1)S(1)}, u32[]{:S(2)}, u32[]{:S(2)}) collective-permute-start(bf16[256,2048]{1,0:T(8,128)(2,1)S(1)} %constant_dynamic-update-slice_fusion.al_ref), channel_id=1, source_target_pairs={{0,1},{1,0},{2,3},{3,2},{4,5},{5,4},{6,7},{7,6},{8,9},{9,8},{10,11... | collective-permute-start | bytes 3145736 | tf_op jit(solution)/shard_map/ppermute | solution.py:419
  80.4 71.9 %collective-permute-start.13 = (bf16[256,6912]{1,0:T(8,128)(2,1)}, bf16[256,6912]{1,0:T(8,128)(2,1)}, u32[]{:S(2)}, u32[]{:S(2)}) collective-permute-start(bf16[256,6912]{1,0:T(8,128)(2,1)} %constant_dynamic-update-slice_fusion.7.bl_ref), channel_id=1, source_target_pairs={{0,1},{1,0},{2,3},{3,2},{4,5},{5,4},{6,7},{7,6},{8,9},{9,8},{10,11... | collective-permute-start | bytes 10616840 | tf_op jit(solution)/shard_map/ppermute | solution.py:419
  238.9 105.4 %collective-permute-start.21 = (bf16[256,6912]{1,0:T(8,128)(2,1)}, bf16[256,6912]{1,0:T(8,128)(2,1)S(1)}, u32[]{:S(2)}, u32[]{:S(2)}) collective-permute-start(bf16[256,6912]{1,0:T(8,128)(2,1)} %get-tuple-element.51), channel_id=1, source_target_pairs={{0,1},{1,0},{2,3},{3,2},{4,5},{5,4},{6,7},{7,6},{8,9},{9,8},{10,11... | collective-permute-start | bytes 10616840 | tf_op jit(solution)/shard_map/ppermute | solution.py:419
  321.1 24.9 %copy-start = (bf16[256,6912]{1,0:T(8,128)(2,1)S(1)}, bf16[256,6912]{1,0:T(8,128)(2,1)}, u32[]{:S(2)}) copy-start(bf16[256,6912]{1,0:T(8,128)(2,1)} %get-tuple-element.50) | copy-start | bytes 10616836
  321.1 2.9 collective-permute-start.14
  325.7 14.0 %collective-permute-start.15 = (bf16[64,2048]{1,0:T(8,128)(2,1)S(1)}, bf16[64,2048]{1,0:T(8,128)(2,1)S(1)}, u32[]{:S(2)}, u32[]{:S(2)}) collective-permute-start(bf16[64,2048]{1,0:T(8,128)(2,1)S(1)} %get-tuple-element.63), channel_id=1, source_target_pairs={{0,2},{1,3},{2,0},{3,1},{4,6},{5,7},{6,4},{7,5},{8,10},{9,11},{10,... | collective-permute-start | bytes 786440 | tf_op jit(solution)/shard_map/ppermute | solution.py:419
  327.3 12.4 %collective-permute-start.17 = (bf16[64,2048]{1,0:T(8,128)(2,1)S(1)}, bf16[64,2048]{1,0:T(8,128)(2,1)S(1)}, u32[]{:S(2)}, u32[]{:S(2)}) collective-permute-start(bf16[64,2048]{1,0:T(8,128)(2,1)S(1)} %get-tuple-element.64), channel_id=1, source_target_pairs={{0,6},{1,7},{2,4},{3,5},{4,2},{5,3},{6,0},{7,1},{8,14},{9,15},{10,... | collective-permute-start | bytes 786440 | tf_op jit(solution)/shard_map/ppermute | solution.py:419
  328.8 12.2 %collective-permute-start.16 = (bf16[64,2048]{1,0:T(8,128)(2,1)S(1)}, bf16[64,2048]{1,0:T(8,128)(2,1)S(1)}, u32[]{:S(2)}, u32[]{:S(2)}) collective-permute-start(bf16[64,2048]{1,0:T(8,128)(2,1)S(1)} %get-tuple-element.65), channel_id=1, source_target_pairs={{0,4},{1,5},{2,6},{3,7},{4,0},{5,1},{6,2},{7,3},{8,12},{9,13},{10,... | collective-permute-start | bytes 786440 | tf_op jit(solution)/shard_map/ppermute | solution.py:419
  341.1 16.3 %collective-permute-start.18 = (bf16[16,2048]{1,0:T(8,128)(2,1)S(1)}, bf16[16,2048]{1,0:T(8,128)(2,1)S(1)}, u32[]{:S(2)}, u32[]{:S(2)}) collective-permute-start(bf16[16,2048]{1,0:T(8,128)(2,1)S(1)} %get-tuple-element.71), channel_id=1, source_target_pairs={{0,8},{1,9},{2,10},{3,11},{4,12},{5,13},{6,14},{7,15},{8,0},{9,1},... | collective-permute-start | bytes 196616 | tf_op jit(solution)/shard_map/ppermute | solution.py:419
  350.5 39.6 %collective-permute-start.22 = (bf16[64,6912]{1,0:T(8,128)(2,1)}, bf16[64,6912]{1,0:T(8,128)(2,1)}, u32[]{:S(2)}, u32[]{:S(2)}) collective-permute-start(bf16[64,6912]{1,0:T(8,128)(2,1)} %get-tuple-element.60), channel_id=1, source_target_pairs={{0,2},{1,3},{2,0},{3,1},{4,6},{5,7},{6,4},{7,5},{8,10},{9,11},{10,... | collective-permute-start | bytes 2654216 | tf_op jit(solution)/shard_map/ppermute | solution.py:419
  352.0 38.1 %collective-permute-start.24 = (bf16[64,6912]{1,0:T(8,128)(2,1)}, bf16[64,6912]{1,0:T(8,128)(2,1)}, u32[]{:S(2)}, u32[]{:S(2)}) collective-permute-start(bf16[64,6912]{1,0:T(8,128)(2,1)} %get-tuple-element.61), channel_id=1, source_target_pairs={{0,6},{1,7},{2,4},{3,5},{4,2},{5,3},{6,0},{7,1},{8,14},{9,15},{10,... | collective-permute-start | bytes 2654216 | tf_op jit(solution)/shard_map/ppermute | solution.py:419
  353.5 37.9 %collective-permute-start.23 = (bf16[64,6912]{1,0:T(8,128)(2,1)}, bf16[64,6912]{1,0:T(8,128)(2,1)}, u32[]{:S(2)}, u32[]{:S(2)}) collective-permute-start(bf16[64,6912]{1,0:T(8,128)(2,1)} %get-tuple-element.62), channel_id=1, source_target_pairs={{0,4},{1,5},{2,6},{3,7},{4,0},{5,1},{6,2},{7,3},{8,12},{9,13},{10,... | collective-permute-start | bytes 2654216 | tf_op jit(solution)/shard_map/ppermute | solution.py:419
  354.0 6.2 %collective-permute-start.20 = (bf16[16,2048]{1,0:T(8,128)(2,1)S(1)}, bf16[16,2048]{1,0:T(8,128)(2,1)S(1)}, u32[]{:S(2)}, u32[]{:S(2)}) collective-permute-start(bf16[16,2048]{1,0:T(8,128)(2,1)S(1)} %get-tuple-element.72), channel_id=1, source_target_pairs={{0,24},{1,25},{2,26},{3,27},{4,28},{5,29},{6,30},{7,31},{8,16},{9,... | collective-permute-start | bytes 196616 | tf_op jit(solution)/shard_map/ppermute | solution.py:419
  357.4 5.2 %collective-permute-start.19 = (bf16[16,2048]{1,0:T(8,128)(2,1)S(1)}, bf16[16,2048]{1,0:T(8,128)(2,1)S(1)}, u32[]{:S(2)}, u32[]{:S(2)}) collective-permute-start(bf16[16,2048]{1,0:T(8,128)(2,1)S(1)} %get-tuple-element.73), channel_id=1, source_target_pairs={{0,16},{1,17},{2,18},{3,19},{4,20},{5,21},{6,22},{7,23},{8,24},{9,... | collective-permute-start | bytes 196616 | tf_op jit(solution)/shard_map/ppermute | solution.py:419
  393.5 9.3 %collective-permute-start.25 = (bf16[16,6912]{1,0:T(8,128)(2,1)S(1)}, bf16[16,6912]{1,0:T(8,128)(2,1)S(1)}, u32[]{:S(2)}, u32[]{:S(2)}) collective-permute-start(bf16[16,6912]{1,0:T(8,128)(2,1)S(1)} %get-tuple-element.66), channel_id=1, source_target_pairs={{0,8},{1,9},{2,10},{3,11},{4,12},{5,13},{6,14},{7,15},{8,0},{9,1},... | collective-permute-start | bytes 663560 | tf_op jit(solution)/shard_map/ppermute | solution.py:419
  393.9 13.8 %collective-permute-start.27 = (bf16[16,6912]{1,0:T(8,128)(2,1)S(1)}, bf16[16,6912]{1,0:T(8,128)(2,1)S(1)}, u32[]{:S(2)}, u32[]{:S(2)}) collective-permute-start(bf16[16,6912]{1,0:T(8,128)(2,1)S(1)} %get-tuple-element.67), channel_id=1, source_target_pairs={{0,24},{1,25},{2,26},{3,27},{4,28},{5,29},{6,30},{7,31},{8,16},{9,... | collective-permute-start | bytes 663560 | tf_op jit(solution)/shard_map/ppermute | solution.py:419
  397.7 17.2 %collective-permute-start.26 = (bf16[16,6912]{1,0:T(8,128)(2,1)S(1)}, bf16[16,6912]{1,0:T(8,128)(2,1)S(1)}, u32[]{:S(2)}, u32[]{:S(2)}) collective-permute-start(bf16[16,6912]{1,0:T(8,128)(2,1)S(1)} %get-tuple-element.68), channel_id=1, source_target_pairs={{0,16},{1,17},{2,18},{3,19},{4,20},{5,21},{6,22},{7,23},{8,24},{9,... | collective-permute-start | bytes 663560 | tf_op jit(solution)/shard_map/ppermute | solution.py:419
  (4 other events, 22.5 us)

commit v2 on v1

v2 whole, which is shorter than its diff:
```python
import functools
import math

import jax
import jax.numpy as jnp
import numpy as np
from jax import lax
from jax.experimental import pallas as pl
from jax.experimental.pallas import tpu as pltpu
from jax.sharding import PartitionSpec as P

D = 512
H = 8
FF = 3200
HD = 64
PACK = 640
LONG = 302
PLACES = 384
SCALE = 0.125
EPS = 1e-05
NEG = -1e9
WT = 3 * D + PLACES
WA = WT + 128
BLOCK = 16
BLOCKS = D // BLOCK
WB = D + 2 * FF
TILE = 512
FF_CHUNKS = ((0, 768), (768, 768), (1536, 768), (2304, 896))
ITEMS = 9
SHORT_WINDOW = (96, 128)
LONG_WINDOW = (320, 384)
SHORT_MOST = SHORT_WINDOW[0] - 15
PROB_ROWS = 1024
GROUP = 4
GROUPS = H // GROUP
GD = GROUP * HD
PROB_COLS = GROUP * LONG_WINDOW[1]
AXES = ("wide", "narrow")
VMEM = 60 * 1024 * 1024
BF = jnp.bfloat16
F32 = jnp.float32


def nn(a, b):
    return lax.dot_general(a, b, (((1,), (0,)), ((), ())), preferred_element_type=F32)


def nt(a, b):
    return lax.dot_general(a, b, (((1,), (1,)), ((), ())), preferred_element_type=F32)


def item_masks(seg_row):
    wide = jnp.broadcast_to(seg_row.astype(F32), (8, PACK))
    col = jnp.transpose(wide)[:, 0:1]
    return col == wide[0:1]


def place_picks(same):
    lane = lax.broadcasted_iota(jnp.int32, (PACK, PACK), 1).astype(F32)
    first = jnp.min(jnp.where(same, lane, 1e6), axis=1, keepdims=True)
    place = lax.broadcasted_iota(jnp.int32, (PACK, 1), 0).astype(F32) - first
    slot = lax.broadcasted_iota(jnp.int32, (PACK, PLACES), 1).astype(F32)
    return jnp.where(place == slot, 1.0, 0.0).astype(BF)


def each_item(starts_ref, pack, body):
    def visit(n, place):
        first = starts_ref[pack * (ITEMS + 1) + n]
        end = starts_ref[pack * (ITEMS + 1) + n + 1]
        length = end - first

        def window(sizes):
            spans = []
            for size in sizes:
                base = pl.multiple_of(jnp.minimum(lax.div(first, 16) * 16, PACK - size), 16)
                spans.append((size, pl.ds(base, size), first - base, end - base))
            body(*spans, pl.ds(pl.multiple_of(place, 16), sizes[0]))

        short = length <= SHORT_MOST

        @pl.when((length > 0) & short)
        def _():
            window(SHORT_WINDOW)

        @pl.when(length > SHORT_MOST)
        def _():
            window(LONG_WINDOW)

        return place + jnp.where(length > 0, jnp.where(short, SHORT_WINDOW[0], LONG_WINDOW[0]), 0)

    lax.fori_loop(0, ITEMS, visit, jnp.int32(0))


def by_head(block):
    lane = lax.broadcasted_iota(jnp.int32, block.shape, 1)
    zero = jnp.zeros_like(block)
    return jnp.concatenate([jnp.where((lane >= h * HD) & (lane < (h + 1) * HD), block, zero) for h in range(GROUP)], axis=0)


def heads_turned(left_t, right, size):
    parts = [nn(left_t[h * HD : (h + 1) * HD], right[:, h * size : (h + 1) * size]) for h in range(GROUP)]
    return jnp.concatenate(parts, axis=0)


GROUP_LANES = [slice(g * GD, (g + 1) * GD) for g in range(GROUPS)]


def block_rows(me_ref, place):
    owner = me_ref[0] ^ offsets(BLOCKS)[place]
    return pl.ds(pl.multiple_of(owner * BLOCK, BLOCK), BLOCK)


def load_blocks(me_ref, halves, full_ref, sem):
    copies = []
    for place in range(BLOCKS):
        half, at = divmod(place, BLOCKS // 2)
        copies.append(pltpu.make_async_copy(halves[half].at[at * BLOCK : (at + 1) * BLOCK], full_ref.at[block_rows(me_ref, place)], sem))
    for copy in copies:
        copy.start()
    for copy in copies:
        copy.wait()


def store_blocks(me_ref, spans, halves, sem):
    copies = []
    for place in range(BLOCKS):
        half, at = divmod(place, BLOCKS // 2)
        for ref, col, width in spans:
            target = halves[half].at[at * BLOCK : (at + 1) * BLOCK, col : col + width]
            copies.append(pltpu.make_async_copy(ref.at[block_rows(me_ref, place)], target, sem))
    for copy in copies:
        copy.start()
    for copy in copies:
        copy.wait()


def attend_kernel(me_ref, starts_ref, seg_ref, x_ref, al_ref, ar_ref, st_ref, q_ref, k_ref, v_ref, mix_ref, attn_ref, pt_ref, vec_ref, pieces_ref, ga_ref, hi_ref, lo_ref, sem):
    @pl.when(pl.program_id(0) == 0)
    def _():
        load_blocks(me_ref, (al_ref, ar_ref), ga_ref, sem)
        pieces_ref[...] = ga_ref[:, WT:].astype(F32)
        vec_ref[...] = jnp.transpose(pieces_ref[...])
        pos = st_ref[...] + ga_ref[:, 3 * D : 3 * D + PLACES].astype(F32)
        hi = pos.astype(BF)
        hi_ref[...] = hi
        lo_ref[...] = (pos - hi.astype(F32)).astype(BF)

    same = item_masks(seg_ref[...])
    picks = place_picks(same)
    x = x_ref[...]
    positions = nt(picks, hi_ref[...]) + nt(picks, lo_ref[...])
    mixed = (x.astype(F32) + positions).astype(BF)
    mix_ref[...] = mixed
    q_ref[...] = ((nt(mixed, ga_ref[:, 0:D]) + vec_ref[0:1]).astype(BF).astype(F32) * SCALE).astype(BF)
    k_ref[...] = nt(mixed, ga_ref[:, D : 2 * D]).astype(BF)
    v = (nt(x, ga_ref[:, 2 * D : 3 * D]) + vec_ref[1:2]).astype(BF)
    v_ref[...] = v
    attn_ref[...] = jnp.zeros_like(attn_ref)

    def item(key_span, query_span, store):
        keys, key_rows, low, high = key_span
        down = lax.broadcasted_iota(jnp.int32, (keys, 1), 0)
        shut = jnp.where((down >= low) & (down < high), 0.0, NEG)
        queries, query_rows, low, high = query_span
        across = lax.broadcasted_iota(jnp.int32, (1, queries), 1)
        live = jnp.where((across >= low) & (across < high), 1.0, 0.0)
        live = jnp.concatenate([live] * GROUP, axis=1)
        scores = [nt(k_ref[key_rows, lanes], by_head(q_ref[query_rows, lanes])) + shut for lanes in GROUP_LANES]
        probs = []
        for g in range(GROUPS):
            exps = jnp.exp(scores[g] - jnp.max(scores[g], axis=0, keepdims=True))
            scale = live / jnp.sum(exps, axis=0, keepdims=True)
            probs.append((exps * scale).astype(BF))
            pt_ref[0, g, store, 0 : GROUP * queries] = probs[g]
        for g, lanes in enumerate(GROUP_LANES):
            outs = heads_turned(jnp.transpose(v_ref[key_rows, lanes]), probs[g], queries)
            attn_ref[query_rows, lanes] += jnp.transpose(outs.astype(BF))

    each_item(starts_ref, pl.program_id(0), item)


def whole(shape):
    return pl.BlockSpec(shape, lambda i: tuple(0 for _ in shape), pipeline_mode=pl.Buffered(1))


def rows_of(count, width):
    return pl.BlockSpec((count, width), lambda i: (i, 0))


SCALAR = pl.BlockSpec(memory_space=pltpu.SMEM)
LOOSE = pl.BlockSpec(memory_space=pl.ANY)


def attend(where, starts, seg, x, halves, st):
    tokens = seg.shape[1]
    packs = tokens // PACK
    low = jax.ShapeDtypeStruct((tokens, D), BF)
    return pl.pallas_call(
        attend_kernel,
        grid=(packs,),
        in_specs=[SCALAR, SCALAR, pl.BlockSpec((1, PACK), lambda i: (0, i)), rows_of(PACK, D), LOOSE, LOOSE, whole((D, PLACES))],
        out_specs=[rows_of(PACK, D)] * 5 + [pl.BlockSpec((1, GROUPS, PROB_ROWS, PROB_COLS), lambda i: (i, 0, 0, 0)), whole((128, D)), whole((D, 128))],
        out_shape=[low] * 5
        + [jax.ShapeDtypeStruct((packs, GROUPS, PROB_ROWS, PROB_COLS), BF), jax.ShapeDtypeStruct((128, D), F32), jax.ShapeDtypeStruct((D, 128), F32)],
        scratch_shapes=[
            pltpu.VMEM((D, WA), BF),
            pltpu.VMEM((D, PLACES), BF),
            pltpu.VMEM((D, PLACES), BF),
            pltpu.SemaphoreType.DMA,
        ],
        compiler_params=pltpu.CompilerParams(vmem_limit_bytes=VMEM),
        cost_estimate=pl.CostEstimate(flops=40 * 10**9, bytes_accessed=50 * 10**6, transcendentals=0),
        name="attend",
    )(where, starts, seg, x, *halves, st)


def centre(v):
    c = v - jnp.mean(v, axis=-1, keepdims=True)
    r = lax.rsqrt(jnp.mean(c * c, axis=-1, keepdims=True) + EPS)
    return c * r, r


def norm_back(g, n, r):
    return r * (g - jnp.mean(g, axis=-1, keepdims=True) - n * jnp.mean(g * n, axis=-1, keepdims=True))


def col_sum(v):
    return jnp.sum(v, axis=0, keepdims=True)


GELU_A = math.sqrt(2.0 / math.pi)
GELU_B = 0.044715


def feed_kernel(me_ref, x_ref, attn_ref, cot_ref, pad_ref, gb_ref, vec_ref, bup_ref, out_ref, dfirst_ref, dattn_ref, keep_ref, send_ref, gv_ref, gbu_ref, act_ref, slope_ref, up_acc, down_acc, wo_acc, wo_low, sem):
    step = pl.program_id(0)

    @pl.when(step == 0)
    def _():
        up_acc[...] = jnp.zeros_like(up_acc)
        down_acc[...] = jnp.zeros_like(down_acc)
        wo_acc[...] = jnp.zeros_like(wo_acc)
        gv_ref[...] = jnp.zeros_like(gv_ref)
        gbu_ref[...] = jnp.zeros_like(gbu_ref)

    keep = jnp.transpose(jnp.broadcast_to(pad_ref[...].astype(F32), (8, TILE)))[:, 0:1]
    attn = attn_ref[...]
    gain_one, gain_two = vec_ref[3:4], vec_ref[6:7]
    first_sum = x_ref[...].astype(F32) + (nt(attn, gb_ref[:, 0:D]) + vec_ref[2:3])
    norm_one, r_one = centre(first_sum)
    hidden = gain_one * norm_one + vec_ref[4:5]
    hidden_low = hidden.astype(BF)
    hidden_t = jnp.transpose(hidden_low)
    ff = jnp.zeros((TILE, D), F32)
    for start, size in FF_CHUNKS:
        cols = slice(start, start + size)
        u = nn(hidden_low, gb_ref[:, D + start : D + start + size]) + bup_ref[0:1, cols]
        u2 = u * u
        t = jnp.tanh(u * (GELU_A + GELU_A * GELU_B * u2))
        h = 0.5 + 0.5 * t
        act = (u * h).astype(BF)
        act_ref[:, cols] = act
        slope_ref[:, cols] = (h + (u * h) * (1.0 - t) * (GELU_A + 3.0 * GELU_A * GELU_B * u2)).astype(BF)
        ff = ff + nt(act, gb_ref[:, D + FF + start : D + FF + start + size])
    norm_two, r_two = centre(hidden + (ff + vec_ref[5:6]))
    out_ref[...] = ((gain_two * norm_two + vec_ref[7:8]) * keep).astype(BF)
    top = cot_ref[...].astype(F32) * keep
    gv_ref[6:7] += col_sum(top * norm_two)
    gv_ref[7:8] += col_sum(top)
    d_second = norm_back(top * gain_two, norm_two, r_two)
    d_ff = d_second.astype(BF)
    gv_ref[5:6] += col_sum(d_ff.astype(F32))
    d_ff_t = jnp.transpose(d_ff)
    d_hidden = d_second
    for start, size in FF_CHUNKS:
        cols = slice(start, start + size)
        d_act = nn(d_ff, gb_ref[:, D + FF + start : D + FF + start + size])
        d_pre = (slope_ref[:, cols].astype(F32) * d_act).astype(BF)
        gbu_ref[0:1, cols] += col_sum(d_pre.astype(F32))
        down_acc[:, cols] += nn(d_ff_t, act_ref[:, cols])
        up_acc[:, cols] += nn(hidden_t, d_pre)
        d_hidden = d_hidden + nt(d_pre, gb_ref[:, D + start : D + start + size])
    gv_ref[3:4] += col_sum(d_hidden * norm_one)
    gv_ref[4:5] += col_sum(d_hidden)
    d_first = norm_back(d_hidden * gain_one, norm_one, r_one)
    dfirst_ref[...] = d_first
    d_branch = d_first.astype(BF)
    gv_ref[2:3] += col_sum(d_branch.astype(F32))
    wo_acc[...] += nn(jnp.transpose(d_branch), attn)
    dattn_ref[...] = nn(d_branch, gb_ref[:, 0:D]).astype(BF)

    @pl.when(step == pl.num_programs(0) - 1)
    def _():
        wo_low[...] = wo_acc[...].astype(BF)
        act_ref[...] = up_acc[...].astype(BF)
        slope_ref[...] = down_acc[...].astype(BF)
        spans = ((wo_low, 0, D), (act_ref, D, FF), (slope_ref, D + FF, FF))
        store_blocks(me_ref, spans, (keep_ref, send_ref), sem)


def feed(where, x, attn, cot, pad, gb, vec, bup):
    tokens = x.shape[0]
    return pl.pallas_call(
        feed_kernel,
        grid=(tokens // TILE,),
        in_specs=[
            SCALAR,
            rows_of(TILE, D),
            rows_of(TILE, D),
            rows_of(TILE, D),
            pl.BlockSpec((1, TILE), lambda i: (0, i)),
            whole((D, WB)),
            whole((128, D)),
            whole((1, FF)),
        ],
        out_specs=[rows_of(TILE, D), rows_of(TILE, D), rows_of(TILE, D), LOOSE, LOOSE, whole((8, D)), whole((1, FF))],
        out_shape=[
            jax.ShapeDtypeStruct((tokens, D), BF),
            jax.ShapeDtypeStruct((tokens, D), F32),
            jax.ShapeDtypeStruct((tokens, D), BF),
            jax.ShapeDtypeStruct((D // 2, WB), BF),
            jax.ShapeDtypeStruct((D // 2, WB), BF),
            jax.ShapeDtypeStruct((8, D), F32),
            jax.ShapeDtypeStruct((1, FF), F32),
        ],
        scratch_shapes=[
            pltpu.VMEM((TILE, FF), BF),
            pltpu.VMEM((TILE, FF), BF),
            pltpu.VMEM((D, FF), F32),
            pltpu.VMEM((D, FF), F32),
            pltpu.VMEM((D, D), F32),
            pltpu.VMEM((D, D), BF),
            pltpu.SemaphoreType.DMA,
        ],
        compiler_params=pltpu.CompilerParams(vmem_limit_bytes=VMEM),
        cost_estimate=pl.CostEstimate(flops=80 * 10**9, bytes_accessed=40 * 10**6, transcendentals=0),
        name="feed",
    )(where, x, attn, cot, pad.reshape(1, tokens), gb, vec, bup)


def tn(a, b):
    return lax.dot_general(a, b, (((0,), (0,)), ((), ())), preferred_element_type=F32)


def core_kernel(first_pack, starts_ref, q_ref, k_ref, v_ref, dattn_ref, pt_ref, *refs):
    dq_ref, dk_ref, dv_ref, dqt_ref, dkt_ref, dvt_ref = refs[-6:]
    for ref in (dq_ref, dk_ref, dv_ref):
        ref[...] = jnp.zeros_like(ref)

    def item(key_span, query_span, store):
        key_rows = key_span[1]
        queries, query_rows = query_span[:2]
        d_outs = [by_head(dattn_ref[query_rows, lanes]) for lanes in GROUP_LANES]
        d_probs = [nt(v_ref[key_rows, lanes], d_outs[g]) for g, lanes in enumerate(GROUP_LANES)]
        probs = [pt_ref[0, g, store, 0 : GROUP * queries] for g in range(GROUPS)]
        d_scores = []
        for g in range(GROUPS):
            wide = probs[g].astype(F32)
            delta = jnp.sum(wide * d_probs[g], axis=0, keepdims=True)
            d_scores.append((wide * (d_probs[g] - delta)).astype(BF))
        for g, lanes in enumerate(GROUP_LANES):
            dv_ref[key_rows, lanes] += nn(probs[g], d_outs[g]).astype(BF)
            dk_ref[key_rows, lanes] += nn(d_scores[g], by_head(q_ref[query_rows, lanes])).astype(BF)
            d_queries = heads_turned(jnp.transpose(k_ref[key_rows, lanes]), d_scores[g], queries) * SCALE
            dq_ref[query_rows, lanes] += jnp.transpose(d_queries.astype(BF))

    each_item(starts_ref, pl.program_id(0) + first_pack, item)
    dqt_ref[0] = jnp.transpose(dq_ref[...])
    dkt_ref[0] = jnp.transpose(dk_ref[...])
    dvt_ref[0] = jnp.transpose(dv_ref[...])


def core_back(first, steps, starts, q, k, v, d_attn, pt, earlier=(), after=()):
    tokens = q.shape[0]
    packs = tokens // PACK
    flat = pl.BlockSpec((PACK, D), lambda i: (i + first, 0))
    turned = pl.BlockSpec((1, D, PACK), lambda i: (i + first, 0, 0))
    shapes = [jax.ShapeDtypeStruct((tokens, D), BF)] * 3 + [jax.ShapeDtypeStruct((packs, D, PACK), BF)] * 3
    return pl.pallas_call(
        functools.partial(core_kernel, first),
        grid=(steps,),
        in_specs=[SCALAR] + [flat] * 4 + [pl.BlockSpec((1, GROUPS, PROB_ROWS, PROB_COLS), lambda i: (i + first, 0, 0, 0))] + [LOOSE] * (len(earlier) + len(after)),
        out_specs=[flat] * 3 + [turned] * 3,
        out_shape=shapes,
        input_output_aliases={6 + n: n for n in range(len(earlier))},
        compiler_params=pltpu.CompilerParams(vmem_limit_bytes=VMEM),
        cost_estimate=pl.CostEstimate(flops=18 * 10**9 * steps, bytes_accessed=12 * 10**6 * steps, transcendentals=0),
        name="core_back",
    )(starts, q, k, v, d_attn, pt, *earlier, *after)


def grads_kernel(me_ref, seg_ref, x_ref, mix_ref, dqt_ref, dkt_ref, dvt_ref, al_ref, ar_ref, gv_ref, extra_ref, *refs):
    keep_ref, send_ref, ga_ref, gw_ref, q_acc, k_acc, v_acc, tq_acc, tk_acc, b_acc, sem = refs[-11:]
    step = pl.program_id(0)

    @pl.when(step == 0)
    def _():
        load_blocks(me_ref, (al_ref, ar_ref), ga_ref, sem)
        for acc in (q_acc, k_acc, v_acc, tq_acc, tk_acc, b_acc):
            acc[...] = jnp.zeros_like(acc)

    dq_t, dk_t, dv_t = dqt_ref[0], dkt_ref[0], dvt_ref[0]
    mixed = mix_ref[...]
    picks = place_picks(item_masks(seg_ref[...]))
    q_acc[...] += nn(dq_t, mixed)
    k_acc[...] += nn(dk_t, mixed)
    v_acc[...] += nn(dv_t, x_ref[...])
    tq_acc[...] += nn(dq_t, picks)
    tk_acc[...] += nn(dk_t, picks)
    lane = lax.broadcasted_iota(jnp.int32, (1, 128), 1)
    b_acc[...] += jnp.where(lane == 0, jnp.sum(dq_t.astype(F32), axis=1, keepdims=True), 0.0)
    b_acc[...] += jnp.where(lane == 1, jnp.sum(dv_t.astype(F32), axis=1, keepdims=True), 0.0)

    @pl.when(step == pl.num_programs(0) - 1)
    def _():
        gw_ref[:, 0:D] = q_acc[...].astype(BF)
        gw_ref[:, D : 2 * D] = k_acc[...].astype(BF)
        gw_ref[:, 2 * D : 3 * D] = v_acc[...].astype(BF)
        table = tn(ga_ref[:, 0:D], tq_acc[...].astype(BF)) + tn(ga_ref[:, D : 2 * D], tk_acc[...].astype(BF))
        gw_ref[:, 3 * D : WT] = table.astype(BF)
        vec = jnp.concatenate([gv_ref[...], jnp.zeros((120, D), F32)], axis=0)
        gw_ref[:, WT : WT + 128] = (jnp.transpose(vec) + b_acc[...] + extra_ref[:, 0:128]).astype(BF)
        for at in range(128, extra_ref.shape[1], 128):
            gw_ref[:, WT + at : WT + at + 128] = extra_ref[:, at : at + 128].astype(BF)
        store_blocks(me_ref, ((gw_ref, 0, gw_ref.shape[1]),), (keep_ref, send_ref), sem)


def grads(where, seg, x, mixed, turned, halves, gv, extra, after):
    packs = seg.shape[1] // PACK
    width = WT + extra.shape[1]
    return pl.pallas_call(
        grads_kernel,
        grid=(packs,),
        in_specs=[SCALAR, pl.BlockSpec((1, PACK), lambda i: (0, i))]
        + [rows_of(PACK, D)] * 2
        + [pl.BlockSpec((1, D, PACK), lambda i: (i, 0, 0))] * 3
        + [LOOSE, LOOSE, whole((8, D)), whole(extra.shape)]
        + [LOOSE] * len(after),
        out_specs=[LOOSE, LOOSE],
        out_shape=[jax.ShapeDtypeStruct((D // 2, width), BF)] * 2,
        scratch_shapes=[
            pltpu.VMEM((D, WA), BF),
            pltpu.VMEM((D, width), BF),
            pltpu.VMEM((D, D), F32),
            pltpu.VMEM((D, D), F32),
            pltpu.VMEM((D, D), F32),
            pltpu.VMEM((D, PLACES), F32),
            pltpu.VMEM((D, PLACES), F32),
            pltpu.VMEM((D, 128), F32),
            pltpu.SemaphoreType.DMA,
        ],
        compiler_params=pltpu.CompilerParams(vmem_limit_bytes=VMEM),
        cost_estimate=pl.CostEstimate(flops=10 * 10**9, bytes_accessed=20 * 10**6, transcendentals=0),
        name="grads",
    )(where, seg, x, mixed, *turned, *halves, gv, extra, *after)


def inputs_kernel(me_ref, dq_ref, dk_ref, dv_ref, dfirst_ref, al_ref, ar_ref, after_ref, out_ref, ga_ref, sem):
    @pl.when(pl.program_id(0) == 0)
    def _():
        load_blocks(me_ref, (al_ref, ar_ref), ga_ref, sem)

    d_mixed = nn(dq_ref[...], ga_ref[:, 0:D]) + nn(dk_ref[...], ga_ref[:, D : 2 * D])
    out_ref[...] = (dfirst_ref[...] + d_mixed + nn(dv_ref[...], ga_ref[:, 2 * D : 3 * D])).astype(BF)


def input_grads(where, flat, d_first, halves, after):
    tokens = d_first.shape[0]
    return pl.pallas_call(
        inputs_kernel,
        grid=(tokens // PACK,),
        in_specs=[SCALAR] + [rows_of(PACK, D)] * 4 + [LOOSE, LOOSE, LOOSE],
        out_specs=rows_of(PACK, D),
        out_shape=jax.ShapeDtypeStruct((tokens, D), BF),
        scratch_shapes=[pltpu.VMEM((D, WA), BF), pltpu.SemaphoreType.DMA],
        compiler_params=pltpu.CompilerParams(vmem_limit_bytes=VMEM),
        cost_estimate=pl.CostEstimate(flops=8 * 10**9, bytes_accessed=20 * 10**6, transcendentals=0),
        name="input_grads",
    )(where, *flat, d_first, *halves, after)


def sines():
    half = D // 2
    frequency = np.exp(np.arange(half, dtype=np.float32) * np.float32(-2.0 * math.log(10000.0) / D))
    angles = frequency[:, None] * np.arange(PLACES, dtype=np.float32)[None, :]
    return jnp.asarray(np.concatenate([np.sin(angles), np.cos(angles)], axis=0).astype(np.float32))


def pack_kernel(piece, wide_ref, wq_ref, wk_ref, wv_ref, table_ref, wo_ref, up_ref, down_ref, bup_ref, *refs):
    vectors, (a_ref, b_ref, turn_ref, bias_ref) = refs[:8], refs[8:]
    rows = a_ref.shape[0]
    a_ref[:, 0:D] = wq_ref[...]
    a_ref[:, D : 2 * D] = wk_ref[...]
    a_ref[:, 2 * D : 3 * D] = wv_ref[...]
    a_ref[:, 3 * D : WT] = jnp.zeros((rows, PLACES), BF)
    a_ref[:, 3 * D : 3 * D + LONG] = table_ref[...]
    b_ref[:, 0:D] = wo_ref[...]
    b_ref[:, D : D + FF] = up_ref[...]
    b_ref[:, D + FF :] = down_ref[...]
    turn_ref[...] = jnp.zeros_like(turn_ref)
    for n, vector in enumerate(vectors):
        turn_ref[n : n + 1, 0:rows] = vector[...].astype(F32)
    bias_ref[...] = jnp.zeros_like(bias_ref)
    bias_ref[0:1, 0 : bup_ref.shape[1]] = bup_ref[...].astype(F32)
    span = bias_ref.shape[1]
    shift = lax.rem(span + 8 - wide_ref[0] * piece, span)
    moved = pltpu.roll(bias_ref[...], shift, 1)[0:1, 0:128]
    lane = lax.broadcasted_iota(jnp.int32, (rows, 128), 1)
    row = lax.broadcasted_iota(jnp.int32, (rows, 128), 0)
    mine = (row == 0) & (lane >= 8) & (lane < 8 + piece)
    columns = jnp.transpose(turn_ref[...])[0:rows]
    a_ref[:, WT:] = jnp.where(mine, moved, columns).astype(BF)


def pack(wide_index, piece, matrices, b_up, vectors):
    rows = matrices[0].shape[0]
    span = -(-(b_up.shape[0] + 8) // 128) * 128
    return pl.pallas_call(
        functools.partial(pack_kernel, piece),
        in_specs=[SCALAR] + [pl.BlockSpec(memory_space=pltpu.VMEM)] * 16,
        out_specs=[pl.BlockSpec(memory_space=pltpu.VMEM)] * 2,
        out_shape=[jax.ShapeDtypeStruct((rows, WA), BF), jax.ShapeDtypeStruct((rows, WB), BF)],
        scratch_shapes=[pltpu.VMEM((128, 128), F32), pltpu.VMEM((8, span), F32)],
        name="pack",
    )(wide_index.reshape(1), *matrices, b_up.reshape(1, -1), *[vector.reshape(1, rows) for vector in vectors])


def bit_groups(count):
    bits = count.bit_length() - 1
    return [(0,)] + [tuple(range(at, min(at + 2, bits))) for at in range(1, bits, 2)]


def offsets(count):
    found = [0]
    for group in bit_groups(count):
        found = [old | mask for old in found for mask in masks(group)]
    return found


def masks(group):
    return [index << group[0] for index in range(1 << len(group))]


def swap(block, mask, count):
    return lax.ppermute(block, AXES, [(i, i ^ mask) for i in range(count)])


def gather_phase(own, group, count):
    return [own] + [swap(own, mask, count) for mask in masks(group)[1:]]


def scatter_phase(pieces, group, count):
    total = pieces[0].astype(F32)
    for piece, mask in zip(pieces[1:], masks(group)[1:]):
        total = total + swap(piece, mask, count).astype(F32)
    return total


def split_rows(block, count):
    rows = block.shape[0] // count
    return [block[at * rows : (at + 1) * rows] for at in range(count)]


def scatter_rest(block, groups, count):
    for group in groups:
        block = scatter_phase(split_rows(block.astype(BF), 1 << len(group)), group, count)
    return block


def local(
    inputs,
    segments,
    pad_mask,
    cotangent,
    w_query,
    b_query,
    w_key,
    w_value,
    b_value,
    w_out,
    b_out,
    gain_one,
    shift_one,
    w_up,
    b_up,
    w_down,
    b_down,
    gain_two,
    shift_two,
    pos_table,
):
    tokens = inputs.shape[0]
    narrow = lax.axis_size("narrow")
    wide = lax.axis_size("wide")
    count = wide * narrow
    me = lax.axis_index(AXES)
    groups = bit_groups(count)
    own_rows = D // count
    bits = count.bit_length() - 1
    places = [bits - 1 - bit for group in groups for bit in reversed(group)] + [bits, bits + 1]
    in_kernel = own_rows == BLOCK
    where = (me if in_kernel else jnp.zeros((), jnp.int32)).reshape(1).astype(jnp.int32)

    def flips(full):
        for axis in range(bits):
            mine = (me >> (bits - 1 - axis)) & 1
            full = jnp.where(mine == 1, jnp.flip(full, axis), full)
        return full

    def absolute(halves):
        if in_kernel:
            return halves
        full = jnp.concatenate(halves, axis=0).reshape([2] * bits + [own_rows, -1])
        full = flips(full.transpose([places.index(axis) for axis in range(bits + 2)])).reshape(D, -1)
        return full[: D // 2], full[D // 2 :]

    def relative(halves):
        if in_kernel:
            return halves
        full = flips(jnp.concatenate(halves, axis=0).reshape([2] * bits + [own_rows, -1]))
        full = full.transpose(places).reshape(D, -1)
        return full[: D // 2], full[D // 2 :]

    seg = segments.reshape(1, tokens)
    packs = tokens // PACK
    below = segments.reshape(packs, 1, PACK) < jnp.arange(ITEMS + 1, dtype=jnp.int32)[None, :, None]
    starts = jnp.sum(below.astype(jnp.int32), axis=2).reshape(packs * (ITEMS + 1))
    bias_width = b_up.shape[0]
    bias_piece = -(-bias_width // wide)
    own_a, own_b = pack(
        lax.axis_index("wide").astype(jnp.int32),
        bias_piece,
        (w_query.T, w_key.T, w_value.T, pos_table.T, w_out.T, w_up, w_down.T),
        b_up,
        (b_query, b_value, b_out, gain_one, shift_one, b_down, gain_two, shift_two),
    )
    gb = lax.all_gather(own_b, AXES, axis=0, tiled=True)
    for group in reversed(groups[1:]):
        own_a = jnp.concatenate(gather_phase(own_a, group, count), axis=0)
    a_halves = absolute(tuple(gather_phase(own_a, groups[0], count)))
    q, k, v, mixed, attn, pt, vec, pieces = attend(where, starts, seg, inputs, a_halves, sines())
    bup = pieces.reshape(wide, narrow, own_rows, 128)[:, :, 0, 8 : 8 + bias_piece].transpose(1, 0, 2)
    bup = bup.reshape(narrow, wide * bias_piece)[:, :bias_width].reshape(1, FF)
    layer_out, d_first, d_attn, keep_b, send_b, gv, gbu = feed(where, inputs, attn, cotangent, pad_mask, gb, vec, bup)
    grad_cols = -(-bias_width // own_rows)
    extra = jnp.pad(gbu.reshape(narrow, bias_width), ((0, 0), (0, grad_cols * own_rows - bias_width)))
    extra = jnp.broadcast_to(extra.reshape(1, narrow, own_rows, grad_cols), (wide, narrow, own_rows, grad_cols))
    extra_width = -(-(8 + grad_cols) // 128) * 128
    extra = jnp.pad(extra.reshape(D, grad_cols), ((0, 0), (8, extra_width - 8 - grad_cols)))
    early = packs // 2
    back = core_back(0, early, starts, q, k, v, d_attn, pt)
    sum_b = scatter_phase(relative((keep_b, send_b)), groups[0], count).astype(BF)
    parts_b = split_rows(sum_b, 1 << len(groups[1]))
    back = core_back(early, packs - early, starts, q, k, v, d_attn, pt, back, parts_b)
    sum_b = scatter_phase(parts_b, groups[1], count).astype(BF)
    parts_b = split_rows(sum_b, 1 << len(groups[2]))
    keep_a, send_a = grads(where, seg, inputs, mixed, back[3:], a_halves, gv, extra, parts_b)
    own_grad_b = scatter_rest(scatter_phase(parts_b, groups[2], count), groups[3:], count)
    input_grad = input_grads(where, back[:3], d_first, a_halves, keep_a)
    own_grad_a = scatter_phase(relative((keep_a, send_a)), groups[0], count)
    own_grad_a = scatter_rest(own_grad_a, groups[1:], count)
    grad_b_up = own_grad_a[:, WT + 8 : WT + 8 + grad_cols].reshape(grad_cols * own_rows)[:bias_width]
    own_vec = own_grad_a[:, WT : WT + 8]
    return (
        layer_out,
        input_grad,
        own_grad_a[:, 0:D].T,
        own_vec[:, 0],
        own_grad_a[:, D : 2 * D].T,
        own_grad_a[:, 2 * D : 3 * D].T,
        own_vec[:, 1],
        own_grad_b[:, 0:D].T,
        own_vec[:, 2],
        own_vec[:, 3],
        own_vec[:, 4],
        own_grad_b[:, D : D + FF],
        grad_b_up,
        own_grad_b[:, D + FF :].T,
        own_vec[:, 5],
        own_vec[:, 6],
        own_vec[:, 7],
        own_grad_a[:, 3 * D : 3 * D + LONG].T,
    )


def solution(mesh):
    both = P(("wide", "narrow"))
    rows = P(("wide", "narrow"), None)
    cols = P(None, ("wide", "narrow"))
    in_specs = (rows, both, both, rows, cols, both, cols, cols, both, cols, both, both, both, rows, P("narrow"), cols, both, both, both, cols)
    out_specs = (rows, rows, cols, both, cols, cols, both, cols, both, both, both, rows, P("narrow"), cols, both, both, both, cols)
    return jax.shard_map(local, mesh=mesh, in_specs=in_specs, out_specs=out_specs, check_vma=False)
```

time: 417 us -> 314 us (0.75)
  Pallas kernels: 236 us -> 187 us
  waiting for transfers between devices: 98.2 us -> 59.4 us
  between operations: 0.94 us -> 14.3 us
  starting transfers between devices: 38.9 us -> 25.6 us
  local copies, waits for them, and re-layouts: 30.9 us -> 18.9 us
    pallas_call x2 -> x6, Pallas kernels: 150 us -> 102 us  [the longest x1 37.5 us: attend(): pl.pallas_call(attend_kernel, grid=(packs,), in_specs=[SCALAR, SCALAR, pl...]
    ppermute x28 -> x21, waiting for transfers between devices: 98.2 us -> 51.9 us  [swap(): return lax.ppermute(block, AXES, [(i, i ^ mask) for i in range(count)])]
    ppermute x28 -> x21, starting transfers between devices: 38.9 us -> 25.6 us  [swap(): return lax.ppermute(block, AXES, [(i, i ^ mask) for i in range(count)])]
    all_gather x0 -> x1, waiting for transfers between devices: none -> 7.48 us  [local(): gb = lax.all_gather(own_b, AXES, axis=0, tiled=True)]
    convert_element_type x4 -> x2, other arithmetic: 6.84 us -> 0.52 us  [scatter_rest(): block.astype(BF)]
    convert_element_type x0 -> x2, other arithmetic: none -> 6.01 us  [the longest x1 3.88 us: local(): scatter_phase(relative((keep_b, send_b)), groups[0], count).astype(BF)]
    another operation x8 -> x0, local copies, waits for them, and re-layouts: 5.96 us -> none  [local(): jnp.stack([b_query, b_value, b_out, gain_one, shift_one, b_down, gain_two...]
  transfers between devices with their start and end apart: 28 -> 22, of which waited for: 14 -> 14; matrix products, arithmetic and copies ran while one was open for 6% -> 3% of each run, Pallas kernels for 36% -> 32%
where the time goes in v2:
time: 314 us; the launch traced here: 313 us
  Pallas kernels  187 us (60%)
  waiting for transfers between devices  59.4 us (19%)
  starting transfers between devices  25.6 us (8%)
  local copies, waits for them, and re-layouts  18.9 us (6%)
  between operations  14.3 us (5%)
  other arithmetic  8.6 us (3%)
    pallas_call x1, Pallas kernels, feed(): pl.pallas_call(feed_kernel, grid=(tokens // TILE,), in_specs=[SCALAR, row...  84.3 us
    ppermute x21, waiting for transfers between devices, swap(): return lax.ppermute(block, AXES, [(i, i ^ mask) for i in range(count)])  51.9 us
    pallas_call x1, Pallas kernels, attend(): pl.pallas_call(attend_kernel, grid=(packs,), in_specs=[SCALAR, SCALAR, pl...  37.5 us
    pallas_call x2, Pallas kernels, core_back(): pl.pallas_call(functools.partial(core_kernel, first), grid=(steps,), in_s...  37 us
    ppermute x21, starting transfers between devices, swap(): return lax.ppermute(block, AXES, [(i, i ^ mask) for i in range(count)])  25.6 us
    pallas_call x1, Pallas kernels, grads(): pl.pallas_call(grads_kernel, grid=(packs,), in_specs=[SCALAR, pl.BlockSpe...  15.5 us
    pallas_call x1, Pallas kernels, input_grads(): pl.pallas_call(inputs_kernel, grid=(tokens // PACK,), in_specs=[SCALAR] +...  10.5 us
    all_gather x1, waiting for transfers between devices, local(): gb = lax.all_gather(own_b, AXES, axis=0, tiled=True)  7.48 us
  transfers between devices with their start and end apart: 22, of which 14 were waited for; matrix products, arithmetic and copies ran while one was open for 3% of the time, Pallas kernels for 32%

profile of v2, /device:TPU:0, one launch (start us, length us, event | category | flops | bytes accessed | tf_op | source)
XLA Modules:
  0.0 313.5 jit_solution(2124824483137596838)
XLA Ops:
  8.5 1.8 pack.1
  10.4 3.1 collective-permute-start
  13.5 2.6 collective-permute-start.1
  17.0 3.9 %collective-permute-done.1 = bf16[16,2048]{1,0:T(8,128)(2,1)S(1)} collective-permute-done((bf16[16,2048]{1,0:T(8,128)(2,1)}, bf16[16,2048]{1,0:T(8,128)(2,1)S(1)}, u32[]{:S(2)}, u32[]{:S(2)}) %collective-permute-start.1) | collective-permute-done | bytes 65568 | tf_op jit(solution)/shard_map/ppermute | solution.py:545
  22.4 1.6 collective-permute-start.3
  24.0 1.5 collective-permute-start.4
  25.9 5.1 %collective-permute-done.3 = bf16[64,2048]{1,0:T(8,128)(2,1)S(1)} collective-permute-done((bf16[64,2048]{1,0:T(8,128)(2,1)S(1)}, bf16[64,2048]{1,0:T(8,128)(2,1)S(1)}, u32[]{:S(2)}, u32[]{:S(2)}) %collective-permute-start.3) | collective-permute-done | bytes 262176 | tf_op jit(solution)/shard_map/ppermute | solution.py:545
  31.1 2.1 collective-permute-done.4
  33.2 4.0 %collective-permute-done.5 = bf16[64,2048]{1,0:T(8,128)(2,1)S(1)} collective-permute-done((bf16[64,2048]{1,0:T(8,128)(2,1)S(1)}, bf16[64,2048]{1,0:T(8,128)(2,1)S(1)}, u32[]{:S(2)}, u32[]{:S(2)}) %collective-permute-start.5) | collective-permute-done | bytes 262176 | tf_op jit(solution)/shard_map/ppermute | solution.py:545
  41.0 37.5 %attend.1 = (bf16[2560,512]{1,0:T(8,128)(2,1)}, bf16[2560,512]{1,0:T(8,128)(2,1)}, bf16[2560,512]{1,0:T(8,128)(2,1)}, bf16[2560,512]{1,0:T(8,128)(2,1)}, bf16[25...) custom-call(s32[1]{0:T(128)} %bitcast.me_ref, ...), custom_call_target="tpu_custom_call" | custom-call | flops 40000000000 | bytes 50000000 | tf_op jit(solution)/shard_map/attend/pallas_call | solution.py:198
  80.2 7.5 %all-gather.2.cloned.1.call-done.gb_ref = bf16[512,6912]{1,0:T(8,128)(2,1)} async-done(((bf16[16,6912]{1,0:T(8,128)(2,1)}), bf16[512,6912]{1,0:T(8,128)(2,1)}) %all-gather.2.cloned.1.call-update) | async-done | bytes 7077904 | tf_op jit(solution)/shard_map/all_gather | solution.py:637
  87.7 84.3 %feed.1 = (bf16[2560,512]{1,0:T(8,128)(2,1)}, f32[2560,512]{1,0:T(8,128)}, bf16[2560,512]{1,0:T(8,128)(2,1)}, bf16[256,6912]{1,0:T(8,128)(2,1)}, bf16[256,6912]{...) custom-call(s32[1]{0:T(128)} %bitcast.me_ref, bf16[2560,512]{1,0:T(8,128)(2,1)} %x_ref.5, ...), custom_call_target="tpu_custom_call" | custom-call | flops 80000000000 | bytes 40000000 | tf_op jit(solution)/shard_map/feed/pallas_call | solution.py:303
  175.4 18.6 %core_back.2 = (bf16[2560,512]{1,0:T(8,128)(2,1)}, bf16[2560,512]{1,0:T(8,128)(2,1)}, bf16[2560,512]{1,0:T(8,128)(2,1)}, bf16[4,512,640]{2,1,0:T(8,128)(2,1)}, b...) custom-call(s32[40]{0:T(128)} %reshape.94.starts_ref, bf16[2560,512]{1,0:T(8,128)(2,1)} %get-tuple-element.55.q_ref, ...), custom_call_target="tpu_custom_call" | custom-call | flops 35999997952 | bytes 24000000 | tf_op jit(solution)/shard_map/core_back/pallas_call | solution.py:379
  194.0 1.7 copy-done.1
  195.7 3.9 %add_convert_fusion = bf16[256,6912]{1,0:T(8,128)(2,1)S(1)} fusion(bf16[256,6912]{1,0:T(8,128)(2,1)} %copy-done.1, bf16[256,6912]{1,0:T(8,128)(2,1)} %get-tuple-element.66), kind=kLoop, calls=%fused_computation | loop fusion | flops 7077888 | bytes 10616832 | tf_op jit(solution)/shard_map/convert_element_type | solution.py:652
  199.6 1.8 fusion
  201.4 1.5 collective-permute-start.10
  202.9 1.4 collective-permute-start.8
  204.9 18.4 %core_back.3 = (bf16[2560,512]{1,0:T(8,128)(2,1)}, bf16[2560,512]{1,0:T(8,128)(2,1)}, bf16[2560,512]{1,0:T(8,128)(2,1)}, bf16[4,512,640]{2,1,0:T(8,128)(2,1)}, b...) custom-call(s32[40]{0:T(128)} %reshape.94.starts_ref, ...), custom_call_target="tpu_custom_call", output_to_operand_aliasing={{0}: (6, {}), {1}: (7, {}), {2}: (8, {}), {3}: (9, {}), {4}... | custom-call | flops 35999997952 | bytes 24000000 | tf_op jit(solution)/shard_map/core_back/pallas_call | solution.py:379
  223.4 1.8 collective-permute-done.10
  225.2 18.2 %collective-permute-done.8 = bf16[64,6912]{1,0:T(8,128)(2,1)} collective-permute-done((bf16[64,6912]{1,0:T(8,128)(2,1)}, bf16[64,6912]{1,0:T(8,128)(2,1)}, u32[]{:S(2)}, u32[]{:S(2)}) %collective-permute-start.8) | collective-permute-done | bytes 884768 | tf_op jit(solution)/shard_map/ppermute | solution.py:545
  243.4 2.1 add_convert_fusion.2
  247.2 1.6 collective-permute-start.18
  249.7 1.8 collective-permute-start.20
  251.6 15.5 %grads.1 = (bf16[256,2048]{1,0:T(8,128)(2,1)}, bf16[256,2048]{1,0:T(8,128)(2,1)}) custom-call(s32[1]{0:T(128)} %bitcast.me_ref, s32[1,2560]{1,0:T(1,128)} %reshape.95.seg_ref, bf16[2560,512]{1,0:T(8,128)(2,1)} %x_ref.5, bf16[2560,512]{1,0:T(8,128)(2,1)} %get-tuple-element.72.mix_ref, bf16[4,512,640]{2,1,0:T(8,128)(2,1)} %get-tuple-element.73.dqt_ref, ...), custom_call_target="tpu_custom_call" | custom-call | flops 10000000000 | bytes 20000000 | tf_op jit(solution)/shard_map/grads/pallas_call | solution.py:431
  267.2 10.5 %input_grads.1 = bf16[2560,512]{1,0:T(8,128)(2,1)} custom-call(s32[1]{0:T(128)} %bitcast.me_ref, bf16[2560,512]{1,0:T(8,128)(2,1)} %get-tuple-element.68.dq_ref, bf16[2560,512]{1,0:T(8,128)(2,1)} %get-tuple-element.69.dk_ref, bf16[2560,512]{1,0:T(8,128)(2,1)} %get-tuple-element.70.dv_ref, f32[2560,512]{1,0:T(8,128)} %get-tuple-element.71.dfirst_ref, ...), custom_call_target="tpu_custom_call" | custom-call | flops 8000000000 | bytes 20000000 | tf_op jit(solution)/shard_map/input_grads/pallas_call | solution.py:469
  283.6 4.4 %collective-permute-done.12 = bf16[64,2048]{1,0:T(8,128)(2,1)S(1)} collective-permute-done((bf16[64,2048]{1,0:T(8,128)(2,1)S(1)}, bf16[64,2048]{1,0:T(8,128)(2,1)S(1)}, u32[]{:S(2)}, u32[]{:S(2)}) %collective-permute-start.12) | collective-permute-done | bytes 262176 | tf_op jit(solution)/shard_map/ppermute | solution.py:545
  288.1 1.8 collective-permute-done.13
  289.8 5.0 %collective-permute-done.14 = bf16[64,2048]{1,0:T(8,128)(2,1)S(1)} collective-permute-done((bf16[64,2048]{1,0:T(8,128)(2,1)S(1)}, bf16[64,2048]{1,0:T(8,128)(2,1)S(1)}, u32[]{:S(2)}, u32[]{:S(2)}) %collective-permute-start.14) | collective-permute-done | bytes 262176 | tf_op jit(solution)/shard_map/ppermute | solution.py:545
  295.8 1.8 collective-permute-start.16
  297.6 1.8 collective-permute-start.17
  300.1 2.5 collective-permute-done.16
  (78 shorter events, 27.7 us)
Async XLA Ops:
  7.2 30.2 %copy-start.6 = (s32[2560]{0:T(1024)S(1)}, s32[2560]{0:T(1024)}, u32[]{:S(2)}) copy-start(s32[2560]{0:T(1024)} %param.22) | copy-start | bytes 30724
  7.2 31.8 %copy-start.7 = (s32[2560]{0:T(1024)S(1)}, s32[2560]{0:T(1024)}, u32[]{:S(2)}) copy-start(s32[2560]{0:T(1024)} %param.23) | copy-start | bytes 30724
  7.2 80.4 %all-gather.2.cloned.1.call-start = ((), (), s32[]{:S(2)}) async-start(), calls=%async_computation | async-start | bytes 7299072 | tf_op jit(solution)/shard_map/all_gather | solution.py:637
  10.4 6.6 %collective-permute-start = (bf16[16,2048]{1,0:T(8,128)(2,1)}, bf16[16,2048]{1,0:T(8,128)(2,1)S(1)}, u32[]{:S(2)}, u32[]{:S(2)}) collective-permute-start(bf16[16,2048]{1,0:T(8,128)(2,1)} %get-tuple-element.49), channel_id=1, source_target_pairs={{0,8},{1,9},{2,10},{3,11},{4,12},{5,13},{6,14},{7,15},{8,0},{9,1},... | collective-permute-start | bytes 196616 | tf_op jit(solution)/shard_map/ppermute | solution.py:545
  13.5 7.5 %collective-permute-start.1 = (bf16[16,2048]{1,0:T(8,128)(2,1)}, bf16[16,2048]{1,0:T(8,128)(2,1)S(1)}, u32[]{:S(2)}, u32[]{:S(2)}) collective-permute-start(bf16[16,2048]{1,0:T(8,128)(2,1)} %get-tuple-element.49), channel_id=1, source_target_pairs={{0,16},{1,17},{2,18},{3,19},{4,20},{5,21},{6,22},{7,23},{8,24},{9,... | collective-permute-start | bytes 196616 | tf_op jit(solution)/shard_map/ppermute | solution.py:545
  16.1 6.3 %collective-permute-start.2 = (bf16[16,2048]{1,0:T(8,128)(2,1)}, bf16[16,2048]{1,0:T(8,128)(2,1)S(1)}, u32[]{:S(2)}, u32[]{:S(2)}) collective-permute-start(bf16[16,2048]{1,0:T(8,128)(2,1)} %get-tuple-element.49), channel_id=1, source_target_pairs={{0,24},{1,25},{2,26},{3,27},{4,28},{5,29},{6,30},{7,31},{8,16},{9,... | collective-permute-start | bytes 196616 | tf_op jit(solution)/shard_map/ppermute | solution.py:545
  22.4 8.7 %collective-permute-start.3 = (bf16[64,2048]{1,0:T(8,128)(2,1)S(1)}, bf16[64,2048]{1,0:T(8,128)(2,1)S(1)}, u32[]{:S(2)}, u32[]{:S(2)}) collective-permute-start(bf16[64,2048]{1,0:T(8,128)(2,1)S(1)} %get-tuple-element.107), channel_id=1, source_target_pairs={{0,2},{1,3},{2,0},{3,1},{4,6},{5,7},{6,4},{7,5},{8,10},{9,11},{10,... | collective-permute-start | bytes 786440 | tf_op jit(solution)/shard_map/ppermute | solution.py:545
  24.0 9.2 %collective-permute-start.4 = (bf16[64,2048]{1,0:T(8,128)(2,1)S(1)}, bf16[64,2048]{1,0:T(8,128)(2,1)S(1)}, u32[]{:S(2)}, u32[]{:S(2)}) collective-permute-start(bf16[64,2048]{1,0:T(8,128)(2,1)S(1)} %get-tuple-element.107), channel_id=1, source_target_pairs={{0,4},{1,5},{2,6},{3,7},{4,0},{5,1},{6,2},{7,3},{8,12},{9,13},{10,... | collective-permute-start | bytes 786440 | tf_op jit(solution)/shard_map/ppermute | solution.py:545
  25.5 11.8 %collective-permute-start.5 = (bf16[64,2048]{1,0:T(8,128)(2,1)S(1)}, bf16[64,2048]{1,0:T(8,128)(2,1)S(1)}, u32[]{:S(2)}, u32[]{:S(2)}) collective-permute-start(bf16[64,2048]{1,0:T(8,128)(2,1)S(1)} %get-tuple-element.107), channel_id=1, source_target_pairs={{0,6},{1,7},{2,4},{3,5},{4,2},{5,3},{6,0},{7,1},{8,14},{9,15},{10,... | collective-permute-start | bytes 786440 | tf_op jit(solution)/shard_map/ppermute | solution.py:545
  37.3 2.7 copy-start.8
  37.3 2.7 collective-permute-start.6
  40.0 1.0 copy-start.9
  171.9 22.0 %collective-permute-start.7 = (bf16[256,6912]{1,0:T(8,128)(2,1)}, bf16[256,6912]{1,0:T(8,128)(2,1)S(1)}, u32[]{:S(2)}, u32[]{:S(2)}) collective-permute-start(bf16[256,6912]{1,0:T(8,128)(2,1)} %get-tuple-element.67), channel_id=1, source_target_pairs={{0,1},{1,0},{2,3},{3,2},{4,5},{5,4},{6,7},{7,6},{8,9},{9,8},{10,11... | collective-permute-start | bytes 10616840 | tf_op jit(solution)/shard_map/ppermute | solution.py:545
  194.0 1.8 copy-start.1
  201.4 23.7 %collective-permute-start.10 = (bf16[64,6912]{1,0:T(8,128)(2,1)}, bf16[64,6912]{1,0:T(8,128)(2,1)}, u32[]{:S(2)}, u32[]{:S(2)}) collective-permute-start(bf16[64,6912]{1,0:T(8,128)(2,1)} %get-tuple-element.88.refs_9_), channel_id=1, source_target_pairs={{0,6},{1,7},{2,4},{3,5},{4,2},{5,3},{6,0},{7,1},{8,14},{9,15},{10,... | collective-permute-start | bytes 2654216 | tf_op jit(solution)/shard_map/ppermute | solution.py:545
  202.9 40.5 %collective-permute-start.8 = (bf16[64,6912]{1,0:T(8,128)(2,1)}, bf16[64,6912]{1,0:T(8,128)(2,1)}, u32[]{:S(2)}, u32[]{:S(2)}) collective-permute-start(bf16[64,6912]{1,0:T(8,128)(2,1)} %get-tuple-element.90.refs_7_), channel_id=1, source_target_pairs={{0,2},{1,3},{2,0},{3,1},{4,6},{5,7},{6,4},{7,5},{8,10},{9,11},{10,... | collective-permute-start | bytes 2654216 | tf_op jit(solution)/shard_map/ppermute | solution.py:545
  204.3 39.1 %collective-permute-start.9 = (bf16[64,6912]{1,0:T(8,128)(2,1)}, bf16[64,6912]{1,0:T(8,128)(2,1)}, u32[]{:S(2)}, u32[]{:S(2)}) collective-permute-start(bf16[64,6912]{1,0:T(8,128)(2,1)} %get-tuple-element.89.refs_8_), channel_id=1, source_target_pairs={{0,4},{1,5},{2,6},{3,7},{4,0},{5,1},{6,2},{7,3},{8,12},{9,13},{10,... | collective-permute-start | bytes 2654216 | tf_op jit(solution)/shard_map/ppermute | solution.py:545
  245.5 0.9 copy-start
  247.2 4.4 %copy-start.3 = (bf16[16,6912]{1,0:T(8,128)(2,1)}, bf16[16,6912]{1,0:T(8,128)(2,1)S(1)}, u32[]{:S(2)}) copy-start(bf16[16,6912]{1,0:T(8,128)(2,1)S(1)} %get-tuple-element.95.refs_3_) | copy-start | bytes 663556
  247.2 4.4 %copy-start.4 = (bf16[16,6912]{1,0:T(8,128)(2,1)}, bf16[16,6912]{1,0:T(8,128)(2,1)S(1)}, u32[]{:S(2)}) copy-start(bf16[16,6912]{1,0:T(8,128)(2,1)S(1)} %get-tuple-element.96.refs_2_) | copy-start | bytes 663556
  247.2 4.4 %copy-start.5 = (bf16[16,6912]{1,0:T(8,128)(2,1)}, bf16[16,6912]{1,0:T(8,128)(2,1)S(1)}, u32[]{:S(2)}) copy-start(bf16[16,6912]{1,0:T(8,128)(2,1)S(1)} %get-tuple-element.97.refs_1_) | copy-start | bytes 663556
  247.2 30.5 %collective-permute-start.18 = (bf16[16,6912]{1,0:T(8,128)(2,1)S(1)}, bf16[16,6912]{1,0:T(8,128)(2,1)S(1)}, u32[]{:S(2)}, u32[]{:S(2)}) collective-permute-start(bf16[16,6912]{1,0:T(8,128)(2,1)S(1)} %get-tuple-element.97.refs_1_), channel_id=1, source_target_pairs={{0,8},{1,9},{2,10},{3,11},{4,12},{5,13},{6,14},{7,15},{8,0},{9,1},... | collective-permute-start | bytes 663560 | tf_op jit(solution)/shard_map/ppermute | solution.py:545
  248.8 28.9 %collective-permute-start.19 = (bf16[16,6912]{1,0:T(8,128)(2,1)S(1)}, bf16[16,6912]{1,0:T(8,128)(2,1)S(1)}, u32[]{:S(2)}, u32[]{:S(2)}) collective-permute-start(bf16[16,6912]{1,0:T(8,128)(2,1)S(1)} %get-tuple-element.96.refs_2_), channel_id=1, source_target_pairs={{0,16},{1,17},{2,18},{3,19},{4,20},{5,21},{6,22},{7,23},{8,24},{9,... | collective-permute-start | bytes 663560 | tf_op jit(solution)/shard_map/ppermute | solution.py:545
  249.7 28.0 %collective-permute-start.20 = (bf16[16,6912]{1,0:T(8,128)(2,1)S(1)}, bf16[16,6912]{1,0:T(8,128)(2,1)S(1)}, u32[]{:S(2)}, u32[]{:S(2)}) collective-permute-start(bf16[16,6912]{1,0:T(8,128)(2,1)S(1)} %get-tuple-element.95.refs_3_), channel_id=1, source_target_pairs={{0,24},{1,25},{2,26},{3,27},{4,28},{5,29},{6,30},{7,31},{8,16},{9,... | collective-permute-start | bytes 663560 | tf_op jit(solution)/shard_map/ppermute | solution.py:545
  267.1 11.7 %collective-permute-start.11 = (bf16[256,2048]{1,0:T(8,128)(2,1)}, bf16[256,2048]{1,0:T(8,128)(2,1)S(1)}, u32[]{:S(2)}, u32[]{:S(2)}) collective-permute-start(bf16[256,2048]{1,0:T(8,128)(2,1)} %get-tuple-element.79), channel_id=1, source_target_pairs={{0,1},{1,0},{2,3},{3,2},{4,5},{5,4},{6,7},{7,6},{8,9},{9,8},{10,11... | collective-permute-start | bytes 3145736 | tf_op jit(solution)/shard_map/ppermute | solution.py:545
  267.2 11.6 %copy-start.2 = (bf16[256,2048]{1,0:T(8,128)(2,1)S(1)}, bf16[256,2048]{1,0:T(8,128)(2,1)}, u32[]{:S(2)}) copy-start(bf16[256,2048]{1,0:T(8,128)(2,1)} %get-tuple-element.78.after_ref) | copy-start | bytes 3145732
  279.3 8.8 %collective-permute-start.12 = (bf16[64,2048]{1,0:T(8,128)(2,1)S(1)}, bf16[64,2048]{1,0:T(8,128)(2,1)S(1)}, u32[]{:S(2)}, u32[]{:S(2)}) collective-permute-start(bf16[64,2048]{1,0:T(8,128)(2,1)S(1)} %get-tuple-element.92), channel_id=1, source_target_pairs={{0,2},{1,3},{2,0},{3,1},{4,6},{5,7},{6,4},{7,5},{8,10},{9,11},{10,... | collective-permute-start | bytes 786440 | tf_op jit(solution)/shard_map/ppermute | solution.py:545
  280.7 9.1 %collective-permute-start.13 = (bf16[64,2048]{1,0:T(8,128)(2,1)S(1)}, bf16[64,2048]{1,0:T(8,128)(2,1)S(1)}, u32[]{:S(2)}, u32[]{:S(2)}) collective-permute-start(bf16[64,2048]{1,0:T(8,128)(2,1)S(1)} %get-tuple-element.94), channel_id=1, source_target_pairs={{0,4},{1,5},{2,6},{3,7},{4,0},{5,1},{6,2},{7,3},{8,12},{9,13},{10,... | collective-permute-start | bytes 786440 | tf_op jit(solution)/shard_map/ppermute | solution.py:545
  281.6 13.3 %collective-permute-start.14 = (bf16[64,2048]{1,0:T(8,128)(2,1)S(1)}, bf16[64,2048]{1,0:T(8,128)(2,1)S(1)}, u32[]{:S(2)}, u32[]{:S(2)}) collective-permute-start(bf16[64,2048]{1,0:T(8,128)(2,1)S(1)} %get-tuple-element.93), channel_id=1, source_target_pairs={{0,6},{1,7},{2,4},{3,5},{4,2},{5,3},{6,0},{7,1},{8,14},{9,15},{10,... | collective-permute-start | bytes 786440 | tf_op jit(solution)/shard_map/ppermute | solution.py:545
  295.0 5.1 %collective-permute-start.15 = (bf16[16,2048]{1,0:T(8,128)(2,1)S(1)}, bf16[16,2048]{1,0:T(8,128)(2,1)S(1)}, u32[]{:S(2)}, u32[]{:S(2)}) collective-permute-start(bf16[16,2048]{1,0:T(8,128)(2,1)S(1)} %get-tuple-element.101), channel_id=1, source_target_pairs={{0,8},{1,9},{2,10},{3,11},{4,12},{5,13},{6,14},{7,15},{8,0},{9,1},... | collective-permute-start | bytes 196616 | tf_op jit(solution)/shard_map/ppermute | solution.py:545
  295.8 6.8 %collective-permute-start.16 = (bf16[16,2048]{1,0:T(8,128)(2,1)S(1)}, bf16[16,2048]{1,0:T(8,128)(2,1)S(1)}, u32[]{:S(2)}, u32[]{:S(2)}) collective-permute-start(bf16[16,2048]{1,0:T(8,128)(2,1)S(1)} %get-tuple-element.103), channel_id=1, source_target_pairs={{0,16},{1,17},{2,18},{3,19},{4,20},{5,21},{6,22},{7,23},{8,24},{9,... | collective-permute-start | bytes 196616 | tf_op jit(solution)/shard_map/ppermute | solution.py:545
  297.6 6.2 %collective-permute-start.17 = (bf16[16,2048]{1,0:T(8,128)(2,1)S(1)}, bf16[16,2048]{1,0:T(8,128)(2,1)S(1)}, u32[]{:S(2)}, u32[]{:S(2)}) collective-permute-start(bf16[16,2048]{1,0:T(8,128)(2,1)S(1)} %get-tuple-element.102), channel_id=1, source_target_pairs={{0,24},{1,25},{2,26},{3,27},{4,28},{5,29},{6,30},{7,31},{8,16},{9,... | collective-permute-start | bytes 196616 | tf_op jit(solution)/shard_map/ppermute | solution.py:545
Sparse Core Ops, SparseCore 0:
  11.0 76.6 all-gather.1

commit v3 on v2

v3 whole, which is shorter than its diff:
```python
import functools
import math

import jax
import jax.numpy as jnp
import numpy as np
from jax import lax
from jax.experimental import pallas as pl
from jax.experimental.pallas import tpu as pltpu
from jax.sharding import PartitionSpec as P

D = 512
H = 8
FF = 3200
HD = 64
PACK = 640
LONG = 302
PLACES = 384
SCALE = 0.125
EPS = 1e-05
NEG = -1e9
WT = 3 * D + PLACES
WA = WT + 128
BLOCK = 16
BLOCKS = D // BLOCK
PIECES = 4
PIECE = D // (2 * PIECES)
WB = D + 2 * FF
TILE = 512
PARTS = 1
FF_CHUNKS = ((0, 1536), (1536, 1664))
ITEMS = 9
SHORT_WINDOW = (96, 128)
LONG_WINDOW = (320, 384)
SHORT_MOST = SHORT_WINDOW[0] - 15
PROB_ROWS = 1024
GROUP = 4
GROUPS = H // GROUP
GD = GROUP * HD
PROB_COLS = GROUP * LONG_WINDOW[1]
AXES = ("wide", "narrow")
VMEM = 60 * 1024 * 1024
BF = jnp.bfloat16
F32 = jnp.float32


def nn(a, b):
    return lax.dot_general(a, b, (((1,), (0,)), ((), ())), preferred_element_type=F32)


def nt(a, b):
    return lax.dot_general(a, b, (((1,), (1,)), ((), ())), preferred_element_type=F32)


def item_masks(seg_row):
    wide = jnp.broadcast_to(seg_row.astype(F32), (8, PACK))
    col = jnp.transpose(wide)[:, 0:1]
    return col == wide[0:1]


def place_picks(same):
    lane = lax.broadcasted_iota(jnp.int32, (PACK, PACK), 1).astype(F32)
    first = jnp.min(jnp.where(same, lane, 1e6), axis=1, keepdims=True)
    place = lax.broadcasted_iota(jnp.int32, (PACK, 1), 0).astype(F32) - first
    slot = lax.broadcasted_iota(jnp.int32, (PACK, PLACES), 1).astype(F32)
    return jnp.where((place == slot) | (slot == PLACES - 1), 1.0, 0.0).astype(BF)


def each_item(starts_ref, pack, body):
    def visit(n, place):
        first = starts_ref[pack * (ITEMS + 1) + n]
        end = starts_ref[pack * (ITEMS + 1) + n + 1]
        length = end - first

        def window(sizes):
            spans = []
            for size in sizes:
                base = pl.multiple_of(jnp.minimum(lax.div(first, 16) * 16, PACK - size), 16)
                spans.append((size, pl.ds(base, size), first - base, end - base))
            body(*spans, pl.ds(pl.multiple_of(place, 16), sizes[0]))

        short = length <= SHORT_MOST

        @pl.when((length > 0) & short)
        def _():
            window(SHORT_WINDOW)

        @pl.when(length > SHORT_MOST)
        def _():
            window(LONG_WINDOW)

        return place + jnp.where(length > 0, jnp.where(short, SHORT_WINDOW[0], LONG_WINDOW[0]), 0)

    lax.fori_loop(0, ITEMS, visit, jnp.int32(0))


def by_head(block):
    lane = lax.broadcasted_iota(jnp.int32, block.shape, 1)
    zero = jnp.zeros_like(block)
    return jnp.concatenate([jnp.where((lane >= h * HD) & (lane < (h + 1) * HD), block, zero) for h in range(GROUP)], axis=0)


def heads_turned(left_t, right, size):
    parts = [nn(left_t[h * HD : (h + 1) * HD], right[:, h * size : (h + 1) * size]) for h in range(GROUP)]
    return jnp.concatenate(parts, axis=0)


GROUP_LANES = [slice(g * GD, (g + 1) * GD) for g in range(GROUPS)]


def block_rows(me_ref, place):
    owner = me_ref[0] ^ offsets(BLOCKS)[place]
    return pl.ds(pl.multiple_of(owner * BLOCK, BLOCK), BLOCK)


def block_loads(me_ref, halves, full_ref, sem):
    copies = []
    for place in range(BLOCKS):
        half, at = divmod(place, BLOCKS // 2)
        copies.append(pltpu.make_async_copy(halves[half].at[at * BLOCK : (at + 1) * BLOCK], full_ref.at[block_rows(me_ref, place)], sem))
    return copies


def load_blocks(me_ref, halves, full_ref, sem):
    copies = block_loads(me_ref, halves, full_ref, sem)
    for copy in copies:
        copy.start()
    for copy in copies:
        copy.wait()


def block_copies(me_ref, ref, col, width, pieces, sem):
    copies = []
    for place in range(BLOCKS):
        piece, at = divmod(place * BLOCK, PIECE)
        target = pieces[piece].at[at : at + BLOCK, col : col + width]
        copies.append(pltpu.make_async_copy(ref.at[block_rows(me_ref, place)], target, sem))
    return copies


def store_blocks(me_ref, ref, pieces, sem):
    copies = block_copies(me_ref, ref, 0, ref.shape[1], pieces, sem)
    for copy in copies:
        copy.start()
    for copy in copies:
        copy.wait()


def attend_kernel(me_ref, starts_ref, seg_ref, x_ref, al_ref, ar_ref, st_ref, q_ref, k_ref, v_ref, mix_ref, attn_ref, picks_ref, pt_ref, vec_ref, pieces_ref, ga_ref, hi_ref, lo_ref, sem):
    @pl.when(pl.program_id(0) == 0)
    def _():
        load_blocks(me_ref, (al_ref, ar_ref), ga_ref, sem)
        pieces_ref[...] = ga_ref[:, WT:].astype(F32)
        vec_ref[...] = jnp.transpose(pieces_ref[...])
        pos = st_ref[...] + ga_ref[:, 3 * D : 3 * D + PLACES].astype(F32)
        pos = jnp.where(lax.broadcasted_iota(jnp.int32, pos.shape, 1) < LONG, pos, 0.0)
        hi = pos.astype(BF)
        hi_ref[...] = hi
        lo_ref[...] = (pos - hi.astype(F32)).astype(BF)

    picks = place_picks(item_masks(seg_ref[...]))
    picks_ref[...] = picks
    x = x_ref[...]
    positions = nt(picks, hi_ref[...]) + nt(picks, lo_ref[...])
    mixed = (x.astype(F32) + positions).astype(BF)
    mix_ref[...] = mixed
    q_ref[...] = ((nt(mixed, ga_ref[:, 0:D]) + vec_ref[0:1]).astype(BF).astype(F32) * SCALE).astype(BF)
    k_ref[...] = nt(mixed, ga_ref[:, D : 2 * D]).astype(BF)
    v = (nt(x, ga_ref[:, 2 * D : 3 * D]) + vec_ref[1:2]).astype(BF)
    v_ref[...] = v
    attn_ref[...] = jnp.zeros_like(attn_ref)

    def item(key_span, query_span, store):
        keys, key_rows, low, high = key_span
        down = lax.broadcasted_iota(jnp.int32, (keys, 1), 0)
        shut = jnp.where((down >= low) & (down < high), 0.0, NEG)
        queries, query_rows, low, high = query_span
        across = lax.broadcasted_iota(jnp.int32, (1, queries), 1)
        live = jnp.where((across >= low) & (across < high), 1.0, 0.0)
        live = jnp.concatenate([live] * GROUP, axis=1)
        scores = [nt(k_ref[key_rows, lanes], by_head(q_ref[query_rows, lanes])) + shut for lanes in GROUP_LANES]
        probs = []
        for g in range(GROUPS):
            exps = jnp.exp(scores[g] - jnp.max(scores[g], axis=0, keepdims=True))
            scale = live / jnp.sum(exps, axis=0, keepdims=True)
            probs.append((exps * scale).astype(BF))
            pt_ref[0, g, store, 0 : GROUP * queries] = probs[g]
        for g, lanes in enumerate(GROUP_LANES):
            outs = heads_turned(jnp.transpose(v_ref[key_rows, lanes]), probs[g], queries)
            attn_ref[query_rows, lanes] += jnp.transpose(outs.astype(BF))

    each_item(starts_ref, pl.program_id(0), item)


def whole(shape):
    return pl.BlockSpec(shape, lambda i: tuple(0 for _ in shape), pipeline_mode=pl.Buffered(1))


def rows_of(count, width):
    return pl.BlockSpec((count, width), lambda i: (i, 0))


SCALAR = pl.BlockSpec(memory_space=pltpu.SMEM)
LOOSE = pl.BlockSpec(memory_space=pl.ANY)


def attend(where, starts, seg, x, halves, st):
    tokens = seg.shape[1]
    packs = tokens // PACK
    low = jax.ShapeDtypeStruct((tokens, D), BF)
    return pl.pallas_call(
        attend_kernel,
        grid=(packs,),
        in_specs=[SCALAR, SCALAR, pl.BlockSpec((1, PACK), lambda i: (0, i)), rows_of(PACK, D), LOOSE, LOOSE, whole((D, PLACES))],
        out_specs=[rows_of(PACK, D)] * 5 + [rows_of(PACK, PLACES), pl.BlockSpec((1, GROUPS, PROB_ROWS, PROB_COLS), lambda i: (i, 0, 0, 0)), whole((128, D)), whole((D, 128))],
        out_shape=[low] * 5
        + [
            jax.ShapeDtypeStruct((tokens, PLACES), BF),
            jax.ShapeDtypeStruct((packs, GROUPS, PROB_ROWS, PROB_COLS), BF), jax.ShapeDtypeStruct((128, D), F32), jax.ShapeDtypeStruct((D, 128), F32)],
        scratch_shapes=[
            pltpu.VMEM((D, WA), BF),
            pltpu.VMEM((D, PLACES), BF),
            pltpu.VMEM((D, PLACES), BF),
            pltpu.SemaphoreType.DMA,
        ],
        compiler_params=pltpu.CompilerParams(vmem_limit_bytes=VMEM),
        cost_estimate=pl.CostEstimate(flops=40 * 10**9, bytes_accessed=50 * 10**6, transcendentals=0),
        name="attend",
    )(where, starts, seg, x, *halves, st)


def centre(v):
    c = v - jnp.mean(v, axis=-1, keepdims=True)
    r = lax.rsqrt(jnp.mean(c * c, axis=-1, keepdims=True) + EPS)
    return c * r, r


def norm_back(g, n, r):
    return r * (g - jnp.mean(g, axis=-1, keepdims=True) - n * jnp.mean(g * n, axis=-1, keepdims=True))


def col_sum(v):
    return jnp.sum(v, axis=0, keepdims=True)


GELU_A = math.sqrt(2.0 / math.pi)
GELU_B = 0.044715


def feed_kernel(narrow, own_rows, me_ref, x_ref, attn_ref, cot_ref, pad_ref, gb_ref, vec_ref, bup_ref, out_ref, dfirst_ref, dattn_ref, *refs):
    pieces, scratch = refs[: 2 * PIECES], refs[2 * PIECES :]
    act_ref, slope_ref, up_acc, down_acc, wo_acc, wo_low, side_ref, gv_ref, gbu_ref, sem = scratch
    step = pl.program_id(0)

    @pl.when(step == 0)
    def _():
        up_acc[...] = jnp.zeros_like(up_acc)
        down_acc[...] = jnp.zeros_like(down_acc)
        wo_acc[...] = jnp.zeros_like(wo_acc)
        gv_ref[...] = jnp.zeros_like(gv_ref)
        gbu_ref[...] = jnp.zeros_like(gbu_ref)

    gain_one, gain_two = vec_ref[3:4], vec_ref[6:7]
    keep_all = jnp.transpose(jnp.broadcast_to(pad_ref[...].astype(F32), (8, TILE)))[:, 0:1]
    parts = [slice(at, at + TILE // PARTS) for at in range(0, TILE, TILE // PARTS)]
    hidden, norm_one, r_one, hidden_t = {}, {}, {}, {}
    d_second, d_ff_t, d_hidden, d_branch_t, ff = {}, {}, {}, {}, {}

    def enter(p):
        rows = parts[p]
        first_sum = x_ref[rows].astype(F32) + (nt(attn_ref[rows], gb_ref[:, 0:D]) + vec_ref[2:3])
        norm_one[p], r_one[p] = centre(first_sum)
        hidden[p] = gain_one * norm_one[p] + vec_ref[4:5]

    def ahead(p):
        rows = parts[p]
        hidden_low = hidden[p].astype(BF)
        hidden_t[p] = jnp.transpose(hidden_low)
        ff[p] = 0.0
        for start, size in FF_CHUNKS:
            cols = slice(start, start + size)
            u = nn(hidden_low, gb_ref[:, D + start : D + start + size]) + bup_ref[0:1, cols]
            u2 = u * u
            t = jnp.tanh(u * (GELU_A + GELU_A * GELU_B * u2))
            h = 0.5 + 0.5 * t
            act = (u * h).astype(BF)
            act_ref[rows, cols] = act
            slope_ref[rows, cols] = (h + (u * h) * (1.0 - t) * (GELU_A + 3.0 * GELU_A * GELU_B * u2)).astype(BF)
            ff[p] = ff[p] + nt(act, gb_ref[:, D + FF + start : D + FF + start + size])

    def turn(p):
        rows = parts[p]
        keep = keep_all[rows]
        norm_two, r_two = centre(hidden[p] + (ff[p] + vec_ref[5:6]))
        out_ref[rows] = ((gain_two * norm_two + vec_ref[7:8]) * keep).astype(BF)
        top = cot_ref[rows].astype(F32) * keep
        gv_ref[6:7] += col_sum(top * norm_two)
        gv_ref[7:8] += col_sum(top)
        d_second[p] = norm_back(top * gain_two, norm_two, r_two)

    def behind(p):
        rows = parts[p]
        d_ff = d_second[p].astype(BF)
        gv_ref[5:6] += col_sum(d_ff.astype(F32))
        d_ff_t[p] = jnp.transpose(d_ff)
        d_hidden[p] = d_second[p]
        for start, size in FF_CHUNKS:
            cols = slice(start, start + size)
            d_act = nn(d_ff, gb_ref[:, D + FF + start : D + FF + start + size])
            d_pre = (slope_ref[rows, cols].astype(F32) * d_act).astype(BF)
            slope_ref[rows, cols] = d_pre
            gbu_ref[0:1, cols] += col_sum(d_pre.astype(F32))
            d_hidden[p] = d_hidden[p] + nt(d_pre, gb_ref[:, D + start : D + start + size])

    def leave(p):
        rows = parts[p]
        gv_ref[3:4] += col_sum(d_hidden[p] * norm_one[p])
        gv_ref[4:5] += col_sum(d_hidden[p])
        d_first = norm_back(d_hidden[p] * gain_one, norm_one[p], r_one[p])
        dfirst_ref[rows] = d_first
        d_branch = d_first.astype(BF)
        gv_ref[2:3] += col_sum(d_branch.astype(F32))
        d_branch_t[p] = jnp.transpose(d_branch)
        dattn_ref[rows] = nn(d_branch, gb_ref[:, 0:D]).astype(BF)

    def joined(pieces):
        return jnp.concatenate([pieces[p] for p in range(PARTS)], axis=1)

    def weights():
        ff_t, low_t = joined(d_ff_t), joined(hidden_t)
        for start, size in FF_CHUNKS:
            cols = slice(start, start + size)
            down_acc[:, cols] += nn(ff_t, act_ref[:, cols])
            up_acc[:, cols] += nn(low_t, slope_ref[:, cols])

    enter(0); ahead(0); turn(0); behind(0); leave(0); weights()
    wo_acc[...] += nn(joined(d_branch_t), attn_ref[...])

    @pl.when(step == pl.num_programs(0) - 1)
    def _():
        def send(ref, at, size):
            copies = block_copies(me_ref, ref, at, size, pieces, sem)
            for copy in copies:
                copy.start()
            return copies

        act_ref[...] = up_acc[...].astype(BF)
        copies = send(act_ref, D, FF)
        slope_ref[...] = down_acc[...].astype(BF)
        copies += send(slope_ref, D + FF, FF)
        wo_low[...] = wo_acc[...].astype(BF)
        copies += send(wo_low, 0, D)
        side = side_columns(narrow, own_rows, gbu_ref, side_ref.shape[1])
        vectors = jnp.transpose(jnp.concatenate([gv_ref[...], jnp.zeros((120, D), F32)], axis=0))
        first = side[:, 0:128] + vectors
        side_ref[:, 0:128] = first.astype(BF)
        if side_ref.shape[1] > 128:
            side_ref[:, 128:] = side[:, 128:].astype(BF)
        copies += send(side_ref, WB, side_ref.shape[1])
        for copy in copies:
            copy.wait()


def side_columns(narrow, own_rows, sums_ref, width):
    span = sums_ref.shape[1]
    bias = FF // narrow
    lane = lax.broadcasted_iota(jnp.int32, (1, width), 1)
    lines = []
    for n in range(narrow):
        for r in range(own_rows):
            at = r * (width - 8)
            if at < bias:
                moved = pltpu.roll(sums_ref[...], (span + 8 - n * bias - at) % span, 1)[0:1, 0:width]
                lines.append(jnp.where((lane >= 8) & (lane - 8 + at < bias), moved, 0.0))
            else:
                lines.append(jnp.zeros((1, width), F32))
    block = jnp.concatenate(lines, axis=0)
    return jnp.concatenate([block] * (D // block.shape[0]), axis=0)


def side_width(narrow, own_rows):
    return -(-(8 + -(-(FF // narrow) // own_rows)) // 128) * 128


def feed(narrow, own_rows, where, x, attn, cot, pad, gb, vec, bup):
    tokens = x.shape[0]
    side = side_width(narrow, own_rows)
    return pl.pallas_call(
        functools.partial(feed_kernel, narrow, own_rows),
        grid=(tokens // TILE,),
        in_specs=[
            SCALAR,
            rows_of(TILE, D),
            rows_of(TILE, D),
            rows_of(TILE, D),
            pl.BlockSpec((1, TILE), lambda i: (0, i)),
            whole((D, WB)),
            whole((128, D)),
            whole((1, FF)),
        ],
        out_specs=[rows_of(TILE, D), rows_of(TILE, D), rows_of(TILE, D)] + [LOOSE] * (2 * PIECES),
        out_shape=[
            jax.ShapeDtypeStruct((tokens, D), BF),
            jax.ShapeDtypeStruct((tokens, D), F32),
            jax.ShapeDtypeStruct((tokens, D), BF),
        ]
        + [jax.ShapeDtypeStruct((PIECE, WB + side), BF)] * (2 * PIECES),
        scratch_shapes=[
            pltpu.VMEM((TILE, FF), BF),
            pltpu.VMEM((TILE, FF), BF),
            pltpu.VMEM((D, FF), F32),
            pltpu.VMEM((D, FF), F32),
            pltpu.VMEM((D, D), F32),
            pltpu.VMEM((D, D), BF),
            pltpu.VMEM((D, side), BF),
            pltpu.VMEM((8, D), F32),
            pltpu.VMEM((8, FF + 128), F32),
            pltpu.SemaphoreType.DMA,
        ],
        compiler_params=pltpu.CompilerParams(vmem_limit_bytes=VMEM),
        cost_estimate=pl.CostEstimate(flops=80 * 10**9, bytes_accessed=40 * 10**6, transcendentals=0),
        name="feed",
    )(where, x, attn, cot, pad.reshape(1, tokens), gb, vec, bup)


def tn(a, b):
    return lax.dot_general(a, b, (((0,), (0,)), ((), ())), preferred_element_type=F32)


ACC = 3 * D + 2 * PLACES + 128


def core_kernel(me_ref, starts_ref, q_ref, k_ref, v_ref, dattn_ref, pt_ref, x_ref, mix_ref, picks_ref, al_ref, ar_ref, *refs):
    dq_ref, dk_ref, dv_ref, *pieces, acc, ga_ref, gw_ref, sem = refs[-(3 + 2 * PIECES + 4) :]
    step = pl.program_id(0)

    @pl.when(step == 0)
    def _():
        acc[...] = jnp.zeros_like(acc)

    for ref in (dq_ref, dk_ref, dv_ref):
        ref[...] = jnp.zeros_like(ref)

    def item(key_span, query_span, store):
        key_rows = key_span[1]
        queries, query_rows = query_span[:2]
        d_outs = [by_head(dattn_ref[query_rows, lanes]) for lanes in GROUP_LANES]
        d_probs = [nt(v_ref[key_rows, lanes], d_outs[g]) for g, lanes in enumerate(GROUP_LANES)]
        probs = [pt_ref[0, g, store, 0 : GROUP * queries] for g in range(GROUPS)]
        d_scores = []
        for g in range(GROUPS):
            wide = probs[g].astype(F32)
            delta = jnp.sum(wide * d_probs[g], axis=0, keepdims=True)
            d_scores.append((wide * (d_probs[g] - delta)).astype(BF))
        for g, lanes in enumerate(GROUP_LANES):
            dv_ref[key_rows, lanes] += nn(probs[g], d_outs[g]).astype(BF)
            dk_ref[key_rows, lanes] += nn(d_scores[g], by_head(q_ref[query_rows, lanes])).astype(BF)
            d_queries = heads_turned(jnp.transpose(k_ref[key_rows, lanes]), d_scores[g], queries) * SCALE
            dq_ref[query_rows, lanes] += jnp.transpose(d_queries.astype(BF))

    each_item(starts_ref, step, item)
    dq_t, dk_t, dv_t = (jnp.transpose(ref[...]) for ref in (dq_ref, dk_ref, dv_ref))
    mixed, picks = mix_ref[...], picks_ref[...]
    acc[:, 0:D] += nn(dq_t, mixed)
    acc[:, D : 2 * D] += nn(dk_t, mixed)
    acc[:, 2 * D : 3 * D] += nn(dv_t, x_ref[...])
    acc[:, 3 * D : 3 * D + PLACES] += nn(dq_t, picks)
    acc[:, 3 * D + PLACES : 3 * D + 2 * PLACES] += nn(dk_t, picks)
    acc[:, 3 * D + 2 * PLACES :] += nn(dv_t, jnp.ones((PACK, 128), BF))

    @pl.when(step == pl.num_programs(0) - 1)
    def _():
        load_blocks(me_ref, (al_ref, ar_ref), ga_ref, sem)
        gw_ref[:, 0 : 3 * D] = acc[:, 0 : 3 * D].astype(BF)
        table = tn(ga_ref[:, 0:D], acc[:, 3 * D : 3 * D + PLACES].astype(BF))
        table = table + tn(ga_ref[:, D : 2 * D], acc[:, 3 * D + PLACES : 3 * D + 2 * PLACES].astype(BF))
        gw_ref[:, 3 * D : WT] = table.astype(BF)
        lane = lax.broadcasted_iota(jnp.int32, (D, 128), 1)
        query_sum = acc[:, 3 * D + PLACES - 1 : 3 * D + PLACES]
        sums = jnp.where(lane == 0, query_sum, jnp.where(lane == 1, acc[:, 3 * D + 2 * PLACES :], 0.0))
        gw_ref[:, WT:] = sums.astype(BF)
        store_blocks(me_ref, gw_ref, pieces, sem)


def core_back(where, starts, q, k, v, d_attn, pt, x, mixed, picks, halves, after):
    tokens = x.shape[0]
    probs = pl.BlockSpec((1, GROUPS, PROB_ROWS, PROB_COLS), lambda i: (i, 0, 0, 0))
    flat = rows_of(PACK, D)
    return pl.pallas_call(
        core_kernel,
        grid=(tokens // PACK,),
        in_specs=[SCALAR, SCALAR] + [flat] * 4 + [probs, flat, flat, rows_of(PACK, PLACES)] + [LOOSE] * (2 + len(after)),
        out_specs=[flat] * 3 + [LOOSE] * (2 * PIECES),
        out_shape=[jax.ShapeDtypeStruct((tokens, D), BF)] * 3 + [jax.ShapeDtypeStruct((PIECE, WA), BF)] * (2 * PIECES),
        scratch_shapes=[pltpu.VMEM((D, ACC), F32), pltpu.VMEM((D, WA), BF), pltpu.VMEM((D, WA), BF), pltpu.SemaphoreType.DMA],
        compiler_params=pltpu.CompilerParams(vmem_limit_bytes=VMEM),
        cost_estimate=pl.CostEstimate(flops=50 * 10**9, bytes_accessed=50 * 10**6, transcendentals=0),
        name="core_back",
    )(where, starts, q, k, v, d_attn, pt, x, mixed, picks, *halves, *after)


def inputs_kernel(me_ref, dq_ref, dk_ref, dv_ref, dfirst_ref, al_ref, ar_ref, *refs):
    out_ref, ga_ref, sem = refs[-3:]

    @pl.when(pl.program_id(0) == 0)
    def _():
        load_blocks(me_ref, (al_ref, ar_ref), ga_ref, sem)

    d_mixed = nn(dq_ref[...], ga_ref[:, 0:D]) + nn(dk_ref[...], ga_ref[:, D : 2 * D])
    out_ref[...] = (dfirst_ref[...] + d_mixed + nn(dv_ref[...], ga_ref[:, 2 * D : 3 * D])).astype(BF)


def input_grads(where, flat, d_first, halves, after):
    tokens = d_first.shape[0]
    return pl.pallas_call(
        inputs_kernel,
        grid=(tokens // PACK,),
        in_specs=[SCALAR] + [rows_of(PACK, D)] * 4 + [LOOSE] * (2 + len(after)),
        out_specs=rows_of(PACK, D),
        out_shape=jax.ShapeDtypeStruct((tokens, D), BF),
        scratch_shapes=[pltpu.VMEM((D, WA), BF), pltpu.SemaphoreType.DMA],
        compiler_params=pltpu.CompilerParams(vmem_limit_bytes=VMEM),
        cost_estimate=pl.CostEstimate(flops=8 * 10**9, bytes_accessed=20 * 10**6, transcendentals=0),
        name="input_grads",
    )(where, *flat, d_first, *halves, *after)


def finish_kernel(count, *refs):
    a_refs, b_refs, outs, turn_ref = refs[:count], refs[count : 2 * count], refs[2 * count : -1], refs[-1]

    def total(pieces, start, size):
        result = pieces[0][:, start : start + size].astype(F32)
        for piece in pieces[1:]:
            result = result + piece[:, start : start + size].astype(F32)
        return result

    query, key, value, out, up, down, table = outs[:7]
    for at, ref in enumerate((query, key, value)):
        ref[...] = total(a_refs, at * D, D)
    out[...] = total(b_refs, 0, D)
    up[...] = total(b_refs, D, FF)
    down[...] = total(b_refs, D + FF, FF)
    table[...] = total(a_refs, 3 * D, PLACES)[:, 0:LONG]
    rows = query.shape[0]
    side = total(b_refs, WB, outs[-1].shape[1])
    outs[-1][...] = side
    lane = lax.broadcasted_iota(jnp.int32, (rows, 128), 1)
    turn_ref[...] = jnp.zeros_like(turn_ref)
    turn_ref[0:rows] = jnp.where(lane < 2, total(a_refs, WT, 128), side[:, 0:128])
    turned = jnp.transpose(turn_ref[...])
    for n, ref in enumerate(outs[7:15]):
        ref[...] = turned[n : n + 1, 0:rows]


def finish(a_parts, b_parts):
    rows = a_parts[0].shape[0]
    widths = [D, D, D, D, FF, FF, LONG]
    shapes = [(rows, width) for width in widths] + [(1, rows)] * 8 + [(rows, b_parts[0].shape[1] - WB)]
    vmem = pl.BlockSpec(memory_space=pltpu.VMEM)
    outs = pl.pallas_call(
        functools.partial(finish_kernel, len(a_parts)),
        in_specs=[vmem] * (2 * len(a_parts)),
        out_specs=[vmem] * len(shapes),
        out_shape=[jax.ShapeDtypeStruct(shape, F32) for shape in shapes],
        scratch_shapes=[pltpu.VMEM((128, 128), F32)],
        name="finish",
    )(*a_parts, *b_parts)
    return (*outs[:7], outs[7:15], outs[15])


def sines():
    half = D // 2
    frequency = np.exp(np.arange(half, dtype=np.float32) * np.float32(-2.0 * math.log(10000.0) / D))
    angles = frequency[:, None] * np.arange(PLACES, dtype=np.float32)[None, :]
    return jnp.asarray(np.concatenate([np.sin(angles), np.cos(angles)], axis=0).astype(np.float32))


def pack_kernel(piece, wide_ref, wq_ref, wk_ref, wv_ref, table_ref, wo_ref, up_ref, down_ref, bup_ref, *refs):
    vectors, (a_ref, b_ref, turn_ref, bias_ref) = refs[:8], refs[8:]
    rows = a_ref.shape[0]
    a_ref[:, 0:D] = wq_ref[...]
    a_ref[:, D : 2 * D] = wk_ref[...]
    a_ref[:, 2 * D : 3 * D] = wv_ref[...]
    a_ref[:, 3 * D : WT] = jnp.zeros((rows, PLACES), BF)
    a_ref[:, 3 * D : 3 * D + LONG] = table_ref[...]
    b_ref[:, 0:D] = wo_ref[...]
    b_ref[:, D : D + FF] = up_ref[...]
    b_ref[:, D + FF :] = down_ref[...]
    turn_ref[...] = jnp.zeros_like(turn_ref)
    for n, vector in enumerate(vectors):
        turn_ref[n : n + 1, 0:rows] = vector[...].astype(F32)
    bias_ref[...] = jnp.zeros_like(bias_ref)
    bias_ref[0:1, 0 : bup_ref.shape[1]] = bup_ref[...].astype(F32)
    span = bias_ref.shape[1]
    shift = lax.rem(span + 8 - wide_ref[0] * piece, span)
    moved = pltpu.roll(bias_ref[...], shift, 1)[0:1, 0:128]
    lane = lax.broadcasted_iota(jnp.int32, (rows, 128), 1)
    row = lax.broadcasted_iota(jnp.int32, (rows, 128), 0)
    mine = (row == 0) & (lane >= 8) & (lane < 8 + piece)
    columns = jnp.transpose(turn_ref[...])[0:rows]
    a_ref[:, WT:] = jnp.where(mine, moved, columns).astype(BF)


def pack(wide_index, piece, matrices, b_up, vectors):
    rows = matrices[0].shape[0]
    span = -(-(b_up.shape[0] + 8) // 128) * 128
    return pl.pallas_call(
        functools.partial(pack_kernel, piece),
        in_specs=[SCALAR] + [pl.BlockSpec(memory_space=pltpu.VMEM)] * 16,
        out_specs=[pl.BlockSpec(memory_space=pltpu.VMEM)] * 2,
        out_shape=[jax.ShapeDtypeStruct((rows, WA), BF), jax.ShapeDtypeStruct((rows, WB), BF)],
        scratch_shapes=[pltpu.VMEM((128, 128), F32), pltpu.VMEM((8, span), F32)],
        name="pack",
    )(wide_index.reshape(1), *matrices, b_up.reshape(1, -1), *[vector.reshape(1, rows) for vector in vectors])


def bit_groups(count):
    bits = count.bit_length() - 1
    return [(0,)] + [tuple(range(at, min(at + 2, bits))) for at in range(1, bits, 2)]


def offsets(count):
    found = [0]
    for group in bit_groups(count):
        found = [old | mask for old in found for mask in masks(group)]
    return found


def masks(group):
    return [index << group[0] for index in range(1 << len(group))]


def swap(block, mask, count):
    return lax.ppermute(block, AXES, [(i, i ^ mask) for i in range(count)])


def gather_phase(own, group, count):
    return [own] + [swap(own, mask, count) for mask in masks(group)[1:]]


def split_rows(block, count):
    rows = block.shape[0] // count
    return [block[at * rows : (at + 1) * rows] for at in range(count)]


def added(sources, parts):
    return split_rows(sum(source.astype(F32) for source in sources).astype(BF), parts)


def combine_kernel(count, parts, loose, *refs):
    sources, outs = refs[:count], refs[count + loose : count + loose + parts]
    total = sources[0][...].astype(F32)
    for source in sources[1:]:
        total = total + source[...].astype(F32)
    for n, out in enumerate(outs):

        @pl.when(pl.program_id(0) == n)
        def _(out=out):
            out[...] = total.astype(BF)


def combine(sources, parts, after=(), through=()):
    rows, width = sources[0].shape
    rows //= parts
    if rows % BLOCK:
        return added(sources, parts) + list(through)
    return list(pl.pallas_call(
        functools.partial(combine_kernel, len(sources), parts, len(after) + len(through)),
        grid=(parts,),
        in_specs=[rows_of(rows, width)] * len(sources) + [LOOSE] * (len(after) + len(through)),
        out_specs=[pl.BlockSpec((rows, width), lambda i: (0, 0), pipeline_mode=pl.Buffered(1))] * parts + [LOOSE] * len(through),
        out_shape=[jax.ShapeDtypeStruct((rows, width), BF)] * parts + [jax.ShapeDtypeStruct(array.shape, array.dtype) for array in through],
        input_output_aliases={len(sources) + len(after) + n: parts + n for n in range(len(through))},
        compiler_params=pltpu.CompilerParams(vmem_limit_bytes=VMEM),
        cost_estimate=pl.CostEstimate(flops=10**6, bytes_accessed=sum(2 * source.size * 2 for source in sources), transcendentals=0),
        name="combine",
    )(*sources, *after, *through))


def exchange(parts, group, count):
    return [parts[0]] + [swap(part, mask, count) for part, mask in zip(parts[1:], masks(group)[1:])]


def scatter_core(pieces, count):
    pairs = list(zip(pieces[:PIECES], pieces[PIECES:]))
    sums = [None] * PIECES
    for n in (1, 2, 3, 0):
        keep, send = pairs[n]
        sums[n] = (keep.astype(F32) + swap(send, 1, count).astype(F32)).astype(BF)
    return sums


def local(
    inputs,
    segments,
    pad_mask,
    cotangent,
    w_query,
    b_query,
    w_key,
    w_value,
    b_value,
    w_out,
    b_out,
    gain_one,
    shift_one,
    w_up,
    b_up,
    w_down,
    b_down,
    gain_two,
    shift_two,
    pos_table,
):
    tokens = inputs.shape[0]
    narrow = lax.axis_size("narrow")
    wide = lax.axis_size("wide")
    count = wide * narrow
    me = lax.axis_index(AXES)
    groups = bit_groups(count)
    own_rows = D // count
    bits = count.bit_length() - 1
    places = [bits - 1 - bit for group in groups for bit in reversed(group)] + [bits, bits + 1]
    in_kernel = own_rows == BLOCK
    where = (me if in_kernel else jnp.zeros((), jnp.int32)).reshape(1).astype(jnp.int32)

    def flips(full):
        for axis in range(bits):
            mine = (me >> (bits - 1 - axis)) & 1
            full = jnp.where(mine == 1, jnp.flip(full, axis), full)
        return full

    def absolute(halves):
        if in_kernel:
            return halves
        full = jnp.concatenate(halves, axis=0).reshape([2] * bits + [own_rows, -1])
        full = flips(full.transpose([places.index(axis) for axis in range(bits + 2)])).reshape(D, -1)
        return full[: D // 2], full[D // 2 :]

    def relative(pieces):
        if in_kernel:
            return pieces
        full = flips(jnp.concatenate(pieces, axis=0).reshape([2] * bits + [own_rows, -1]))
        return split_rows(full.transpose(places).reshape(D, -1), 2 * PIECES)

    seg = segments.reshape(1, tokens)
    packs = tokens // PACK
    below = segments.reshape(packs, 1, PACK) < jnp.arange(ITEMS + 1, dtype=jnp.int32)[None, :, None]
    starts = jnp.sum(below.astype(jnp.int32), axis=2).reshape(packs * (ITEMS + 1))
    bias_width = b_up.shape[0]
    bias_piece = -(-bias_width // wide)
    own_a, own_b = pack(
        lax.axis_index("wide").astype(jnp.int32),
        bias_piece,
        (w_query.T, w_key.T, w_value.T, pos_table.T, w_out.T, w_up, w_down.T),
        b_up,
        (b_query, b_value, b_out, gain_one, shift_one, b_down, gain_two, shift_two),
    )
    gb = lax.all_gather(own_b, AXES, axis=0, tiled=True)
    for group in reversed(groups[1:]):
        own_a = jnp.concatenate(gather_phase(own_a, group, count), axis=0)
    a_halves = absolute(tuple(gather_phase(own_a, groups[0], count)))
    q, k, v, mixed, attn, picks, pt, vec, pieces = attend(where, starts, seg, inputs, a_halves, sines())
    bup = pieces.reshape(wide, narrow, own_rows, 128)[:, :, 0, 8 : 8 + bias_piece].transpose(1, 0, 2)
    bup = bup.reshape(narrow, wide * bias_piece)[:, :bias_width].reshape(1, FF)
    layer_out, d_first, d_attn, *grads_b = feed(narrow, own_rows, where, inputs, attn, cotangent, pad_mask, gb, vec, bup)
    parts_b = scatter_core(relative(grads_b), count)
    back = core_back(where, starts, q, k, v, d_attn, pt, inputs, mixed, picks, a_halves, parts_b)
    grads_a = relative(back[3:])
    next_parts = 1 << len(groups[2])
    parts_b = combine(exchange(parts_b, groups[1], count), next_parts, (), grads_a[PIECES:])
    grads_a = [*grads_a[:PIECES], *parts_b[next_parts:]]
    parts_b = parts_b[:next_parts]
    parts_a = scatter_core(grads_a, count)
    input_grad = input_grads(where, back[:3], d_first, a_halves, parts_a + parts_b)
    parts_a = combine(exchange(parts_a, groups[1], count), 1 << len(groups[2]), [input_grad])
    for at in range(2, len(groups) - 1):
        next_parts = 1 << len(groups[at + 1])
        parts_b = added(exchange(parts_b, groups[at], count), next_parts)
        parts_a = added(exchange(parts_a, groups[at], count), next_parts)
    g_query, g_key, g_value, g_out, g_up, g_down, g_table, vectors, side = finish(
        exchange(parts_a, groups[-1], count), exchange(parts_b, groups[-1], count)
    )
    vectors = [vector.reshape(own_rows) for vector in vectors]
    grad_b_up = side[:, 8:].reshape(-1)[:bias_width]
    return (
        layer_out,
        input_grad,
        g_query.T,
        vectors[0],
        g_key.T,
        g_value.T,
        vectors[1],
        g_out.T,
        vectors[2],
        vectors[3],
        vectors[4],
        g_up,
        grad_b_up,
        g_down.T,
        vectors[5],
        vectors[6],
        vectors[7],
        g_table.T,
    )


def solution(mesh):
    both = P(("wide", "narrow"))
    rows = P(("wide", "narrow"), None)
    cols = P(None, ("wide", "narrow"))
    in_specs = (rows, both, both, rows, cols, both, cols, cols, both, cols, both, both, both, rows, P("narrow"), cols, both, both, both, cols)
    out_specs = (rows, rows, cols, both, cols, cols, both, cols, both, both, both, rows, P("narrow"), cols, both, both, both, cols)
    return jax.shard_map(local, mesh=mesh, in_specs=in_specs, out_specs=out_specs, check_vma=False)
```

time: 314 us -> 280 us (0.89)
  waiting for transfers between devices: 59.4 us -> 35.3 us
  local copies, waits for them, and re-layouts: 18.9 us -> 11.4 us
  other arithmetic: 8.6 us -> 4.21 us
  starting transfers between devices: 25.6 us -> 29 us
    ppermute x21 -> x27, waiting for transfers between devices: 51.9 us -> 29.4 us  [swap(): return lax.ppermute(block, AXES, [(i, i ^ mask) for i in range(count)])]
    ppermute x21 -> x27, starting transfers between devices: 25.6 us -> 29 us  [swap(): return lax.ppermute(block, AXES, [(i, i ^ mask) for i in range(count)])]
    pallas_call x4 -> x5, Pallas kernels: 137 us -> 134 us  [the longest x1 81.5 us: feed(): pl.pallas_call(functools.partial(feed_kernel, narrow, own_rows), grid=(to...]
    convert_element_type x4 -> x8, other arithmetic: 6.53 us -> 3.96 us  [scatter_core(): sums[n] = (keep.astype(F32) + swap(send, 1, count).astype(F32)).astype(BF)]
  transfers between devices with their start and end apart: 22 -> 28, of which waited for: 14 -> 14; matrix products, arithmetic and copies ran while one was open for 3% -> 3% of each run, Pallas kernels for 32% -> 34%
where the time goes in v3:
time: 280 us; the launch traced here: 279 us
  Pallas kernels  185 us (66%)
  waiting for transfers between devices  35.3 us (13%)
  starting transfers between devices  29 us (10%)
  between operations  14.4 us (5%)
  local copies, waits for them, and re-layouts  11.4 us (4%)
  other arithmetic  4.21 us (2%)
    pallas_call x1, Pallas kernels, feed(): pl.pallas_call(functools.partial(feed_kernel, narrow, own_rows), grid=(to...  81.5 us
    pallas_call x1, Pallas kernels, core_back(): pl.pallas_call(core_kernel, grid=(tokens // PACK,), in_specs=[SCALAR, SCA...  43.2 us
    pallas_call x1, Pallas kernels, attend(): pl.pallas_call(attend_kernel, grid=(packs,), in_specs=[SCALAR, SCALAR, pl...  38.4 us
    ppermute x27, waiting for transfers between devices, swap(): return lax.ppermute(block, AXES, [(i, i ^ mask) for i in range(count)])  29.4 us
    ppermute x27, starting transfers between devices, swap(): return lax.ppermute(block, AXES, [(i, i ^ mask) for i in range(count)])  29 us
    pallas_call x1, Pallas kernels, input_grads(): pl.pallas_call(inputs_kernel, grid=(tokens // PACK,), in_specs=[SCALAR] +...  10.4 us
    pallas_call x2, Pallas kernels, combine(): pl.pallas_call(functools.partial(combine_kernel, len(sources), parts, len...  7.09 us
    all_gather x1, waiting for transfers between devices, local(): gb = lax.all_gather(own_b, AXES, axis=0, tiled=True)  5.88 us
  transfers between devices with their start and end apart: 28, of which 14 were waited for; matrix products, arithmetic and copies ran while one was open for 3% of the time, Pallas kernels for 34%

profile of v3, /device:TPU:0, one launch (start us, length us, event | category | flops | bytes accessed | tf_op | source)
XLA Modules:
  0.0 279.1 jit_solution(6909654589638999394)
XLA Ops:
  7.3 1.3 reshape.114.bup_ref
  8.5 1.8 pack.1
  10.4 5.1 %collective-permute-start.2 = (bf16[16,2048]{1,0:T(8,128)(2,1)}, bf16[16,2048]{1,0:T(8,128)(2,1)S(1)}, u32[]{:S(2)}, u32[]{:S(2)}) collective-permute-start(bf16[16,2048]{1,0:T(8,128)(2,1)} %get-tuple-element.79), channel_id=1, source_target_pairs={{0,24},{1,25},{2,26},{3,27},{4,28},{5,29},{6,30},{7,31},{8,16},{9,... | collective-permute-start | bytes 196616 | tf_op jit(solution)/shard_map/ppermute | solution.py:634
  17.0 3.0 %collective-permute-done = bf16[16,2048]{1,0:T(8,128)(2,1)S(1)} collective-permute-done((bf16[16,2048]{1,0:T(8,128)(2,1)}, bf16[16,2048]{1,0:T(8,128)(2,1)S(1)}, u32[]{:S(2)}, u32[]{:S(2)}) %collective-permute-start) | collective-permute-done | bytes 65568 | tf_op jit(solution)/shard_map/ppermute | solution.py:634
  20.0 1.3 collective-permute-done.1
  21.4 1.6 collective-permute-start.3
  22.9 1.5 collective-permute-start.4
  24.9 6.0 %collective-permute-done.3 = bf16[64,2048]{1,0:T(8,128)(2,1)S(1)} collective-permute-done((bf16[64,2048]{1,0:T(8,128)(2,1)S(1)}, bf16[64,2048]{1,0:T(8,128)(2,1)S(1)}, u32[]{:S(2)}, u32[]{:S(2)}) %collective-permute-start.3) | collective-permute-done | bytes 262176 | tf_op jit(solution)/shard_map/ppermute | solution.py:634
  30.9 1.7 collective-permute-done.4
  32.6 5.1 %collective-permute-done.5 = bf16[64,2048]{1,0:T(8,128)(2,1)S(1)} collective-permute-done((bf16[64,2048]{1,0:T(8,128)(2,1)S(1)}, bf16[64,2048]{1,0:T(8,128)(2,1)S(1)}, u32[]{:S(2)}, u32[]{:S(2)}) %collective-permute-start.5) | collective-permute-done | bytes 262176 | tf_op jit(solution)/shard_map/ppermute | solution.py:634
  41.5 38.4 %attend.1 = (bf16[2560,512]{1,0:T(8,128)(2,1)}, bf16[2560,512]{1,0:T(8,128)(2,1)}, bf16[2560,512]{1,0:T(8,128)(2,1)}, bf16[2560,512]{1,0:T(8,128)(2,1)}, bf16[25...) custom-call(s32[1]{0:T(128)} %bitcast.me_ref, ...), custom_call_target="tpu_custom_call" | custom-call | flops 40000000000 | bytes 50000000 | tf_op jit(solution)/shard_map/attend/pallas_call | solution.py:211
  81.6 5.9 %all-gather.2.cloned.1.call-done.gb_ref = bf16[512,6912]{1,0:T(8,128)(2,1)} async-done(((bf16[16,6912]{1,0:T(8,128)(2,1)}), bf16[512,6912]{1,0:T(8,128)(2,1)}) %all-gather.2.cloned.1.call-update) | async-done | bytes 7077904 | tf_op jit(solution)/shard_map/all_gather | solution.py:759
  87.5 81.5 %feed.1 = (bf16[2560,512]{1,0:T(8,128)(2,1)}, f32[2560,512]{1,0:T(8,128)}, bf16[2560,512]{1,0:T(8,128)(2,1)}, bf16[64,7040]{1,0:T(8,128)(2,1)}, bf16[64,7040]{1,...) custom-call(s32[1]{0:T(128)} %bitcast.me_ref, ...), custom_call_target="tpu_custom_call" | custom-call | flops 80000000000 | bytes 40000000 | tf_op jit(solution)/shard_map/feed/pallas_call | solution.py:388
  170.0 1.6 collective-permute-done.8
  171.7 1.5 add_convert_fusion.2.refs_1_
  173.2 1.5 collective-permute-start.11
  176.2 1.6 collective-permute-start.13
  178.9 43.2 %core_back.1 = (bf16[2560,512]{1,0:T(8,128)(2,1)}, bf16[2560,512]{1,0:T(8,128)(2,1)}, bf16[2560,512]{1,0:T(8,128)(2,1)}, bf16[64,2048]{1,0:T(8,128)(2,1)}, bf16[...) custom-call(s32[1]{0:T(128)} %bitcast.me_ref, ...), custom_call_target="tpu_custom_call" | custom-call | flops 49999998976 | bytes 50000000 | tf_op jit(solution)/shard_map/core_back/pallas_call | solution.py:489
  223.1 4.3 %combine.2 = (bf16[16,7040]{1,0:T(8,128)(2,1)}, bf16[16,7040]{1,0:T(8,128)(2,1)}, bf16[16,7040]{1,0:T(8,128)(2,1)}, bf16[16,7040]{1,0:T(8,128)(2,1)}, bf16[64,20...) custom-call(bf16[64,7040]{1,0:T(8,128)(2,1)} %add_convert_fusion.3.r, ...), custom_call_target="tpu_custom_call", output_to_operand_aliasing={{4}: (4, {}), {5}: (5, {}), {6}: (6, {}), {7}: (7, {})} | custom-call | flops 1000000 | bytes 7208960 | tf_op jit(solution)/shard_map/combine/pallas_call | solution.py:667
  227.4 1.4 collective-permute-start.24
  228.8 1.6 collective-permute-start.25
  230.4 1.4 collective-permute-start.26
  233.9 1.4 collective-permute-start.18
  235.4 1.6 collective-permute-start.19
  237.1 5.4 %collective-permute-done.18.refs_1_ = bf16[64,2048]{1,0:T(8,128)(2,1)S(1)} collective-permute-done((bf16[64,2048]{1,0:T(8,128)(2,1)S(1)}, bf16[64,2048]{1,0:T(8,128)(2,1)S(1)}, u32[]{:S(2)}, u32[]{:S(2)}) %collective-permute-start.18) | collective-permute-done | bytes 262176 | tf_op jit(solution)/shard_map/ppermute | solution.py:634
  242.4 1.9 collective-permute-start.20
  244.4 10.4 %input_grads.1.refs_4_ = bf16[2560,512]{1,0:T(8,128)(2,1)} custom-call(s32[1]{0:T(128)} %bitcast.me_ref, bf16[2560,512]{1,0:T(8,128)(2,1)} %get-tuple-element.100.dq_ref, bf16[2560,512]{1,0:T(8,128)(2,1)} %get-tuple-element.101.dk_ref, bf16[2560,512]{1,0:T(8,128)(2,1)} %get-tuple-element.102.dv_ref, f32[2560,512]{1,0:T(8,128)} %get-tuple-element.103.dfirst_ref, ...), custom_call_target="tpu_custom_call" | custom-call | flops 8000000000 | bytes 20000000 | tf_op jit(solution)/shard_map/input_grads/pallas_call | solution.py:515
  256.2 2.8 %combine.3 = (bf16[16,2048]{1,0:T(8,128)(2,1)}, bf16[16,2048]{1,0:T(8,128)(2,1)}, bf16[16,2048]{1,0:T(8,128)(2,1)}, bf16[16,2048]{1,0:T(8,128)(2,1)}) custom-call(bf16[64,2048]{1,0:T(8,128)(2,1)} %add_convert_fusion.7.refs_0_, bf16[64,2048]{1,0:T(8,128)(2,1)} %copy-done.7, bf16[64,2048]{1,0:T(8,128)(2,1)} %copy-done.8, bf16[64,2048]{1,0:T(8,128)(2,1)} %copy-done.9, ...), custom_call_target="tpu_custom_call" | custom-call | flops 1000000 | bytes 2097152 | tf_op jit(solution)/shard_map/combine/pallas_call | solution.py:667
  259.9 1.7 collective-permute-start.22
  261.5 1.9 collective-permute-start.23
  263.9 2.8 %collective-permute-done.22.refs_2_ = bf16[16,2048]{1,0:T(8,128)(2,1)S(1)} collective-permute-done((bf16[16,2048]{1,0:T(8,128)(2,1)}, bf16[16,2048]{1,0:T(8,128)(2,1)S(1)}, u32[]{:S(2)}, u32[]{:S(2)}) %collective-permute-start.22) | collective-permute-done | bytes 65568 | tf_op jit(solution)/shard_map/ppermute | solution.py:634
  268.5 2.2 finish.1
  (115 shorter events, 20.3 us)
Async XLA Ops:
  7.2 30.6 %copy-start.23 = (s32[2560]{0:T(1024)S(1)}, s32[2560]{0:T(1024)}, u32[]{:S(2)}) copy-start(s32[2560]{0:T(1024)} %param.22) | copy-start | bytes 30724
  7.2 31.4 %copy-start.24 = (s32[2560]{0:T(1024)S(1)}, s32[2560]{0:T(1024)}, u32[]{:S(2)}) copy-start(s32[2560]{0:T(1024)} %param.23) | copy-start | bytes 30724
  7.2 80.3 %all-gather.2.cloned.1.call-start = ((), (), s32[]{:S(2)}) async-start(), calls=%async_computation | async-start | bytes 7299072 | tf_op jit(solution)/shard_map/all_gather | solution.py:759
  10.4 10.9 %collective-permute-start.2 = (bf16[16,2048]{1,0:T(8,128)(2,1)}, bf16[16,2048]{1,0:T(8,128)(2,1)S(1)}, u32[]{:S(2)}, u32[]{:S(2)}) collective-permute-start(bf16[16,2048]{1,0:T(8,128)(2,1)} %get-tuple-element.79), channel_id=1, source_target_pairs={{0,24},{1,25},{2,26},{3,27},{4,28},{5,29},{6,30},{7,31},{8,16},{9,... | collective-permute-start | bytes 196616 | tf_op jit(solution)/shard_map/ppermute | solution.py:634
  15.5 5.8 %collective-permute-start.1 = (bf16[16,2048]{1,0:T(8,128)(2,1)}, bf16[16,2048]{1,0:T(8,128)(2,1)S(1)}, u32[]{:S(2)}, u32[]{:S(2)}) collective-permute-start(bf16[16,2048]{1,0:T(8,128)(2,1)} %get-tuple-element.79), channel_id=1, source_target_pairs={{0,16},{1,17},{2,18},{3,19},{4,20},{5,21},{6,22},{7,23},{8,24},{9,... | collective-permute-start | bytes 196616 | tf_op jit(solution)/shard_map/ppermute | solution.py:634
  15.5 4.5 %collective-permute-start = (bf16[16,2048]{1,0:T(8,128)(2,1)}, bf16[16,2048]{1,0:T(8,128)(2,1)S(1)}, u32[]{:S(2)}, u32[]{:S(2)}) collective-permute-start(bf16[16,2048]{1,0:T(8,128)(2,1)} %get-tuple-element.79), channel_id=1, source_target_pairs={{0,8},{1,9},{2,10},{3,11},{4,12},{5,13},{6,14},{7,15},{8,0},{9,1},... | collective-permute-start | bytes 196616 | tf_op jit(solution)/shard_map/ppermute | solution.py:634
  21.4 9.5 %collective-permute-start.3 = (bf16[64,2048]{1,0:T(8,128)(2,1)S(1)}, bf16[64,2048]{1,0:T(8,128)(2,1)S(1)}, u32[]{:S(2)}, u32[]{:S(2)}) collective-permute-start(bf16[64,2048]{1,0:T(8,128)(2,1)S(1)} %get-tuple-element.140), channel_id=1, source_target_pairs={{0,2},{1,3},{2,0},{3,1},{4,6},{5,7},{6,4},{7,5},{8,10},{9,11},{10,... | collective-permute-start | bytes 786440 | tf_op jit(solution)/shard_map/ppermute | solution.py:634
  22.9 9.6 %collective-permute-start.4 = (bf16[64,2048]{1,0:T(8,128)(2,1)S(1)}, bf16[64,2048]{1,0:T(8,128)(2,1)S(1)}, u32[]{:S(2)}, u32[]{:S(2)}) collective-permute-start(bf16[64,2048]{1,0:T(8,128)(2,1)S(1)} %get-tuple-element.140), channel_id=1, source_target_pairs={{0,4},{1,5},{2,6},{3,7},{4,0},{5,1},{6,2},{7,3},{8,12},{9,13},{10,... | collective-permute-start | bytes 786440 | tf_op jit(solution)/shard_map/ppermute | solution.py:634
  24.4 13.3 %collective-permute-start.5 = (bf16[64,2048]{1,0:T(8,128)(2,1)S(1)}, bf16[64,2048]{1,0:T(8,128)(2,1)S(1)}, u32[]{:S(2)}, u32[]{:S(2)}) collective-permute-start(bf16[64,2048]{1,0:T(8,128)(2,1)S(1)} %get-tuple-element.140), channel_id=1, source_target_pairs={{0,6},{1,7},{2,4},{3,5},{4,2},{5,3},{6,0},{7,1},{8,14},{9,15},{10,... | collective-permute-start | bytes 786440 | tf_op jit(solution)/shard_map/ppermute | solution.py:634
  37.7 2.7 collective-permute-start.6
  169.0 2.7 collective-permute-start.8
  169.3 8.5 %collective-permute-start.7 = (bf16[64,7040]{1,0:T(8,128)(2,1)}, bf16[64,7040]{1,0:T(8,128)(2,1)S(1)}, u32[]{:S(2)}, u32[]{:S(2)}) collective-permute-start(bf16[64,7040]{1,0:T(8,128)(2,1)} %get-tuple-element.93), channel_id=1, source_target_pairs={{0,1},{1,0},{2,3},{3,2},{4,5},{5,4},{6,7},{7,6},{8,9},{9,8},{10,11... | collective-permute-start | bytes 2703368 | tf_op jit(solution)/shard_map/ppermute | solution.py:634
  169.5 5.2 %collective-permute-start.9 = (bf16[64,7040]{1,0:T(8,128)(2,1)}, bf16[64,7040]{1,0:T(8,128)(2,1)S(1)}, u32[]{:S(2)}, u32[]{:S(2)}) collective-permute-start(bf16[64,7040]{1,0:T(8,128)(2,1)} %get-tuple-element.97), channel_id=1, source_target_pairs={{0,1},{1,0},{2,3},{3,2},{4,5},{5,4},{6,7},{7,6},{8,9},{9,8},{10,11... | collective-permute-start | bytes 2703368 | tf_op jit(solution)/shard_map/ppermute | solution.py:634
  169.8 6.2 %collective-permute-start.10 = (bf16[64,7040]{1,0:T(8,128)(2,1)}, bf16[64,7040]{1,0:T(8,128)(2,1)S(1)}, u32[]{:S(2)}, u32[]{:S(2)}) collective-permute-start(bf16[64,7040]{1,0:T(8,128)(2,1)} %get-tuple-element.99), channel_id=1, source_target_pairs={{0,1},{1,0},{2,3},{3,2},{4,5},{5,4},{6,7},{7,6},{8,9},{9,8},{10,11... | collective-permute-start | bytes 2703368 | tf_op jit(solution)/shard_map/ppermute | solution.py:634
  173.2 49.0 %collective-permute-start.11 = (bf16[64,7040]{1,0:T(8,128)(2,1)S(1)}, bf16[64,7040]{1,0:T(8,128)(2,1)S(1)}, u32[]{:S(2)}, u32[]{:S(2)}) collective-permute-start(bf16[64,7040]{1,0:T(8,128)(2,1)S(1)} %add_convert_fusion.2.refs_1_), channel_id=1, source_target_pairs={{0,2},{1,3},{2,0},{3,1},{4,6},{5,7},{6,4},{7,5},{8,10},{9,11},{10,... | collective-permute-start | bytes 2703368 | tf_op jit(solution)/shard_map/ppermute | solution.py:634
  174.9 47.3 %collective-permute-start.12 = (bf16[64,7040]{1,0:T(8,128)(2,1)S(1)}, bf16[64,7040]{1,0:T(8,128)(2,1)}, u32[]{:S(2)}, u32[]{:S(2)}) collective-permute-start(bf16[64,7040]{1,0:T(8,128)(2,1)S(1)} %add_convert_fusion.1.refs_2_), channel_id=1, source_target_pairs={{0,4},{1,5},{2,6},{3,7},{4,0},{5,1},{6,2},{7,3},{8,12},{9,13},{10,... | collective-permute-start | bytes 2703368 | tf_op jit(solution)/shard_map/ppermute | solution.py:634
  176.2 46.0 %collective-permute-start.13 = (bf16[64,7040]{1,0:T(8,128)(2,1)S(1)}, bf16[64,7040]{1,0:T(8,128)(2,1)}, u32[]{:S(2)}, u32[]{:S(2)}) collective-permute-start(bf16[64,7040]{1,0:T(8,128)(2,1)S(1)} %add_convert_fusion.refs_3_), channel_id=1, source_target_pairs={{0,6},{1,7},{2,4},{3,5},{4,2},{5,3},{6,0},{7,1},{8,14},{9,15},{10,... | collective-permute-start | bytes 2703368 | tf_op jit(solution)/shard_map/ppermute | solution.py:634
  223.1 13.9 %copy-start.10 = (bf16[64,2048]{1,0:T(8,128)(2,1)S(1)}, bf16[64,2048]{1,0:T(8,128)(2,1)}, u32[]{:S(2)}) copy-start(bf16[64,2048]{1,0:T(8,128)(2,1)} %get-tuple-element.114) | copy-start | bytes 786436
  227.4 4.4 %collective-permute-start.14 = (bf16[64,2048]{1,0:T(8,128)(2,1)}, bf16[64,2048]{1,0:T(8,128)(2,1)S(1)}, u32[]{:S(2)}, u32[]{:S(2)}) collective-permute-start(bf16[64,2048]{1,0:T(8,128)(2,1)} %get-tuple-element.109), channel_id=1, source_target_pairs={{0,1},{1,0},{2,3},{3,2},{4,5},{5,4},{6,7},{7,6},{8,9},{9,8},{10,11... | collective-permute-start | bytes 786440 | tf_op jit(solution)/shard_map/ppermute | solution.py:634
  227.4 34.1 %collective-permute-start.24 = (bf16[16,7040]{1,0:T(8,128)(2,1)}, bf16[16,7040]{1,0:T(8,128)(2,1)S(1)}, u32[]{:S(2)}, u32[]{:S(2)}) collective-permute-start(bf16[16,7040]{1,0:T(8,128)(2,1)} %get-tuple-element.117.refs_5_), channel_id=1, source_target_pairs={{0,8},{1,9},{2,10},{3,11},{4,12},{5,13},{6,14},{7,15},{8,0},{9,1},... | collective-permute-start | bytes 675848 | tf_op jit(solution)/shard_map/ppermute | solution.py:634
  228.8 34.7 %collective-permute-start.25 = (bf16[16,7040]{1,0:T(8,128)(2,1)}, bf16[16,7040]{1,0:T(8,128)(2,1)S(1)}, u32[]{:S(2)}, u32[]{:S(2)}) collective-permute-start(bf16[16,7040]{1,0:T(8,128)(2,1)} %get-tuple-element.118.refs_6_), channel_id=1, source_target_pairs={{0,16},{1,17},{2,18},{3,19},{4,20},{5,21},{6,22},{7,23},{8,24},{9,... | collective-permute-start | bytes 675848 | tf_op jit(solution)/shard_map/ppermute | solution.py:634
  230.4 33.1 %collective-permute-start.26 = (bf16[16,7040]{1,0:T(8,128)(2,1)}, bf16[16,7040]{1,0:T(8,128)(2,1)S(1)}, u32[]{:S(2)}, u32[]{:S(2)}) collective-permute-start(bf16[16,7040]{1,0:T(8,128)(2,1)} %get-tuple-element.119.refs_7_), channel_id=1, source_target_pairs={{0,24},{1,25},{2,26},{3,27},{4,28},{5,29},{6,30},{7,31},{8,16},{9,... | collective-permute-start | bytes 675848 | tf_op jit(solution)/shard_map/ppermute | solution.py:634
  231.8 1.7 collective-permute-start.15
  231.8 2.1 collective-permute-start.16
  233.5 1.8 collective-permute-start.17
  233.9 8.5 %collective-permute-start.18 = (bf16[64,2048]{1,0:T(8,128)(2,1)S(1)}, bf16[64,2048]{1,0:T(8,128)(2,1)S(1)}, u32[]{:S(2)}, u32[]{:S(2)}) collective-permute-start(bf16[64,2048]{1,0:T(8,128)(2,1)S(1)} %add_convert_fusion.6.refs_1_), channel_id=1, source_target_pairs={{0,2},{1,3},{2,0},{3,1},{4,6},{5,7},{6,4},{7,5},{8,10},{9,11},{10,... | collective-permute-start | bytes 786440 | tf_op jit(solution)/shard_map/ppermute | solution.py:634
  235.4 19.4 %collective-permute-start.19 = (bf16[64,2048]{1,0:T(8,128)(2,1)S(1)}, bf16[64,2048]{1,0:T(8,128)(2,1)S(1)}, u32[]{:S(2)}, u32[]{:S(2)}) collective-permute-start(bf16[64,2048]{1,0:T(8,128)(2,1)S(1)} %add_convert_fusion.5.refs_2_), channel_id=1, source_target_pairs={{0,4},{1,5},{2,6},{3,7},{4,0},{5,1},{6,2},{7,3},{8,12},{9,13},{10,... | collective-permute-start | bytes 786440 | tf_op jit(solution)/shard_map/ppermute | solution.py:634
  242.4 12.4 %copy-start.7 = (bf16[64,2048]{1,0:T(8,128)(2,1)}, bf16[64,2048]{1,0:T(8,128)(2,1)S(1)}, u32[]{:S(2)}) copy-start(bf16[64,2048]{1,0:T(8,128)(2,1)S(1)} %collective-permute-done.18.refs_1_) | copy-start | bytes 786436
  242.4 12.4 %collective-permute-start.20 = (bf16[64,2048]{1,0:T(8,128)(2,1)S(1)}, bf16[64,2048]{1,0:T(8,128)(2,1)S(1)}, u32[]{:S(2)}, u32[]{:S(2)}) collective-permute-start(bf16[64,2048]{1,0:T(8,128)(2,1)S(1)} %add_convert_fusion.4.refs_3_), channel_id=1, source_target_pairs={{0,6},{1,7},{2,4},{3,5},{4,2},{5,3},{6,0},{7,1},{8,14},{9,15},{10,... | collective-permute-start | bytes 786440 | tf_op jit(solution)/shard_map/ppermute | solution.py:634
  259.1 4.8 %collective-permute-start.21 = (bf16[16,2048]{1,0:T(8,128)(2,1)}, bf16[16,2048]{1,0:T(8,128)(2,1)S(1)}, u32[]{:S(2)}, u32[]{:S(2)}) collective-permute-start(bf16[16,2048]{1,0:T(8,128)(2,1)} %get-tuple-element.121), channel_id=1, source_target_pairs={{0,8},{1,9},{2,10},{3,11},{4,12},{5,13},{6,14},{7,15},{8,0},{9,1},... | collective-permute-start | bytes 196616 | tf_op jit(solution)/shard_map/ppermute | solution.py:634
  259.9 6.8 %collective-permute-start.22 = (bf16[16,2048]{1,0:T(8,128)(2,1)}, bf16[16,2048]{1,0:T(8,128)(2,1)S(1)}, u32[]{:S(2)}, u32[]{:S(2)}) collective-permute-start(bf16[16,2048]{1,0:T(8,128)(2,1)} %get-tuple-element.122), channel_id=1, source_target_pairs={{0,16},{1,17},{2,18},{3,19},{4,20},{5,21},{6,22},{7,23},{8,24},{9,... | collective-permute-start | bytes 196616 | tf_op jit(solution)/shard_map/ppermute | solution.py:634
  261.5 6.4 %collective-permute-start.23 = (bf16[16,2048]{1,0:T(8,128)(2,1)}, bf16[16,2048]{1,0:T(8,128)(2,1)S(1)}, u32[]{:S(2)}, u32[]{:S(2)}) collective-permute-start(bf16[16,2048]{1,0:T(8,128)(2,1)} %get-tuple-element.123), channel_id=1, source_target_pairs={{0,24},{1,25},{2,26},{3,27},{4,28},{5,29},{6,30},{7,31},{8,16},{9,... | collective-permute-start | bytes 196616 | tf_op jit(solution)/shard_map/ppermute | solution.py:634
  (23 other events, 110.0 us)
Sparse Core Ops, SparseCore 0:
  11.0 76.4 all-gather.1

commit v4 on v3

--- a/solution.py
+++ b/solution.py
@@ -247,18 +247,25 @@
 GELU_B = 0.044715
 
 
-def feed_kernel(narrow, own_rows, me_ref, x_ref, attn_ref, cot_ref, pad_ref, gb_ref, vec_ref, bup_ref, out_ref, dfirst_ref, dattn_ref, *refs):
+def feed_kernel(narrow, own_rows, me_ref, x_ref, attn_ref, cot_ref, pad_ref, gb_hbm, vec_ref, bup_ref, out_ref, dfirst_ref, dattn_ref, *refs):
     pieces, scratch = refs[: 2 * PIECES], refs[2 * PIECES :]
-    act_ref, slope_ref, up_acc, down_acc, wo_acc, wo_low, side_ref, gv_ref, gbu_ref, sem = scratch
+    gb_ref, act_ref, slope_ref, up_acc, down_acc, wo_acc, wo_low, side_ref, gv_ref, gbu_ref, sem, load_sems = scratch
+    loads = [
+        pltpu.make_async_copy(gb_hbm.at[:, at : at + size], gb_ref.at[:, at : at + size], load_sems.at[n])
+        for n, (at, size) in enumerate(((0, D), (D, FF), (D + FF, FF)))
+    ]
     step = pl.program_id(0)
 
     @pl.when(step == 0)
     def _():
+        for copy in loads:
+            copy.start()
         up_acc[...] = jnp.zeros_like(up_acc)
         down_acc[...] = jnp.zeros_like(down_acc)
         wo_acc[...] = jnp.zeros_like(wo_acc)
         gv_ref[...] = jnp.zeros_like(gv_ref)
         gbu_ref[...] = jnp.zeros_like(gbu_ref)
+        loads[0].wait()
 
     gain_one, gain_two = vec_ref[3:4], vec_ref[6:7]
     keep_all = jnp.transpose(jnp.broadcast_to(pad_ref[...].astype(F32), (8, TILE)))[:, 0:1]
@@ -333,7 +340,18 @@
             down_acc[:, cols] += nn(ff_t, act_ref[:, cols])
             up_acc[:, cols] += nn(low_t, slope_ref[:, cols])
 
-    enter(0); ahead(0); turn(0); behind(0); leave(0); weights()
+    enter(0)
+
+    @pl.when(step == 0)
+    def _():
+        loads[1].wait()
+        loads[2].wait()
+
+    ahead(0)
+    turn(0)
+    behind(0)
+    leave(0)
+    weights()
     wo_acc[...] += nn(joined(d_branch_t), attn_ref[...])
 
     @pl.when(step == pl.num_programs(0) - 1)
@@ -394,7 +412,7 @@
             rows_of(TILE, D),
             rows_of(TILE, D),
             pl.BlockSpec((1, TILE), lambda i: (0, i)),
-            whole((D, WB)),
+            LOOSE,
             whole((128, D)),
             whole((1, FF)),
         ],
@@ -406,6 +424,7 @@
         ]
         + [jax.ShapeDtypeStruct((PIECE, WB + side), BF)] * (2 * PIECES),
         scratch_shapes=[
+            pltpu.VMEM((D, WB), BF),
             pltpu.VMEM((TILE, FF), BF),
             pltpu.VMEM((TILE, FF), BF),
             pltpu.VMEM((D, FF), F32),
@@ -416,6 +435,7 @@
             pltpu.VMEM((8, D), F32),
             pltpu.VMEM((8, FF + 128), F32),
             pltpu.SemaphoreType.DMA,
+            pltpu.SemaphoreType.DMA((3,)),
         ],
         compiler_params=pltpu.CompilerParams(vmem_limit_bytes=VMEM),
         cost_estimate=pl.CostEstimate(flops=80 * 10**9, bytes_accessed=40 * 10**6, transcendentals=0),
@@ -431,11 +451,15 @@
 
 
 def core_kernel(me_ref, starts_ref, q_ref, k_ref, v_ref, dattn_ref, pt_ref, x_ref, mix_ref, picks_ref, al_ref, ar_ref, *refs):
-    dq_ref, dk_ref, dv_ref, *pieces, acc, ga_ref, gw_ref, sem = refs[-(3 + 2 * PIECES + 4) :]
+    dq_ref, dk_ref, dv_ref, *pieces, acc, ga_ref, gw_ref, sem, load_sem = refs[-(3 + 2 * PIECES + 5) :]
     step = pl.program_id(0)
+
+    loads = block_loads(me_ref, (al_ref, ar_ref), ga_ref, load_sem)
 
     @pl.when(step == 0)
     def _():
+        for copy in loads:
+            copy.start()
         acc[...] = jnp.zeros_like(acc)
 
     for ref in (dq_ref, dk_ref, dv_ref):
@@ -470,7 +494,8 @@
 
     @pl.when(step == pl.num_programs(0) - 1)
     def _():
-        load_blocks(me_ref, (al_ref, ar_ref), ga_ref, sem)
+        for copy in loads:
+            copy.wait()
         gw_ref[:, 0 : 3 * D] = acc[:, 0 : 3 * D].astype(BF)
         table = tn(ga_ref[:, 0:D], acc[:, 3 * D : 3 * D + PLACES].astype(BF))
         table = table + tn(ga_ref[:, D : 2 * D], acc[:, 3 * D + PLACES : 3 * D + 2 * PLACES].astype(BF))
@@ -492,7 +517,13 @@
         in_specs=[SCALAR, SCALAR] + [flat] * 4 + [probs, flat, flat, rows_of(PACK, PLACES)] + [LOOSE] * (2 + len(after)),
         out_specs=[flat] * 3 + [LOOSE] * (2 * PIECES),
         out_shape=[jax.ShapeDtypeStruct((tokens, D), BF)] * 3 + [jax.ShapeDtypeStruct((PIECE, WA), BF)] * (2 * PIECES),
-        scratch_shapes=[pltpu.VMEM((D, ACC), F32), pltpu.VMEM((D, WA), BF), pltpu.VMEM((D, WA), BF), pltpu.SemaphoreType.DMA],
+        scratch_shapes=[
+            pltpu.VMEM((D, ACC), F32),
+            pltpu.VMEM((D, WA), BF),
+            pltpu.VMEM((D, WA), BF),
+            pltpu.SemaphoreType.DMA,
+            pltpu.SemaphoreType.DMA,
+        ],
         compiler_params=pltpu.CompilerParams(vmem_limit_bytes=VMEM),
         cost_estimate=pl.CostEstimate(flops=50 * 10**9, bytes_accessed=50 * 10**6, transcendentals=0),
         name="core_back",
@@ -500,7 +531,7 @@
 
 
 def inputs_kernel(me_ref, dq_ref, dk_ref, dv_ref, dfirst_ref, al_ref, ar_ref, *refs):
-    out_ref, ga_ref, sem = refs[-3:]
+    out_ref, _, ga_ref, sem = refs[-4:]
 
     @pl.when(pl.program_id(0) == 0)
     def _():
@@ -510,19 +541,20 @@
     out_ref[...] = (dfirst_ref[...] + d_mixed + nn(dv_ref[...], ga_ref[:, 2 * D : 3 * D])).astype(BF)
 
 
-def input_grads(where, flat, d_first, halves, after):
+def input_grads(where, flat, d_first, halves, after, through):
     tokens = d_first.shape[0]
     return pl.pallas_call(
         inputs_kernel,
         grid=(tokens // PACK,),
-        in_specs=[SCALAR] + [rows_of(PACK, D)] * 4 + [LOOSE] * (2 + len(after)),
-        out_specs=rows_of(PACK, D),
-        out_shape=jax.ShapeDtypeStruct((tokens, D), BF),
+        in_specs=[SCALAR] + [rows_of(PACK, D)] * 4 + [LOOSE] * (3 + len(after)),
+        out_specs=[rows_of(PACK, D), LOOSE],
+        out_shape=[jax.ShapeDtypeStruct((tokens, D), BF), jax.ShapeDtypeStruct(through.shape, through.dtype)],
+        input_output_aliases={7 + len(after): 1},
         scratch_shapes=[pltpu.VMEM((D, WA), BF), pltpu.SemaphoreType.DMA],
         compiler_params=pltpu.CompilerParams(vmem_limit_bytes=VMEM),
         cost_estimate=pl.CostEstimate(flops=8 * 10**9, bytes_accessed=20 * 10**6, transcendentals=0),
         name="input_grads",
-    )(where, *flat, d_first, *halves, *after)
+    )(where, *flat, d_first, *halves, *after, through)
 
 
 def finish_kernel(count, *refs):
@@ -649,14 +681,12 @@
 
 def combine_kernel(count, parts, loose, *refs):
     sources, outs = refs[:count], refs[count + loose : count + loose + parts]
-    total = sources[0][...].astype(F32)
-    for source in sources[1:]:
-        total = total + source[...].astype(F32)
+    rows = outs[0].shape[0]
     for n, out in enumerate(outs):
-
-        @pl.when(pl.program_id(0) == n)
-        def _(out=out):
-            out[...] = total.astype(BF)
+        total = sources[0][n * rows : (n + 1) * rows].astype(F32)
+        for source in sources[1:]:
+            total = total + source[n * rows : (n + 1) * rows].astype(F32)
+        out[...] = total.astype(BF)
 
 
 def combine(sources, parts, after=(), through=()):
@@ -666,9 +696,8 @@
         return added(sources, parts) + list(through)
     return list(pl.pallas_call(
         functools.partial(combine_kernel, len(sources), parts, len(after) + len(through)),
-        grid=(parts,),
-        in_specs=[rows_of(rows, width)] * len(sources) + [LOOSE] * (len(after) + len(through)),
-        out_specs=[pl.BlockSpec((rows, width), lambda i: (0, 0), pipeline_mode=pl.Buffered(1))] * parts + [LOOSE] * len(through),
+        in_specs=[pl.BlockSpec(memory_space=pltpu.VMEM)] * len(sources) + [LOOSE] * (len(after) + len(through)),
+        out_specs=[pl.BlockSpec(memory_space=pltpu.VMEM)] * parts + [LOOSE] * len(through),
         out_shape=[jax.ShapeDtypeStruct((rows, width), BF)] * parts + [jax.ShapeDtypeStruct(array.shape, array.dtype) for array in through],
         input_output_aliases={len(sources) + len(after) + n: parts + n for n in range(len(through))},
         compiler_params=pltpu.CompilerParams(vmem_limit_bytes=VMEM),
@@ -772,7 +801,8 @@
     grads_a = [*grads_a[:PIECES], *parts_b[next_parts:]]
     parts_b = parts_b[:next_parts]
     parts_a = scatter_core(grads_a, count)
-    input_grad = input_grads(where, back[:3], d_first, a_halves, parts_a + parts_b)
+    input_grad, held = input_grads(where, back[:3], d_first, a_halves, parts_a + parts_b[2:], parts_b[1])
+    parts_b = [parts_b[0], held, *parts_b[2:]]
     parts_a = combine(exchange(parts_a, groups[1], count), 1 << len(groups[2]), [input_grad])
     for at in range(2, len(groups) - 1):
         next_parts = 1 << len(groups[at + 1])

time: 280 us -> 271 us (0.968)
  Pallas kernels: 185 us -> 181 us
  waiting for transfers between devices: 35.3 us -> 31.9 us
    ppermute x27, waiting for transfers between devices: 29.4 us -> 25.7 us  [swap(): return lax.ppermute(block, AXES, [(i, i ^ mask) for i in range(count)])]
  transfers between devices with their start and end apart: 28 -> 28, of which waited for: 14 -> 13; matrix products, arithmetic and copies ran while one was open for 3% -> 3% of each run, Pallas kernels for 34% -> 34%
where the time goes in v4:
time: 271 us; the launch traced here: 270 us
  Pallas kernels  181 us (67%)
  waiting for transfers between devices  31.9 us (12%)
  starting transfers between devices  27.2 us (10%)
  between operations  14.5 us (5%)
  local copies, waits for them, and re-layouts  10.7 us (4%)
  other arithmetic  4.22 us (2%)
    pallas_call x1, Pallas kernels, feed(): pl.pallas_call(functools.partial(feed_kernel, narrow, own_rows), grid=(to...  81.8 us
    pallas_call x1, Pallas kernels, core_back(): pl.pallas_call(core_kernel, grid=(tokens // PACK,), in_specs=[SCALAR, SCA...  42 us
    pallas_call x1, Pallas kernels, attend(): pl.pallas_call(attend_kernel, grid=(packs,), in_specs=[SCALAR, SCALAR, pl...  38.1 us
    ppermute x27, starting transfers between devices, swap(): return lax.ppermute(block, AXES, [(i, i ^ mask) for i in range(count)])  27.1 us
    ppermute x27, waiting for transfers between devices, swap(): return lax.ppermute(block, AXES, [(i, i ^ mask) for i in range(count)])  25.7 us
    pallas_call x1, Pallas kernels, input_grads(): pl.pallas_call(inputs_kernel, grid=(tokens // PACK,), in_specs=[SCALAR] +...  10.4 us
    all_gather x1, waiting for transfers between devices, local(): gb = lax.all_gather(own_b, AXES, axis=0, tiled=True)  6.24 us
  transfers between devices with their start and end apart: 28, of which 13 were waited for; matrix products, arithmetic and copies ran while one was open for 3% of the time, Pallas kernels for 34%

profile of v4, /device:TPU:0, one launch (start us, length us, event | category | flops | bytes accessed | tf_op | source)
XLA Modules:
  0.0 270.0 jit_solution(7463533304439337474)
XLA Ops:
  7.3 1.3 reshape.114.bup_ref
  8.5 1.8 pack.1
  10.4 5.1 %collective-permute-start.2 = (bf16[16,2048]{1,0:T(8,128)(2,1)}, bf16[16,2048]{1,0:T(8,128)(2,1)S(1)}, u32[]{:S(2)}, u32[]{:S(2)}) collective-permute-start(bf16[16,2048]{1,0:T(8,128)(2,1)} %get-tuple-element.81), channel_id=1, source_target_pairs={{0,24},{1,25},{2,26},{3,27},{4,28},{5,29},{6,30},{7,31},{8,16},{9,... | collective-permute-start | bytes 196616 | tf_op jit(solution)/shard_map/ppermute | solution.py:666
  17.0 3.0 %collective-permute-done = bf16[16,2048]{1,0:T(8,128)(2,1)S(1)} collective-permute-done((bf16[16,2048]{1,0:T(8,128)(2,1)}, bf16[16,2048]{1,0:T(8,128)(2,1)S(1)}, u32[]{:S(2)}, u32[]{:S(2)}) %collective-permute-start) | collective-permute-done | bytes 65568 | tf_op jit(solution)/shard_map/ppermute | solution.py:666
  20.0 1.3 collective-permute-done.1
  21.4 1.6 collective-permute-start.3
  22.9 1.5 collective-permute-start.4
  24.9 6.0 %collective-permute-done.3 = bf16[64,2048]{1,0:T(8,128)(2,1)S(1)} collective-permute-done((bf16[64,2048]{1,0:T(8,128)(2,1)S(1)}, bf16[64,2048]{1,0:T(8,128)(2,1)S(1)}, u32[]{:S(2)}, u32[]{:S(2)}) %collective-permute-start.3) | collective-permute-done | bytes 262176 | tf_op jit(solution)/shard_map/ppermute | solution.py:666
  30.9 1.7 collective-permute-done.4
  32.6 5.1 %collective-permute-done.5 = bf16[64,2048]{1,0:T(8,128)(2,1)S(1)} collective-permute-done((bf16[64,2048]{1,0:T(8,128)(2,1)S(1)}, bf16[64,2048]{1,0:T(8,128)(2,1)S(1)}, u32[]{:S(2)}, u32[]{:S(2)}) %collective-permute-start.5) | collective-permute-done | bytes 262176 | tf_op jit(solution)/shard_map/ppermute | solution.py:666
  41.4 38.1 %attend.1 = (bf16[2560,512]{1,0:T(8,128)(2,1)}, bf16[2560,512]{1,0:T(8,128)(2,1)}, bf16[2560,512]{1,0:T(8,128)(2,1)}, bf16[2560,512]{1,0:T(8,128)(2,1)}, bf16[25...) custom-call(s32[1]{0:T(128)} %bitcast.me_ref, ...), custom_call_target="tpu_custom_call" | custom-call | flops 40000000000 | bytes 50000000 | tf_op jit(solution)/shard_map/attend/pallas_call | solution.py:211
  81.2 6.2 %all-gather.2.cloned.1.call-done.gb_hbm = bf16[512,6912]{1,0:T(8,128)(2,1)} async-done(((bf16[16,6912]{1,0:T(8,128)(2,1)}), bf16[512,6912]{1,0:T(8,128)(2,1)}) %all-gather.2.cloned.1.call-update) | async-done | bytes 7077904 | tf_op jit(solution)/shard_map/all_gather | solution.py:788
  87.5 81.8 %feed.1 = (bf16[2560,512]{1,0:T(8,128)(2,1)}, f32[2560,512]{1,0:T(8,128)}, bf16[2560,512]{1,0:T(8,128)(2,1)}, bf16[64,7040]{1,0:T(8,128)(2,1)}, bf16[64,7040]{1,...) custom-call(s32[1]{0:T(128)} %bitcast.me_ref, ...), custom_call_target="tpu_custom_call" | custom-call | flops 80000000000 | bytes 40000000 | tf_op jit(solution)/shard_map/feed/pallas_call | solution.py:406
  170.4 1.6 collective-permute-done.8
  172.0 1.5 add_convert_fusion.2.refs_1_
  173.5 1.5 collective-permute-start.11
  176.5 1.6 collective-permute-start.13
  178.1 1.1 add_convert_fusion.3.refs_0_
  179.2 42.0 %core_back.1 = (bf16[2560,512]{1,0:T(8,128)(2,1)}, bf16[2560,512]{1,0:T(8,128)(2,1)}, bf16[2560,512]{1,0:T(8,128)(2,1)}, bf16[64,2048]{1,0:T(8,128)(2,1)}, bf16[...) custom-call(s32[1]{0:T(128)} %bitcast.me_ref, ...), custom_call_target="tpu_custom_call" | custom-call | flops 49999998976 | bytes 50000000 | tf_op jit(solution)/shard_map/core_back/pallas_call | solution.py:514
  222.2 3.2 %combine.2 = (bf16[16,7040]{1,0:T(8,128)(2,1)}, bf16[16,7040]{1,0:T(8,128)(2,1)}, bf16[16,7040]{1,0:T(8,128)(2,1)}, bf16[16,7040]{1,0:T(8,128)(2,1)}, bf16[64,20...) custom-call(bf16[64,7040]{1,0:T(8,128)(2,1)} %add_convert_fusion.3.r, ...), custom_call_target="tpu_custom_call", output_to_operand_aliasing={{4}: (4, {}), {5}: (5, {}), {6}: (6, {}), {7}: (7, {})} | custom-call | flops 1000000 | bytes 7208960 | tf_op jit(solution)/shard_map/combine/pallas_call | solution.py:697
  225.4 2.2 collective-permute-start.25
  227.6 1.7 collective-permute-start.26
  229.9 1.5 collective-permute-done.16
  232.5 1.6 collective-permute-start.19
  234.2 1.1 collective-permute-start.20
  236.1 10.4 %input_grads.1 = (bf16[2560,512]{1,0:T(8,128)(2,1)}, bf16[16,7040]{1,0:T(8,128)(2,1)}) custom-call(s32[1]{0:T(128)} %bitcast.me_ref, bf16[2560,512]{1,0:T(8,128)(2,1)} %get-tuple-element.102.dq_ref, bf16[2560,512]{1,0:T(8,128)(2,1)} %get-tuple-element.103.dk_ref, bf16[2560,512]{1,0:T(8,128)(2,1)} %get-tuple-element.104.dv_ref, ...), custom_call_target="tpu_custom_call", output_to_operand_aliasing={{1}: (13, {})} | custom-call | flops 8000000000 | bytes 20000000 | tf_op jit(solution)/shard_map/input_grads/pallas_call | solution.py:546
  247.5 1.9 combine.3
  249.4 1.9 collective-permute-start.21
  252.1 1.7 collective-permute-start.23
  253.8 1.1 collective-permute-done.24.refs_5_
  255.8 2.9 %collective-permute-done.22.refs_2_ = bf16[16,2048]{1,0:T(8,128)(2,1)S(1)} collective-permute-done((bf16[16,2048]{1,0:T(8,128)(2,1)}, bf16[16,2048]{1,0:T(8,128)(2,1)S(1)}, u32[]{:S(2)}, u32[]{:S(2)}) %collective-permute-start.22) | collective-permute-done | bytes 65568 | tf_op jit(solution)/shard_map/ppermute | solution.py:666
  259.4 2.2 finish.1
  (115 shorter events, 18.2 us)
Async XLA Ops:
  7.2 30.6 %copy-start.23 = (s32[2560]{0:T(1024)S(1)}, s32[2560]{0:T(1024)}, u32[]{:S(2)}) copy-start(s32[2560]{0:T(1024)} %param.22) | copy-start | bytes 30724
  7.2 31.4 %copy-start.24 = (s32[2560]{0:T(1024)S(1)}, s32[2560]{0:T(1024)}, u32[]{:S(2)}) copy-start(s32[2560]{0:T(1024)} %param.23) | copy-start | bytes 30724
  7.2 80.3 %all-gather.2.cloned.1.call-start = ((), (), s32[]{:S(2)}) async-start(), calls=%async_computation | async-start | bytes 7299072 | tf_op jit(solution)/shard_map/all_gather | solution.py:788
  10.4 10.9 %collective-permute-start.2 = (bf16[16,2048]{1,0:T(8,128)(2,1)}, bf16[16,2048]{1,0:T(8,128)(2,1)S(1)}, u32[]{:S(2)}, u32[]{:S(2)}) collective-permute-start(bf16[16,2048]{1,0:T(8,128)(2,1)} %get-tuple-element.81), channel_id=1, source_target_pairs={{0,24},{1,25},{2,26},{3,27},{4,28},{5,29},{6,30},{7,31},{8,16},{9,... | collective-permute-start | bytes 196616 | tf_op jit(solution)/shard_map/ppermute | solution.py:666
  15.5 5.8 %collective-permute-start.1 = (bf16[16,2048]{1,0:T(8,128)(2,1)}, bf16[16,2048]{1,0:T(8,128)(2,1)S(1)}, u32[]{:S(2)}, u32[]{:S(2)}) collective-permute-start(bf16[16,2048]{1,0:T(8,128)(2,1)} %get-tuple-element.81), channel_id=1, source_target_pairs={{0,16},{1,17},{2,18},{3,19},{4,20},{5,21},{6,22},{7,23},{8,24},{9,... | collective-permute-start | bytes 196616 | tf_op jit(solution)/shard_map/ppermute | solution.py:666
  15.5 4.5 %collective-permute-start = (bf16[16,2048]{1,0:T(8,128)(2,1)}, bf16[16,2048]{1,0:T(8,128)(2,1)S(1)}, u32[]{:S(2)}, u32[]{:S(2)}) collective-permute-start(bf16[16,2048]{1,0:T(8,128)(2,1)} %get-tuple-element.81), channel_id=1, source_target_pairs={{0,8},{1,9},{2,10},{3,11},{4,12},{5,13},{6,14},{7,15},{8,0},{9,1},... | collective-permute-start | bytes 196616 | tf_op jit(solution)/shard_map/ppermute | solution.py:666
  21.4 9.5 %collective-permute-start.3 = (bf16[64,2048]{1,0:T(8,128)(2,1)S(1)}, bf16[64,2048]{1,0:T(8,128)(2,1)S(1)}, u32[]{:S(2)}, u32[]{:S(2)}) collective-permute-start(bf16[64,2048]{1,0:T(8,128)(2,1)S(1)} %get-tuple-element.144), channel_id=1, source_target_pairs={{0,2},{1,3},{2,0},{3,1},{4,6},{5,7},{6,4},{7,5},{8,10},{9,11},{10,... | collective-permute-start | bytes 786440 | tf_op jit(solution)/shard_map/ppermute | solution.py:666
  22.9 9.6 %collective-permute-start.4 = (bf16[64,2048]{1,0:T(8,128)(2,1)S(1)}, bf16[64,2048]{1,0:T(8,128)(2,1)S(1)}, u32[]{:S(2)}, u32[]{:S(2)}) collective-permute-start(bf16[64,2048]{1,0:T(8,128)(2,1)S(1)} %get-tuple-element.144), channel_id=1, source_target_pairs={{0,4},{1,5},{2,6},{3,7},{4,0},{5,1},{6,2},{7,3},{8,12},{9,13},{10,... | collective-permute-start | bytes 786440 | tf_op jit(solution)/shard_map/ppermute | solution.py:666
  24.4 13.3 %collective-permute-start.5 = (bf16[64,2048]{1,0:T(8,128)(2,1)S(1)}, bf16[64,2048]{1,0:T(8,128)(2,1)S(1)}, u32[]{:S(2)}, u32[]{:S(2)}) collective-permute-start(bf16[64,2048]{1,0:T(8,128)(2,1)S(1)} %get-tuple-element.144), channel_id=1, source_target_pairs={{0,6},{1,7},{2,4},{3,5},{4,2},{5,3},{6,0},{7,1},{8,14},{9,15},{10,... | collective-permute-start | bytes 786440 | tf_op jit(solution)/shard_map/ppermute | solution.py:666
  37.7 2.7 %collective-permute-start.6 = (bf16[256,2048]{1,0:T(8,128)(2,1)S(1)}, bf16[256,2048]{1,0:T(8,128)(2,1)S(1)}, u32[]{:S(2)}, u32[]{:S(2)}) collective-permute-start(bf16[256,2048]{1,0:T(8,128)(2,1)S(1)} %constant_dynamic-update-slice_fusion.4.al_ref), channel_id=1, source_target_pairs={{0,1},{1,0},{2,3},{3,2},{4,5},{5,4},{6,7},{7,6},{8,9},{9,8},{10,11... | collective-permute-start | bytes 3145736 | tf_op jit(solution)/shard_map/ppermute | solution.py:666
  169.3 2.7 %collective-permute-start.8 = (bf16[64,7040]{1,0:T(8,128)(2,1)}, bf16[64,7040]{1,0:T(8,128)(2,1)S(1)}, u32[]{:S(2)}, u32[]{:S(2)}) collective-permute-start(bf16[64,7040]{1,0:T(8,128)(2,1)} %get-tuple-element.97), channel_id=1, source_target_pairs={{0,1},{1,0},{2,3},{3,2},{4,5},{5,4},{6,7},{7,6},{8,9},{9,8},{10,11... | collective-permute-start | bytes 2703368 | tf_op jit(solution)/shard_map/ppermute | solution.py:666
  169.6 8.5 %collective-permute-start.7 = (bf16[64,7040]{1,0:T(8,128)(2,1)}, bf16[64,7040]{1,0:T(8,128)(2,1)S(1)}, u32[]{:S(2)}, u32[]{:S(2)}) collective-permute-start(bf16[64,7040]{1,0:T(8,128)(2,1)} %get-tuple-element.95), channel_id=1, source_target_pairs={{0,1},{1,0},{2,3},{3,2},{4,5},{5,4},{6,7},{7,6},{8,9},{9,8},{10,11... | collective-permute-start | bytes 2703368 | tf_op jit(solution)/shard_map/ppermute | solution.py:666
  169.8 5.2 %collective-permute-start.9 = (bf16[64,7040]{1,0:T(8,128)(2,1)}, bf16[64,7040]{1,0:T(8,128)(2,1)S(1)}, u32[]{:S(2)}, u32[]{:S(2)}) collective-permute-start(bf16[64,7040]{1,0:T(8,128)(2,1)} %get-tuple-element.99), channel_id=1, source_target_pairs={{0,1},{1,0},{2,3},{3,2},{4,5},{5,4},{6,7},{7,6},{8,9},{9,8},{10,11... | collective-permute-start | bytes 2703368 | tf_op jit(solution)/shard_map/ppermute | solution.py:666
  170.1 6.2 %collective-permute-start.10 = (bf16[64,7040]{1,0:T(8,128)(2,1)}, bf16[64,7040]{1,0:T(8,128)(2,1)S(1)}, u32[]{:S(2)}, u32[]{:S(2)}) collective-permute-start(bf16[64,7040]{1,0:T(8,128)(2,1)} %get-tuple-element.101), channel_id=1, source_target_pairs={{0,1},{1,0},{2,3},{3,2},{4,5},{5,4},{6,7},{7,6},{8,9},{9,8},{10,11... | collective-permute-start | bytes 2703368 | tf_op jit(solution)/shard_map/ppermute | solution.py:666
  173.5 47.8 %collective-permute-start.11 = (bf16[64,7040]{1,0:T(8,128)(2,1)S(1)}, bf16[64,7040]{1,0:T(8,128)(2,1)S(1)}, u32[]{:S(2)}, u32[]{:S(2)}) collective-permute-start(bf16[64,7040]{1,0:T(8,128)(2,1)S(1)} %add_convert_fusion.2.refs_1_), channel_id=1, source_target_pairs={{0,2},{1,3},{2,0},{3,1},{4,6},{5,7},{6,4},{7,5},{8,10},{9,11},{10,... | collective-permute-start | bytes 2703368 | tf_op jit(solution)/shard_map/ppermute | solution.py:666
  175.2 46.0 %collective-permute-start.12 = (bf16[64,7040]{1,0:T(8,128)(2,1)S(1)}, bf16[64,7040]{1,0:T(8,128)(2,1)}, u32[]{:S(2)}, u32[]{:S(2)}) collective-permute-start(bf16[64,7040]{1,0:T(8,128)(2,1)S(1)} %add_convert_fusion.1.refs_2_), channel_id=1, source_target_pairs={{0,4},{1,5},{2,6},{3,7},{4,0},{5,1},{6,2},{7,3},{8,12},{9,13},{10,... | collective-permute-start | bytes 2703368 | tf_op jit(solution)/shard_map/ppermute | solution.py:666
  176.5 44.8 %collective-permute-start.13 = (bf16[64,7040]{1,0:T(8,128)(2,1)S(1)}, bf16[64,7040]{1,0:T(8,128)(2,1)}, u32[]{:S(2)}, u32[]{:S(2)}) collective-permute-start(bf16[64,7040]{1,0:T(8,128)(2,1)S(1)} %add_convert_fusion.refs_3_), channel_id=1, source_target_pairs={{0,6},{1,7},{2,4},{3,5},{4,2},{5,3},{6,0},{7,1},{8,14},{9,15},{10,... | collective-permute-start | bytes 2703368 | tf_op jit(solution)/shard_map/ppermute | solution.py:666
  222.2 11.9 %copy-start.11 = (bf16[64,2048]{1,0:T(8,128)(2,1)S(1)}, bf16[64,2048]{1,0:T(8,128)(2,1)}, u32[]{:S(2)}) copy-start(bf16[64,2048]{1,0:T(8,128)(2,1)} %get-tuple-element.116) | copy-start | bytes 786436
  222.2 13.1 %copy-start.10 = (bf16[64,2048]{1,0:T(8,128)(2,1)S(1)}, bf16[64,2048]{1,0:T(8,128)(2,1)}, u32[]{:S(2)}) copy-start(bf16[64,2048]{1,0:T(8,128)(2,1)} %get-tuple-element.106) | copy-start | bytes 786436
  225.4 4.5 %collective-permute-start.15 = (bf16[64,2048]{1,0:T(8,128)(2,1)}, bf16[64,2048]{1,0:T(8,128)(2,1)S(1)}, u32[]{:S(2)}, u32[]{:S(2)}) collective-permute-start(bf16[64,2048]{1,0:T(8,128)(2,1)} %get-tuple-element.113), channel_id=1, source_target_pairs={{0,1},{1,0},{2,3},{3,2},{4,5},{5,4},{6,7},{7,6},{8,9},{9,8},{10,11... | collective-permute-start | bytes 786440 | tf_op jit(solution)/shard_map/ppermute | solution.py:666
  225.4 26.7 %collective-permute-start.25 = (bf16[16,7040]{1,0:T(8,128)(2,1)}, bf16[16,7040]{1,0:T(8,128)(2,1)S(1)}, u32[]{:S(2)}, u32[]{:S(2)}) collective-permute-start(bf16[16,7040]{1,0:T(8,128)(2,1)} %get-tuple-element.118.refs_4_), channel_id=1, source_target_pairs={{0,16},{1,17},{2,18},{3,19},{4,20},{5,21},{6,22},{7,23},{8,24},{9,... | collective-permute-start | bytes 675848 | tf_op jit(solution)/shard_map/ppermute | solution.py:666
  227.6 26.2 %collective-permute-start.26 = (bf16[16,7040]{1,0:T(8,128)(2,1)}, bf16[16,7040]{1,0:T(8,128)(2,1)S(1)}, u32[]{:S(2)}, u32[]{:S(2)}) collective-permute-start(bf16[16,7040]{1,0:T(8,128)(2,1)} %get-tuple-element.119.refs_5_), channel_id=1, source_target_pairs={{0,24},{1,25},{2,26},{3,27},{4,28},{5,29},{6,30},{7,31},{8,16},{9,... | collective-permute-start | bytes 675848 | tf_op jit(solution)/shard_map/ppermute | solution.py:666
  229.3 4.8 %collective-permute-start.14 = (bf16[64,2048]{1,0:T(8,128)(2,1)}, bf16[64,2048]{1,0:T(8,128)(2,1)S(1)}, u32[]{:S(2)}, u32[]{:S(2)}) collective-permute-start(bf16[64,2048]{1,0:T(8,128)(2,1)} %get-tuple-element.111), channel_id=1, source_target_pairs={{0,1},{1,0},{2,3},{3,2},{4,5},{5,4},{6,7},{7,6},{8,9},{9,8},{10,11... | collective-permute-start | bytes 786440 | tf_op jit(solution)/shard_map/ppermute | solution.py:666
  229.3 2.1 collective-permute-start.16
  229.9 2.6 collective-permute-start.17
  231.5 15.0 %collective-permute-start.18 = (bf16[64,2048]{1,0:T(8,128)(2,1)S(1)}, bf16[64,2048]{1,0:T(8,128)(2,1)S(1)}, u32[]{:S(2)}, u32[]{:S(2)}) collective-permute-start(bf16[64,2048]{1,0:T(8,128)(2,1)S(1)} %add_convert_fusion.6.refs_1_), channel_id=1, source_target_pairs={{0,2},{1,3},{2,0},{3,1},{4,6},{5,7},{6,4},{7,5},{8,10},{9,11},{10,... | collective-permute-start | bytes 786440 | tf_op jit(solution)/shard_map/ppermute | solution.py:666
  232.5 14.1 %collective-permute-start.19 = (bf16[64,2048]{1,0:T(8,128)(2,1)S(1)}, bf16[64,2048]{1,0:T(8,128)(2,1)S(1)}, u32[]{:S(2)}, u32[]{:S(2)}) collective-permute-start(bf16[64,2048]{1,0:T(8,128)(2,1)S(1)} %add_convert_fusion.5.refs_2_), channel_id=1, source_target_pairs={{0,4},{1,5},{2,6},{3,7},{4,0},{5,1},{6,2},{7,3},{8,12},{9,13},{10,... | collective-permute-start | bytes 786440 | tf_op jit(solution)/shard_map/ppermute | solution.py:666
  234.2 12.6 %collective-permute-start.20 = (bf16[64,2048]{1,0:T(8,128)(2,1)S(1)}, bf16[64,2048]{1,0:T(8,128)(2,1)S(1)}, u32[]{:S(2)}, u32[]{:S(2)}) collective-permute-start(bf16[64,2048]{1,0:T(8,128)(2,1)S(1)} %add_convert_fusion.4.refs_3_), channel_id=1, source_target_pairs={{0,6},{1,7},{2,4},{3,5},{4,2},{5,3},{6,0},{7,1},{8,14},{9,15},{10,... | collective-permute-start | bytes 786440 | tf_op jit(solution)/shard_map/ppermute | solution.py:666
  246.5 8.4 %collective-permute-start.24 = (bf16[16,7040]{1,0:T(8,128)(2,1)}, bf16[16,7040]{1,0:T(8,128)(2,1)S(1)}, u32[]{:S(2)}, u32[]{:S(2)}) collective-permute-start(bf16[16,7040]{1,0:T(8,128)(2,1)} %get-tuple-element.127), channel_id=1, source_target_pairs={{0,8},{1,9},{2,10},{3,11},{4,12},{5,13},{6,14},{7,15},{8,0},{9,1},... | collective-permute-start | bytes 675848 | tf_op jit(solution)/shard_map/ppermute | solution.py:666
  249.4 6.4 %collective-permute-start.21 = (bf16[16,2048]{1,0:T(8,128)(2,1)}, bf16[16,2048]{1,0:T(8,128)(2,1)S(1)}, u32[]{:S(2)}, u32[]{:S(2)}) collective-permute-start(bf16[16,2048]{1,0:T(8,128)(2,1)} %get-tuple-element.123), channel_id=1, source_target_pairs={{0,8},{1,9},{2,10},{3,11},{4,12},{5,13},{6,14},{7,15},{8,0},{9,1},... | collective-permute-start | bytes 196616 | tf_op jit(solution)/shard_map/ppermute | solution.py:666
  251.3 7.4 %collective-permute-start.22 = (bf16[16,2048]{1,0:T(8,128)(2,1)}, bf16[16,2048]{1,0:T(8,128)(2,1)S(1)}, u32[]{:S(2)}, u32[]{:S(2)}) collective-permute-start(bf16[16,2048]{1,0:T(8,128)(2,1)} %get-tuple-element.124), channel_id=1, source_target_pairs={{0,16},{1,17},{2,18},{3,19},{4,20},{5,21},{6,22},{7,23},{8,24},{9,... | collective-permute-start | bytes 196616 | tf_op jit(solution)/shard_map/ppermute | solution.py:666
  252.1 6.7 %collective-permute-start.23 = (bf16[16,2048]{1,0:T(8,128)(2,1)}, bf16[16,2048]{1,0:T(8,128)(2,1)S(1)}, u32[]{:S(2)}, u32[]{:S(2)}) collective-permute-start(bf16[16,2048]{1,0:T(8,128)(2,1)} %get-tuple-element.125), channel_id=1, source_target_pairs={{0,24},{1,25},{2,26},{3,27},{4,28},{5,29},{6,30},{7,31},{8,16},{9,... | collective-permute-start | bytes 196616 | tf_op jit(solution)/shard_map/ppermute | solution.py:666
  (23 other events, 79.8 us)
Sparse Core Ops, SparseCore 0:
  11.0 76.4 all-gather.1

commit v5 on v4

--- a/solution.py
+++ b/solution.py
@@ -28,12 +28,12 @@
 WB = D + 2 * FF
 TILE = 512
 PARTS = 1
-FF_CHUNKS = ((0, 1536), (1536, 1664))
+FF_CHUNKS = ((0, 1024), (1024, 1024), (2048, 1152))
 ITEMS = 9
 SHORT_WINDOW = (96, 128)
 LONG_WINDOW = (320, 384)
 SHORT_MOST = SHORT_WINDOW[0] - 15
-PROB_ROWS = 1024
+PROB_ROWS = 992
 GROUP = 4
 GROUPS = H // GROUP
 GD = GROUP * HD

time: 271 us -> 272 us (level)
  no operation moved by 1% of the time
where the time goes in v5:
time: 272 us
  Pallas kernels  183 us (67%)
  waiting for transfers between devices  32.3 us (12%)
  starting transfers between devices  27.1 us (10%)
  between operations  14.5 us (5%)
  local copies, waits for them, and re-layouts  10.7 us (4%)
  other arithmetic  4.24 us (2%)
    pallas_call x1, Pallas kernels, feed(): pl.pallas_call(functools.partial(feed_kernel, narrow, own_rows), grid=(to...  83.5 us
    pallas_call x1, Pallas kernels, core_back(): pl.pallas_call(core_kernel, grid=(tokens // PACK,), in_specs=[SCALAR, SCA...  42.2 us
    pallas_call x1, Pallas kernels, attend(): pl.pallas_call(attend_kernel, grid=(packs,), in_specs=[SCALAR, SCALAR, pl...  37.7 us
    ppermute x27, starting transfers between devices, swap(): return lax.ppermute(block, AXES, [(i, i ^ mask) for i in range(count)])  27.1 us
    ppermute x27, waiting for transfers between devices, swap(): return lax.ppermute(block, AXES, [(i, i ^ mask) for i in range(count)])  25.6 us
    pallas_call x1, Pallas kernels, input_grads(): pl.pallas_call(inputs_kernel, grid=(tokens // PACK,), in_specs=[SCALAR] +...  10.4 us
    all_gather x1, waiting for transfers between devices, local(): gb = lax.all_gather(own_b, AXES, axis=0, tiled=True)  6.62 us
  transfers between devices with their start and end apart: 28, of which 13 were waited for; matrix products, arithmetic and copies ran while one was open for 3% of the time, Pallas kernels for 34%

profile of v5, /device:TPU:0, one launch (start us, length us, event | category | flops | bytes accessed | tf_op | source)
XLA Modules:
  0.0 271.7 jit_solution(61823340274289343)
XLA Ops:
  7.3 1.3 reshape.114.bup_ref
  8.5 1.8 pack.1
  10.4 5.1 %collective-permute-start.2 = (bf16[16,2048]{1,0:T(8,128)(2,1)}, bf16[16,2048]{1,0:T(8,128)(2,1)S(1)}, u32[]{:S(2)}, u32[]{:S(2)}) collective-permute-start(bf16[16,2048]{1,0:T(8,128)(2,1)} %get-tuple-element.81), channel_id=1, source_target_pairs={{0,24},{1,25},{2,26},{3,27},{4,28},{5,29},{6,30},{7,31},{8,16},{9,... | collective-permute-start | bytes 196616 | tf_op jit(solution)/shard_map/ppermute | solution.py:666
  17.0 3.0 %collective-permute-done = bf16[16,2048]{1,0:T(8,128)(2,1)S(1)} collective-permute-done((bf16[16,2048]{1,0:T(8,128)(2,1)}, bf16[16,2048]{1,0:T(8,128)(2,1)S(1)}, u32[]{:S(2)}, u32[]{:S(2)}) %collective-permute-start) | collective-permute-done | bytes 65568 | tf_op jit(solution)/shard_map/ppermute | solution.py:666
  20.0 1.3 collective-permute-done.1
  21.4 1.6 collective-permute-start.3
  22.9 1.5 collective-permute-start.4
  24.9 6.0 %collective-permute-done.3 = bf16[64,2048]{1,0:T(8,128)(2,1)S(1)} collective-permute-done((bf16[64,2048]{1,0:T(8,128)(2,1)S(1)}, bf16[64,2048]{1,0:T(8,128)(2,1)S(1)}, u32[]{:S(2)}, u32[]{:S(2)}) %collective-permute-start.3) | collective-permute-done | bytes 262176 | tf_op jit(solution)/shard_map/ppermute | solution.py:666
  30.9 1.7 collective-permute-done.4
  32.6 5.1 %collective-permute-done.5 = bf16[64,2048]{1,0:T(8,128)(2,1)S(1)} collective-permute-done((bf16[64,2048]{1,0:T(8,128)(2,1)S(1)}, bf16[64,2048]{1,0:T(8,128)(2,1)S(1)}, u32[]{:S(2)}, u32[]{:S(2)}) %collective-permute-start.5) | collective-permute-done | bytes 262176 | tf_op jit(solution)/shard_map/ppermute | solution.py:666
  41.5 37.7 %attend.1 = (bf16[2560,512]{1,0:T(8,128)(2,1)}, bf16[2560,512]{1,0:T(8,128)(2,1)}, bf16[2560,512]{1,0:T(8,128)(2,1)}, bf16[2560,512]{1,0:T(8,128)(2,1)}, bf16[25...) custom-call(s32[1]{0:T(128)} %bitcast.me_ref, ...), custom_call_target="tpu_custom_call" | custom-call | flops 40000000000 | bytes 50000000 | tf_op jit(solution)/shard_map/attend/pallas_call | solution.py:211
  80.9 6.6 %all-gather.2.cloned.1.call-done.gb_hbm = bf16[512,6912]{1,0:T(8,128)(2,1)} async-done(((bf16[16,6912]{1,0:T(8,128)(2,1)}), bf16[512,6912]{1,0:T(8,128)(2,1)}) %all-gather.2.cloned.1.call-update) | async-done | bytes 7077904 | tf_op jit(solution)/shard_map/all_gather | solution.py:788
  87.5 83.5 %feed.1 = (bf16[2560,512]{1,0:T(8,128)(2,1)}, f32[2560,512]{1,0:T(8,128)}, bf16[2560,512]{1,0:T(8,128)(2,1)}, bf16[64,7040]{1,0:T(8,128)(2,1)}, bf16[64,7040]{1,...) custom-call(s32[1]{0:T(128)} %bitcast.me_ref, ...), custom_call_target="tpu_custom_call" | custom-call | flops 80000000000 | bytes 40000000 | tf_op jit(solution)/shard_map/feed/pallas_call | solution.py:406
  172.1 1.6 collective-permute-done.8
  173.7 1.5 add_convert_fusion.2.refs_1_
  175.2 1.5 collective-permute-start.11
  178.2 1.6 collective-permute-start.13
  179.8 1.1 add_convert_fusion.3.refs_0_
  181.0 42.2 %core_back.1 = (bf16[2560,512]{1,0:T(8,128)(2,1)}, bf16[2560,512]{1,0:T(8,128)(2,1)}, bf16[2560,512]{1,0:T(8,128)(2,1)}, bf16[64,2048]{1,0:T(8,128)(2,1)}, bf16[...) custom-call(s32[1]{0:T(128)} %bitcast.me_ref, ...), custom_call_target="tpu_custom_call" | custom-call | flops 49999998976 | bytes 50000000 | tf_op jit(solution)/shard_map/core_back/pallas_call | solution.py:514
  224.1 3.2 %combine.2 = (bf16[16,7040]{1,0:T(8,128)(2,1)}, bf16[16,7040]{1,0:T(8,128)(2,1)}, bf16[16,7040]{1,0:T(8,128)(2,1)}, bf16[16,7040]{1,0:T(8,128)(2,1)}, bf16[64,20...) custom-call(bf16[64,7040]{1,0:T(8,128)(2,1)} %add_convert_fusion.3.r, ...), custom_call_target="tpu_custom_call", output_to_operand_aliasing={{4}: (4, {}), {5}: (5, {}), {6}: (6, {}), {7}: (7, {})} | custom-call | flops 1000000 | bytes 7208960 | tf_op jit(solution)/shard_map/combine/pallas_call | solution.py:697
  227.5 1.6 collective-permute-start.25
  229.1 2.0 collective-permute-start.26
  231.7 1.5 collective-permute-done.16
  233.3 1.0 collective-permute-start.18
  235.1 1.9 collective-permute-start.20
  237.8 10.4 %input_grads.1 = (bf16[2560,512]{1,0:T(8,128)(2,1)}, bf16[16,7040]{1,0:T(8,128)(2,1)}) custom-call(s32[1]{0:T(128)} %bitcast.me_ref, bf16[2560,512]{1,0:T(8,128)(2,1)} %get-tuple-element.102.dq_ref, bf16[2560,512]{1,0:T(8,128)(2,1)} %get-tuple-element.103.dk_ref, bf16[2560,512]{1,0:T(8,128)(2,1)} %get-tuple-element.104.dv_ref, ...), custom_call_target="tpu_custom_call", output_to_operand_aliasing={{1}: (13, {})} | custom-call | flops 8000000000 | bytes 20000000 | tf_op jit(solution)/shard_map/input_grads/pallas_call | solution.py:546
  249.3 2.0 combine.3
  251.2 1.9 collective-permute-start.21
  253.6 2.0 collective-permute-start.23
  256.5 1.3 collective-permute-done.21.refs_1_
  257.9 2.6 collective-permute-done.22.refs_2_
  261.2 2.2 finish.1
  (115 shorter events, 17.9 us)
Async XLA Ops:
  7.2 30.6 %copy-start.23 = (s32[2560]{0:T(1024)S(1)}, s32[2560]{0:T(1024)}, u32[]{:S(2)}) copy-start(s32[2560]{0:T(1024)} %param.22) | copy-start | bytes 30724
  7.2 31.4 %copy-start.24 = (s32[2560]{0:T(1024)S(1)}, s32[2560]{0:T(1024)}, u32[]{:S(2)}) copy-start(s32[2560]{0:T(1024)} %param.23) | copy-start | bytes 30724
  7.2 80.3 %all-gather.2.cloned.1.call-start = ((), (), s32[]{:S(2)}) async-start(), calls=%async_computation | async-start | bytes 7299072 | tf_op jit(solution)/shard_map/all_gather | solution.py:788
  10.4 10.9 %collective-permute-start.2 = (bf16[16,2048]{1,0:T(8,128)(2,1)}, bf16[16,2048]{1,0:T(8,128)(2,1)S(1)}, u32[]{:S(2)}, u32[]{:S(2)}) collective-permute-start(bf16[16,2048]{1,0:T(8,128)(2,1)} %get-tuple-element.81), channel_id=1, source_target_pairs={{0,24},{1,25},{2,26},{3,27},{4,28},{5,29},{6,30},{7,31},{8,16},{9,... | collective-permute-start | bytes 196616 | tf_op jit(solution)/shard_map/ppermute | solution.py:666
  15.5 5.8 %collective-permute-start.1 = (bf16[16,2048]{1,0:T(8,128)(2,1)}, bf16[16,2048]{1,0:T(8,128)(2,1)S(1)}, u32[]{:S(2)}, u32[]{:S(2)}) collective-permute-start(bf16[16,2048]{1,0:T(8,128)(2,1)} %get-tuple-element.81), channel_id=1, source_target_pairs={{0,16},{1,17},{2,18},{3,19},{4,20},{5,21},{6,22},{7,23},{8,24},{9,... | collective-permute-start | bytes 196616 | tf_op jit(solution)/shard_map/ppermute | solution.py:666
  15.5 4.5 %collective-permute-start = (bf16[16,2048]{1,0:T(8,128)(2,1)}, bf16[16,2048]{1,0:T(8,128)(2,1)S(1)}, u32[]{:S(2)}, u32[]{:S(2)}) collective-permute-start(bf16[16,2048]{1,0:T(8,128)(2,1)} %get-tuple-element.81), channel_id=1, source_target_pairs={{0,8},{1,9},{2,10},{3,11},{4,12},{5,13},{6,14},{7,15},{8,0},{9,1},... | collective-permute-start | bytes 196616 | tf_op jit(solution)/shard_map/ppermute | solution.py:666
  21.4 9.5 %collective-permute-start.3 = (bf16[64,2048]{1,0:T(8,128)(2,1)S(1)}, bf16[64,2048]{1,0:T(8,128)(2,1)S(1)}, u32[]{:S(2)}, u32[]{:S(2)}) collective-permute-start(bf16[64,2048]{1,0:T(8,128)(2,1)S(1)} %get-tuple-element.144), channel_id=1, source_target_pairs={{0,2},{1,3},{2,0},{3,1},{4,6},{5,7},{6,4},{7,5},{8,10},{9,11},{10,... | collective-permute-start | bytes 786440 | tf_op jit(solution)/shard_map/ppermute | solution.py:666
  22.9 9.6 %collective-permute-start.4 = (bf16[64,2048]{1,0:T(8,128)(2,1)S(1)}, bf16[64,2048]{1,0:T(8,128)(2,1)S(1)}, u32[]{:S(2)}, u32[]{:S(2)}) collective-permute-start(bf16[64,2048]{1,0:T(8,128)(2,1)S(1)} %get-tuple-element.144), channel_id=1, source_target_pairs={{0,4},{1,5},{2,6},{3,7},{4,0},{5,1},{6,2},{7,3},{8,12},{9,13},{10,... | collective-permute-start | bytes 786440 | tf_op jit(solution)/shard_map/ppermute | solution.py:666
  24.4 13.3 %collective-permute-start.5 = (bf16[64,2048]{1,0:T(8,128)(2,1)S(1)}, bf16[64,2048]{1,0:T(8,128)(2,1)S(1)}, u32[]{:S(2)}, u32[]{:S(2)}) collective-permute-start(bf16[64,2048]{1,0:T(8,128)(2,1)S(1)} %get-tuple-element.144), channel_id=1, source_target_pairs={{0,6},{1,7},{2,4},{3,5},{4,2},{5,3},{6,0},{7,1},{8,14},{9,15},{10,... | collective-permute-start | bytes 786440 | tf_op jit(solution)/shard_map/ppermute | solution.py:666
  37.7 2.7 %collective-permute-start.6 = (bf16[256,2048]{1,0:T(8,128)(2,1)S(1)}, bf16[256,2048]{1,0:T(8,128)(2,1)S(1)}, u32[]{:S(2)}, u32[]{:S(2)}) collective-permute-start(bf16[256,2048]{1,0:T(8,128)(2,1)S(1)} %constant_dynamic-update-slice_fusion.4.al_ref), channel_id=1, source_target_pairs={{0,1},{1,0},{2,3},{3,2},{4,5},{5,4},{6,7},{7,6},{8,9},{9,8},{10,11... | collective-permute-start | bytes 3145736 | tf_op jit(solution)/shard_map/ppermute | solution.py:666
  171.0 2.7 %collective-permute-start.8 = (bf16[64,7040]{1,0:T(8,128)(2,1)}, bf16[64,7040]{1,0:T(8,128)(2,1)S(1)}, u32[]{:S(2)}, u32[]{:S(2)}) collective-permute-start(bf16[64,7040]{1,0:T(8,128)(2,1)} %get-tuple-element.97), channel_id=1, source_target_pairs={{0,1},{1,0},{2,3},{3,2},{4,5},{5,4},{6,7},{7,6},{8,9},{9,8},{10,11... | collective-permute-start | bytes 2703368 | tf_op jit(solution)/shard_map/ppermute | solution.py:666
  171.3 8.5 %collective-permute-start.7 = (bf16[64,7040]{1,0:T(8,128)(2,1)}, bf16[64,7040]{1,0:T(8,128)(2,1)S(1)}, u32[]{:S(2)}, u32[]{:S(2)}) collective-permute-start(bf16[64,7040]{1,0:T(8,128)(2,1)} %get-tuple-element.95), channel_id=1, source_target_pairs={{0,1},{1,0},{2,3},{3,2},{4,5},{5,4},{6,7},{7,6},{8,9},{9,8},{10,11... | collective-permute-start | bytes 2703368 | tf_op jit(solution)/shard_map/ppermute | solution.py:666
  171.6 5.2 %collective-permute-start.9 = (bf16[64,7040]{1,0:T(8,128)(2,1)}, bf16[64,7040]{1,0:T(8,128)(2,1)S(1)}, u32[]{:S(2)}, u32[]{:S(2)}) collective-permute-start(bf16[64,7040]{1,0:T(8,128)(2,1)} %get-tuple-element.99), channel_id=1, source_target_pairs={{0,1},{1,0},{2,3},{3,2},{4,5},{5,4},{6,7},{7,6},{8,9},{9,8},{10,11... | collective-permute-start | bytes 2703368 | tf_op jit(solution)/shard_map/ppermute | solution.py:666
  171.8 6.2 %collective-permute-start.10 = (bf16[64,7040]{1,0:T(8,128)(2,1)}, bf16[64,7040]{1,0:T(8,128)(2,1)S(1)}, u32[]{:S(2)}, u32[]{:S(2)}) collective-permute-start(bf16[64,7040]{1,0:T(8,128)(2,1)} %get-tuple-element.101), channel_id=1, source_target_pairs={{0,1},{1,0},{2,3},{3,2},{4,5},{5,4},{6,7},{7,6},{8,9},{9,8},{10,11... | collective-permute-start | bytes 2703368 | tf_op jit(solution)/shard_map/ppermute | solution.py:666
  175.2 48.0 %collective-permute-start.11 = (bf16[64,7040]{1,0:T(8,128)(2,1)S(1)}, bf16[64,7040]{1,0:T(8,128)(2,1)S(1)}, u32[]{:S(2)}, u32[]{:S(2)}) collective-permute-start(bf16[64,7040]{1,0:T(8,128)(2,1)S(1)} %add_convert_fusion.2.refs_1_), channel_id=1, source_target_pairs={{0,2},{1,3},{2,0},{3,1},{4,6},{5,7},{6,4},{7,5},{8,10},{9,11},{10,... | collective-permute-start | bytes 2703368 | tf_op jit(solution)/shard_map/ppermute | solution.py:666
  177.0 46.2 %collective-permute-start.12 = (bf16[64,7040]{1,0:T(8,128)(2,1)S(1)}, bf16[64,7040]{1,0:T(8,128)(2,1)}, u32[]{:S(2)}, u32[]{:S(2)}) collective-permute-start(bf16[64,7040]{1,0:T(8,128)(2,1)S(1)} %add_convert_fusion.1.refs_2_), channel_id=1, source_target_pairs={{0,4},{1,5},{2,6},{3,7},{4,0},{5,1},{6,2},{7,3},{8,12},{9,13},{10,... | collective-permute-start | bytes 2703368 | tf_op jit(solution)/shard_map/ppermute | solution.py:666
  178.2 45.0 %collective-permute-start.13 = (bf16[64,7040]{1,0:T(8,128)(2,1)S(1)}, bf16[64,7040]{1,0:T(8,128)(2,1)}, u32[]{:S(2)}, u32[]{:S(2)}) collective-permute-start(bf16[64,7040]{1,0:T(8,128)(2,1)S(1)} %add_convert_fusion.refs_3_), channel_id=1, source_target_pairs={{0,6},{1,7},{2,4},{3,5},{4,2},{5,3},{6,0},{7,1},{8,14},{9,15},{10,... | collective-permute-start | bytes 2703368 | tf_op jit(solution)/shard_map/ppermute | solution.py:666
  224.1 11.0 %copy-start.11 = (bf16[64,2048]{1,0:T(8,128)(2,1)S(1)}, bf16[64,2048]{1,0:T(8,128)(2,1)}, u32[]{:S(2)}) copy-start(bf16[64,2048]{1,0:T(8,128)(2,1)} %get-tuple-element.116) | copy-start | bytes 786436
  224.1 13.0 %copy-start.10 = (bf16[64,2048]{1,0:T(8,128)(2,1)S(1)}, bf16[64,2048]{1,0:T(8,128)(2,1)}, u32[]{:S(2)}) copy-start(bf16[64,2048]{1,0:T(8,128)(2,1)} %get-tuple-element.106) | copy-start | bytes 786436
  227.3 4.4 %collective-permute-start.15 = (bf16[64,2048]{1,0:T(8,128)(2,1)}, bf16[64,2048]{1,0:T(8,128)(2,1)S(1)}, u32[]{:S(2)}, u32[]{:S(2)}) collective-permute-start(bf16[64,2048]{1,0:T(8,128)(2,1)} %get-tuple-element.113), channel_id=1, source_target_pairs={{0,1},{1,0},{2,3},{3,2},{4,5},{5,4},{6,7},{7,6},{8,9},{9,8},{10,11... | collective-permute-start | bytes 786440 | tf_op jit(solution)/shard_map/ppermute | solution.py:666
  227.5 26.1 %collective-permute-start.25 = (bf16[16,7040]{1,0:T(8,128)(2,1)}, bf16[16,7040]{1,0:T(8,128)(2,1)S(1)}, u32[]{:S(2)}, u32[]{:S(2)}) collective-permute-start(bf16[16,7040]{1,0:T(8,128)(2,1)} %get-tuple-element.118.refs_4_), channel_id=1, source_target_pairs={{0,16},{1,17},{2,18},{3,19},{4,20},{5,21},{6,22},{7,23},{8,24},{9,... | collective-permute-start | bytes 675848 | tf_op jit(solution)/shard_map/ppermute | solution.py:666
  229.1 26.5 %collective-permute-start.26 = (bf16[16,7040]{1,0:T(8,128)(2,1)}, bf16[16,7040]{1,0:T(8,128)(2,1)S(1)}, u32[]{:S(2)}, u32[]{:S(2)}) collective-permute-start(bf16[16,7040]{1,0:T(8,128)(2,1)} %get-tuple-element.119.refs_5_), channel_id=1, source_target_pairs={{0,24},{1,25},{2,26},{3,27},{4,28},{5,29},{6,30},{7,31},{8,16},{9,... | collective-permute-start | bytes 675848 | tf_op jit(solution)/shard_map/ppermute | solution.py:666
  231.1 4.0 %collective-permute-start.14 = (bf16[64,2048]{1,0:T(8,128)(2,1)}, bf16[64,2048]{1,0:T(8,128)(2,1)S(1)}, u32[]{:S(2)}, u32[]{:S(2)}) collective-permute-start(bf16[64,2048]{1,0:T(8,128)(2,1)} %get-tuple-element.111), channel_id=1, source_target_pairs={{0,1},{1,0},{2,3},{3,2},{4,5},{5,4},{6,7},{7,6},{8,9},{9,8},{10,11... | collective-permute-start | bytes 786440 | tf_op jit(solution)/shard_map/ppermute | solution.py:666
  231.1 2.1 collective-permute-start.16
  231.7 2.7 collective-permute-start.17
  233.3 15.0 %collective-permute-start.18 = (bf16[64,2048]{1,0:T(8,128)(2,1)S(1)}, bf16[64,2048]{1,0:T(8,128)(2,1)S(1)}, u32[]{:S(2)}, u32[]{:S(2)}) collective-permute-start(bf16[64,2048]{1,0:T(8,128)(2,1)S(1)} %add_convert_fusion.6.refs_1_), channel_id=1, source_target_pairs={{0,2},{1,3},{2,0},{3,1},{4,6},{5,7},{6,4},{7,5},{8,10},{9,11},{10,... | collective-permute-start | bytes 786440 | tf_op jit(solution)/shard_map/ppermute | solution.py:666
  234.4 14.0 %collective-permute-start.19 = (bf16[64,2048]{1,0:T(8,128)(2,1)S(1)}, bf16[64,2048]{1,0:T(8,128)(2,1)S(1)}, u32[]{:S(2)}, u32[]{:S(2)}) collective-permute-start(bf16[64,2048]{1,0:T(8,128)(2,1)S(1)} %add_convert_fusion.5.refs_2_), channel_id=1, source_target_pairs={{0,4},{1,5},{2,6},{3,7},{4,0},{5,1},{6,2},{7,3},{8,12},{9,13},{10,... | collective-permute-start | bytes 786440 | tf_op jit(solution)/shard_map/ppermute | solution.py:666
  235.1 13.4 %collective-permute-start.20 = (bf16[64,2048]{1,0:T(8,128)(2,1)S(1)}, bf16[64,2048]{1,0:T(8,128)(2,1)S(1)}, u32[]{:S(2)}, u32[]{:S(2)}) collective-permute-start(bf16[64,2048]{1,0:T(8,128)(2,1)S(1)} %add_convert_fusion.4.refs_3_), channel_id=1, source_target_pairs={{0,6},{1,7},{2,4},{3,5},{4,2},{5,3},{6,0},{7,1},{8,14},{9,15},{10,... | collective-permute-start | bytes 786440 | tf_op jit(solution)/shard_map/ppermute | solution.py:666
  248.3 8.3 %collective-permute-start.24 = (bf16[16,7040]{1,0:T(8,128)(2,1)}, bf16[16,7040]{1,0:T(8,128)(2,1)S(1)}, u32[]{:S(2)}, u32[]{:S(2)}) collective-permute-start(bf16[16,7040]{1,0:T(8,128)(2,1)} %get-tuple-element.127), channel_id=1, source_target_pairs={{0,8},{1,9},{2,10},{3,11},{4,12},{5,13},{6,14},{7,15},{8,0},{9,1},... | collective-permute-start | bytes 675848 | tf_op jit(solution)/shard_map/ppermute | solution.py:666
  251.2 6.7 %collective-permute-start.21 = (bf16[16,2048]{1,0:T(8,128)(2,1)}, bf16[16,2048]{1,0:T(8,128)(2,1)S(1)}, u32[]{:S(2)}, u32[]{:S(2)}) collective-permute-start(bf16[16,2048]{1,0:T(8,128)(2,1)} %get-tuple-element.123), channel_id=1, source_target_pairs={{0,8},{1,9},{2,10},{3,11},{4,12},{5,13},{6,14},{7,15},{8,0},{9,1},... | collective-permute-start | bytes 196616 | tf_op jit(solution)/shard_map/ppermute | solution.py:666
  253.1 7.4 %collective-permute-start.22 = (bf16[16,2048]{1,0:T(8,128)(2,1)}, bf16[16,2048]{1,0:T(8,128)(2,1)S(1)}, u32[]{:S(2)}, u32[]{:S(2)}) collective-permute-start(bf16[16,2048]{1,0:T(8,128)(2,1)} %get-tuple-element.124), channel_id=1, source_target_pairs={{0,16},{1,17},{2,18},{3,19},{4,20},{5,21},{6,22},{7,23},{8,24},{9,... | collective-permute-start | bytes 196616 | tf_op jit(solution)/shard_map/ppermute | solution.py:666
  253.6 6.9 %collective-permute-start.23 = (bf16[16,2048]{1,0:T(8,128)(2,1)}, bf16[16,2048]{1,0:T(8,128)(2,1)S(1)}, u32[]{:S(2)}, u32[]{:S(2)}) collective-permute-start(bf16[16,2048]{1,0:T(8,128)(2,1)} %get-tuple-element.125), channel_id=1, source_target_pairs={{0,24},{1,25},{2,26},{3,27},{4,28},{5,29},{6,30},{7,31},{8,16},{9,... | collective-permute-start | bytes 196616 | tf_op jit(solution)/shard_map/ppermute | solution.py:666
  (23 other events, 80.5 us)
Sparse Core Ops, SparseCore 0:
  11.0 76.5 all-gather.1
